TPU v7x, 256 devices: a whole 4x4x8 slice. The times are simulated.
256 devices in a mesh: sub: 64 (over y, z, core), inner: 4 (over x).
Axes of the slice: x: 4, y: 4, z: 8, core: 2. Of those that a mesh axis runs over, the one named last changes fastest.
Arguments:
- blocks: bfloat16 [16384, 2, 128, 128], P(('sub', 'inner')), may hold values from -6 to 6
- routes: int32 [16384, 1], P(('sub', 'inner')), may hold values from 0 to 63; in each aligned block of 64 rows (0 to 63, 64 to 127, ...) at most 2 rows name the same one
- offsets: int32 [16384, 2], P(('sub', 'inner')), may hold values from 0 to 203
- live: int32 [16384], P(('sub', 'inner')), may hold values from 32 to 128
- start_modes: bfloat16 [64, 204, 64, 128], P('sub', None, 'inner'), may hold values from -6 to 6
Outputs:
- modes: bfloat16 [64, 204, 64, 128], P('sub', None, 'inner')
- ritz: float32 [64, 64, 64], P('sub')
Inputs may be any that keep to these rules, and one draw needn't show every extreme that they name: `routes`: among the 64 row blocks of one device at most 2 name the same subdomain.
All inputs are finite; a program needn't handle non-finite values.
Results may differ from a plain program's by a relative error of at most 0.025.
Values may be sent and summed in bfloat16 or wider, within the bound.
No kernel may reach another device: no remote copies, remote signals or barrier semaphores. Data moves between devices by JAX's collectives and lax.ppermute only.
A program may use at most 128 MiB of HBM per device.

v0:
```python
import jax
import jax.numpy as jnp
from jax import lax
from jax.sharding import PartitionSpec as P

OV = 8
ITERS = 3


DAMPING = 32.0


def padded_2(block, sides, width):
    for axis, dim in sides:
        count = lax.axis_size(axis)
        forward = [(i, i + 1) for i in range(count - 1)]
        forward.append((count - 1, 0))
        backward = [(target, source) for source, target in forward]
        low = lax.ppermute(
            lax.slice_in_dim(block, block.shape[dim] - width, None, axis=dim), axis, forward
        )
        high = lax.ppermute(lax.slice_in_dim(block, 0, width, axis=dim), axis, backward)
        block = jnp.concatenate([low, block, high], axis=dim)
    return block


def place_rows(targets, capacity, count):
    onehot = (targets[:, None] == jnp.arange(count, dtype=jnp.int32)[None, :]).astype(jnp.int32)
    earlier = jnp.cumsum(onehot, axis=0) - onehot
    ranked = jnp.sum(earlier * onehot, axis=1)
    return targets * capacity + ranked


def orthonormal(applied, gram, modes):
    lower = jnp.linalg.cholesky(gram)
    inverse = lax.linalg.triangular_solve(
        lower, jnp.eye(modes, dtype=jnp.float32), left_side=True, lower=True
    )
    return jnp.einsum(
        "dnc,mn->dmc", applied, inverse.astype(jnp.bfloat16), preferred_element_type=jnp.float32
    ).astype(jnp.bfloat16)


def shards(blocks, routes, offsets, live, start_modes):
    subs = lax.axis_size("sub")
    inners = lax.axis_size("inner")
    rows_here = blocks.shape[0]
    width = blocks.shape[2]
    capacity = max(2, (2 * rows_here + subs - 1) // subs)
    slots = subs * capacity
    places = place_rows(routes[:, 0], capacity, subs)
    send_blocks = jnp.zeros((slots,) + blocks.shape[1:], jnp.bfloat16).at[places].set(blocks)
    send_offsets = jnp.zeros((slots, offsets.shape[1]), jnp.int32).at[places].set(offsets)
    send_live = jnp.zeros((slots,), jnp.int32).at[places].set(live)
    recv_blocks, recv_offsets, recv_live = (
        lax.all_to_all(send_blocks, "sub", split_axis=0, concat_axis=0, tiled=True),
        lax.all_to_all(send_offsets, "sub", split_axis=0, concat_axis=0, tiled=True),
        lax.all_to_all(send_live, "sub", split_axis=0, concat_axis=0, tiled=True),
    )
    domain = start_modes.shape[1]
    share_modes = start_modes.shape[2]
    modes = share_modes * inners
    live_rows = (lax.broadcasted_iota(jnp.int32, (slots, width), 1) < recv_live[:, None]).astype(
        jnp.float32
    )
    as_float = recv_blocks.astype(jnp.float32)
    column_part = jnp.einsum("skrc,sr->skc", as_float * as_float, live_rows)
    own_sums = jnp.zeros((domain, width), jnp.float32).at[recv_offsets].add(column_part)
    summed = lax.psum(own_sums.astype(jnp.bfloat16), "inner").astype(jnp.float32)
    padded = padded_2(summed.astype(jnp.bfloat16), (("sub", 0),), OV).astype(summed.dtype)
    column_sq = summed.at[:OV].add(padded[:OV]).at[domain - OV :].add(padded[domain + OV :])
    scale = lax.rsqrt(column_sq + DAMPING)
    damped = DAMPING * scale * scale
    scaled = (as_float * live_rows[:, None, :, None] * scale[recv_offsets][:, :, None, :]).astype(
        jnp.bfloat16
    )
    current = lax.all_gather(start_modes[0], "inner", axis=1, tiled=True)
    inner_index = lax.axis_index("inner")
    ritz = jnp.zeros((modes, modes), jnp.float32)
    for step in range(ITERS):
        picked = current[recv_offsets]
        projected = jnp.einsum(
            "skrc,skmc->smr", scaled, picked, preferred_element_type=jnp.float32
        ).astype(jnp.bfloat16)
        spread = jnp.einsum("skrc,smr->skmc", scaled, projected, preferred_element_type=jnp.float32)
        image = lax.psum_scatter(
            jnp.zeros((domain, modes, width), jnp.float32)
            .at[recv_offsets]
            .add(spread)
            .astype(jnp.bfloat16),
            "inner",
            scatter_dimension=1,
            tiled=True,
        ).astype(jnp.float32)
        mine = lax.dynamic_slice_in_dim(current, inner_index * share_modes, share_modes, 1)
        image_share = (image + damped[:, None, :] * mine.astype(jnp.float32)).astype(jnp.bfloat16)
        image_full = lax.all_gather(image_share, "inner", axis=1, tiled=True)
        if step == ITERS - 1:
            ritz = jnp.einsum(
                "dmc,dnc->mn", current, image_full, preferred_element_type=jnp.float32
            )
        gram = jnp.einsum("dmc,dnc->mn", image_full, image_full, preferred_element_type=jnp.float32)
        current = orthonormal(image_full, gram, modes)
    final = lax.dynamic_slice_in_dim(current, inner_index * share_modes, share_modes, 1)
    return (final[None], ritz[None])


def solution(mesh):
    return jax.shard_map(
        shards,
        mesh=mesh,
        in_specs=(
            P(("sub", "inner"), None, None, None),
            P(("sub", "inner"), None),
            P(("sub", "inner"), None),
            P(("sub", "inner")),
            P("sub", None, "inner", None),
        ),
        out_specs=(P("sub", None, "inner", None), P("sub", None, None)),
        check_vma=False,
    )
```

profile of v0, /device:TPU:6, one launch (start us, length us, event | category | flops | bytes accessed | tf_op | source)
XLA Modules:
  0.0 817.4 jit_solution(14355783928661023565)
XLA Ops:
  11.2 12.1 %all-to-all-start.2 = ((s32[64,2,1]{1,2,0:T(1,128)}), s32[64,2,1]{1,2,0:T(1,128)S(1)}, u32[]{:S(2)}, u32[]{:S(2)}) async-start(s32[64,2,1]{1,2,0:T(1,128)} %bitcast.7), calls=%async_computation.2 | async-start | bytes 65536 | tf_op jit(solution)/shard_map/all_to_all | solution.py:58
  25.4 7.3 all-to-all-done.2
  37.3 5.3 broadcast_in_dim.10
  42.7 11.9 %scatter_fusion = bf16[128,2,128,128]{3,2,1,0:T(8,128)(2,1)} fusion(bf16[128,2,128,128]{3,2,1,0:T(8,128)(2,1)} %broadcast_in_dim.10, s32[64]{0:T(128)S(1)} %fusion.52, bf16[64,2,128,128]{3,2,1,0:T(8,128)(2,1)} %param.12), kind=kCustom, calls=%fused_computation.5 | custom fusion | bytes 12583168 | tf_op jit(solution)/shard_map/scatter | solution.py:52
  54.6 10.6 %all-to-all-start.1 = ((bf16[128,2,128,128]{3,2,1,0:T(8,128)(2,1)}), bf16[128,2,128,128]{3,2,1,0:T(8,128)(2,1)}, u32[]{:S(2)}, u32[]{:S(2)}) async-start(bf16[128,2,128,128]{3,2,1,0:T(8,128)(2,1)} %scatter_fusion), calls=%async_computation.1 | async-start | bytes 16777216 | tf_op jit(solution)/shard_map/all_to_all | solution.py:56
  67.7 182.5 %all-to-all-done.1 = bf16[128,2,128,128]{3,2,1,0:T(8,128)(2,1)} async-done(((bf16[128,2,128,128]{3,2,1,0:T(8,128)(2,1)}), bf16[128,2,128,128]{3,2,1,0:T(8,128)(2,1)}, u32[]{:S(2)}, u32[]{:S(2)}) %all-to-all-start.1) | async-done | bytes 8388640 | tf_op jit(solution)/shard_map/all_to_all | solution.py:56
  250.1 4.9 fusion.2
  256.6 14.7 %psum.7 = bf16[204,128]{1,0:T(8,128)(2,1)S(1)} all-reduce(bf16[204,128]{1,0:T(8,128)(2,1)S(1)} %convert_element_type.110), channel_id=1, replica_groups=mesh['sub'=64,'inner'=4] {'inner'}, use_global_device_ids=true, to_apply=%region_6.7 | all-reduce | flops 26112 | bytes 104448 | tf_op jit(solution)/shard_map/psum | solution.py:69
  271.4 5.1 collective-permute-start.1
  276.5 5.0 gather_fusion
  282.4 14.0 %fusion.7 = f32[128,64,2,128]{3,1,2,0:T(8,128)} fusion(bf16[128,2,64,128]{3,2,1,0:T(8,128)(2,1)} %bitcast.152, bf16[128,2,128,128]{3,2,1,0:T(8,128)(2,1)} %all-to-all-done.1, f32[128,2,128]{2,1,0:T(2,128)S(1)} %bitcast.156, f32[128,128]{1,0:T(8,128)S(1)} %get-tuple-element.32), kind=kOutput, calls=%fused_computation.25 | convolution fusion | flops 1108344832 | bytes 21168128 | tf_op jit(solution)/shard_map/skrc,smr->skmc/dot_general | solution.py:85
  300.0 38.7 %scatter_fusion.1 = f32[204,64,128]{2,1,0:T(8,128)} fusion(f32[204,64,128]{2,1,0:T(8,128)} %broadcast.112.clone.1, s32[256]{0:T(256)S(1)} %reshape.208, f32[256,64,128]{2,1,0:T(8,128)} %bitcast.149), kind=kCustom, calls=%fused_computation.8 | custom fusion | flops 2097152 | bytes 25166848 | tf_op jit(solution)/shard_map/scatter-add | solution.py:89
  338.7 5.6 convert_element_type.115
  344.3 37.4 %reduce-scatter.4.cloned.1.call-done = bf16[204,16,128]{2,1,0:T(8,128)(2,1)} async-done(((bf16[204,64,128]{2,1,0:T(8,128)(2,1)}), bf16[204,16,128]{2,1,0:T(8,128)(2,1)}) %reduce-scatter.4.cloned.1.call-update) | async-done | bytes 835600 | tf_op jit(solution)/shard_map/reduce_scatter | solution.py:86
  384.4 48.5 %all-gather.6.cloned.1.call-done = bf16[204,64,128]{2,1,0:T(8,128)(2,1)} async-done(((bf16[204,16,128]{2,1,0:T(8,128)(2,1)}), bf16[204,64,128]{2,1,0:T(8,128)(2,1)}) %all-gather.6.cloned.1.call-update) | async-done | bytes 3342352 | tf_op jit(solution)/shard_map/all_gather | solution.py:97
  437.1 5.8 cholesky.59
  444.2 4.9 custom-call.7
  452.2 5.0 gather_fusion.2
  457.2 13.9 %fusion.5 = f32[128,64,2,128]{3,1,2,0:T(8,128)} fusion(bf16[128,2,64,128]{3,2,1,0:T(8,128)(2,1)} %bitcast.154, bf16[128,2,128,128]{3,2,1,0:T(8,128)(2,1)} %all-to-all-done.1, f32[128,2,128]{2,1,0:T(2,128)S(1)} %bitcast.158, f32[128,128]{1,0:T(8,128)S(1)} %copy-done.7), kind=kOutput, calls=%fused_computation.23 | convolution fusion | flops 1108344832 | bytes 21168128 | tf_op jit(solution)/shard_map/skrc,smr->skmc/dot_general | solution.py:85
  474.8 38.7 %scatter_fusion.2 = f32[204,64,128]{2,1,0:T(8,128)} fusion(f32[204,64,128]{2,1,0:T(8,128)} %broadcast.112.clone, s32[256]{0:T(256)S(1)} %reshape.208, f32[256,64,128]{2,1,0:T(8,128)} %bitcast.150), kind=kCustom, calls=%fused_computation.9 | custom fusion | flops 2097152 | bytes 25166848 | tf_op jit(solution)/shard_map/scatter-add | solution.py:89
  513.4 5.6 convert_element_type.124
  519.3 42.1 %reduce-scatter.6.cloned.1.call-done = bf16[204,16,128]{2,1,0:T(8,128)(2,1)} async-done(((bf16[204,64,128]{2,1,0:T(8,128)(2,1)}), bf16[204,16,128]{2,1,0:T(8,128)(2,1)}) %reduce-scatter.6.cloned.1.call-update) | async-done | bytes 835600 | tf_op jit(solution)/shard_map/reduce_scatter | solution.py:86
  564.1 48.5 %all-gather.8.cloned.1.call-done = bf16[204,64,128]{2,1,0:T(8,128)(2,1)} async-done(((bf16[204,16,128]{2,1,0:T(8,128)(2,1)}), bf16[204,64,128]{2,1,0:T(8,128)(2,1)}) %all-gather.8.cloned.1.call-update) | async-done | bytes 3342352 | tf_op jit(solution)/shard_map/all_gather | solution.py:97
  616.7 5.8 cholesky.70
  623.9 4.9 custom-call.8
  635.0 14.0 %fusion.3 = f32[128,64,2,128]{3,1,2,0:T(8,128)} fusion(bf16[128,2,128,128]{3,2,1,0:T(8,128)(2,1)} %all-to-all-done.1, f32[128,2,128]{2,1,0:T(2,128)} %bitcast.157, f32[128,128]{1,0:T(8,128)S(1)} %copy-done.7, bf16[128,2,64,128]{3,2,1,0:T(8,128)(2,1)} %bitcast.153), kind=kOutput, calls=%fused_computation.21 | convolution fusion | flops 1108344832 | bytes 21168128 | tf_op jit(solution)/shard_map/skrc,smr->skmc/dot_general | solution.py:85
  652.7 38.7 %scatter_fusion.3 = f32[204,64,128]{2,1,0:T(8,128)} fusion(f32[204,64,128]{2,1,0:T(8,128)} %broadcast.112, s32[256]{0:T(256)S(1)} %reshape.208, f32[256,64,128]{2,1,0:T(8,128)} %bitcast.148), kind=kCustom, calls=%fused_computation.10 | custom fusion | flops 2097152 | bytes 25166848 | tf_op jit(solution)/shard_map/scatter-add | solution.py:89
  691.4 5.5 convert_element_type.132
  697.3 42.0 %reduce-scatter.8.cloned.1.call-done = bf16[204,16,128]{2,1,0:T(8,128)(2,1)} async-done(((bf16[204,64,128]{2,1,0:T(8,128)(2,1)}), bf16[204,16,128]{2,1,0:T(8,128)(2,1)}) %reduce-scatter.8.cloned.1.call-update) | async-done | bytes 835600 | tf_op jit(solution)/shard_map/reduce_scatter | solution.py:86
  741.7 48.5 %all-gather.10.cloned.1.call-done = bf16[204,64,128]{2,1,0:T(8,128)(2,1)} async-done(((bf16[204,16,128]{2,1,0:T(8,128)(2,1)}), bf16[204,64,128]{2,1,0:T(8,128)(2,1)}) %all-gather.10.cloned.1.call-update) | async-done | bytes 3342352 | tf_op jit(solution)/shard_map/all_gather | solution.py:97
  794.4 5.8 cholesky.81
  801.6 4.9 custom-call.9
  (93 shorter events, 64.7 us)
Async XLA Ops:
  11.2 21.5 %all-to-all-start.2 = ((s32[64,2,1]{1,2,0:T(1,128)}), s32[64,2,1]{1,2,0:T(1,128)S(1)}, u32[]{:S(2)}, u32[]{:S(2)}) async-start(s32[64,2,1]{1,2,0:T(1,128)} %bitcast.7), calls=%async_computation.2 | async-start | bytes 65536 | tf_op jit(solution)/shard_map/all_to_all | solution.py:58
  32.7 21.9 %all-to-all-start = ((s32[64,2,2]{2,1,0:T(2,128)}), s32[64,2,2]{2,1,0:T(2,128)S(1)}, u32[]{:S(2)}, u32[]{:S(2)}) async-start(s32[64,2,2]{2,1,0:T(2,128)} %bitcast.3), calls=%async_computation | async-start | bytes 131072 | tf_op jit(solution)/shard_map/all_to_all | solution.py:57
  54.6 195.5 %all-to-all-start.1 = ((bf16[128,2,128,128]{3,2,1,0:T(8,128)(2,1)}), bf16[128,2,128,128]{3,2,1,0:T(8,128)(2,1)}, u32[]{:S(2)}, u32[]{:S(2)}) async-start(bf16[128,2,128,128]{3,2,1,0:T(8,128)(2,1)} %scatter_fusion), calls=%async_computation.1 | async-start | bytes 16777216 | tf_op jit(solution)/shard_map/all_to_all | solution.py:56
  65.2 211.3 %all-gather.12.cloned.1.call-start = ((), (), s32[]{:S(2)}) async-start(), calls=%async_computation.12 | async-start | bytes 4177920 | tf_op jit(solution)/shard_map/all_gather | solution.py:77
  66.0 315.7 %reduce-scatter.4.cloned.1.call-start = ((), (), s32[]{:S(2)}) async-start(), calls=%async_computation.6 | async-start | bytes 4177920 | tf_op jit(solution)/shard_map/reduce_scatter | solution.py:86
  67.5 214.9 %copy-start.6 = (f32[128,128]{1,0:T(8,128)}, f32[128,128]{1,0:T(8,128)S(1)}, u32[]{:S(2)}) copy-start(f32[128,128]{1,0:T(8,128)S(1)} %get-tuple-element.32) | copy-start | bytes 196612
  271.3 10.1 %collective-permute-start = (bf16[8,128]{1,0:T(8,128)(2,1)S(1)}, bf16[8,128]{1,0:T(8,128)(2,1)S(1)}, u32[]{:S(2)}, u32[]{:S(2)}) collective-permute-start(bf16[8,128]{1,0:T(8,128)(2,1)S(1)} %get-tuple-element.30), channel_id=1, source_target_pairs={{0,4},{4,8},{8,12},{12,16},{16,20},{20,24},{24,28},{28,32},{32,36}... | collective-permute-start | bytes 6152 | tf_op jit(solution)/shard_map/ppermute | solution.py:19
  271.4 10.0 %collective-permute-start.1 = (bf16[8,128]{1,0:T(8,128)(2,1)S(1)}, bf16[8,128]{1,0:T(8,128)(2,1)S(1)}, u32[]{:S(2)}, u32[]{:S(2)}) collective-permute-start(bf16[8,128]{1,0:T(8,128)(2,1)S(1)} %get-tuple-element.31), channel_id=1, source_target_pairs={{4,0},{8,4},{12,8},{16,12},{20,16},{24,20},{28,24},{32,28},{36,32}... | collective-permute-start | bytes 6152 | tf_op jit(solution)/shard_map/ppermute | solution.py:22
  282.4 14.0 %copy-start.4 = (f32[256,128]{1,0:T(8,128)}, f32[256,128]{1,0:T(8,128)S(1)}, u32[]{:S(2)}) copy-start(f32[256,128]{1,0:T(8,128)S(1)} %gather_fusion.1) | copy-start | bytes 393220
  344.2 88.6 %all-gather.6.cloned.1.call-start = ((), (), s32[]{:S(2)}) async-start(), calls=%async_computation.7 | async-start | bytes 4177920 | tf_op jit(solution)/shard_map/all_gather | solution.py:97
  384.3 177.0 %reduce-scatter.6.cloned.1.call-start = ((), (), s32[]{:S(2)}) async-start(), calls=%async_computation.8 | async-start | bytes 4177920 | tf_op jit(solution)/shard_map/reduce_scatter | solution.py:86
  432.8 16.6 %copy-start.3 = (bf16[204,64,128]{2,1,0:T(8,128)(2,1)S(1)}, bf16[204,64,128]{2,1,0:T(8,128)(2,1)}, u32[]{:S(2)}) copy-start(bf16[204,64,128]{2,1,0:T(8,128)(2,1)} %all-gather.6.cloned.1.call-done) | copy-start | bytes 10027012
  452.2 5.0 copy-start.5
  452.2 5.0 copy-start.7
  519.0 93.5 %all-gather.8.cloned.1.call-start = ((), (), s32[]{:S(2)}) async-start(), calls=%async_computation.9 | async-start | bytes 4177920 | tf_op jit(solution)/shard_map/all_gather | solution.py:97
  564.0 175.3 %reduce-scatter.8.cloned.1.call-start = ((), (), s32[]{:S(2)}) async-start(), calls=%async_computation.10 | async-start | bytes 4177920 | tf_op jit(solution)/shard_map/reduce_scatter | solution.py:86
  632.0 107.3 %copy-start.1 = (bf16[64,204,128]{2,0,1:T(8,128)(2,1)}, bf16[64,204,128]{2,0,1:T(8,128)(2,1)S(1)}, u32[]{:S(2)}) copy-start(bf16[64,204,128]{2,0,1:T(8,128)(2,1)S(1)} %convolution_convert_fusion) | copy-start | bytes 10027012
  697.0 93.3 %all-gather.10.cloned.1.call-start = ((), (), s32[]{:S(2)}) async-start(), calls=%async_computation.11 | async-start | bytes 4177920 | tf_op jit(solution)/shard_map/all_gather | solution.py:97
  790.2 16.6 %copy-start = (bf16[204,64,128]{2,1,0:T(8,128)(2,1)S(1)}, bf16[204,64,128]{2,1,0:T(8,128)(2,1)}, u32[]{:S(2)}) copy-start(bf16[204,64,128]{2,1,0:T(8,128)(2,1)} %all-gather.10.cloned.1.call-done) | copy-start | bytes 10027012
  806.8 2.1 copy-start.2
Sparse Core Ops, SparseCore 0:
  67.9 47.7 all-gather.11
  344.4 37.2 reduce-scatter.3
  384.5 48.3 all-gather.5
  519.1 42.1 reduce-scatter.5
  564.1 48.3 all-gather.7
  697.1 42.1 reduce-scatter.7
  741.8 48.3 all-gather.9
where the time goes:
time: 820 us; the launch traced here: 817 us
  waiting for transfers between devices  458 us (56%)
  other arithmetic  181 us (22%)
  matrix products  68.2 us (8%)
  local copies, waits for them, and re-layouts  47.9 us (6%)
  starting transfers between devices  33.2 us (4%)
  blocking collectives  14.7 us (2%)
  between operations  14.5 us (2%)
    all_to_all x1, waiting for transfers between devices, shards(): lax.all_to_all(send_blocks, 'sub', split_axis=0, concat_axis=0, tiled=True)  182 us
    all_gather x3, waiting for transfers between devices, shards(): image_full = lax.all_gather(image_share, 'inner', axis=1, tiled=True)  145 us
    reduce_scatter x3, waiting for transfers between devices, shards(): lax.psum_scatter(jnp.zeros((domain, modes, width), jnp.float32).at[recv_o...  122 us
    scatter-add x3, other arithmetic, shards(): image = lax.psum_scatter(jnp.zeros((domain, modes, width), jnp.float32).a...  116 us
    dot_general x3, matrix products, shards(): jnp.einsum('skrc,smr->skmc', scaled, projected, preferred_element_type=jn...  41.9 us
    another operation x9, other arithmetic, orthonormal(): lower = jnp.linalg.cholesky(gram)  19.6 us
    convert_element_type x3, other arithmetic, shards(): image = lax.psum_scatter(jnp.zeros((domain, modes, width), jnp.float32).a...  16.7 us
    another operation x6, other arithmetic, orthonormal(): lax.linalg.triangular_solve(lower, jnp.eye(modes, dtype=jnp.float32), lef...  16.6 us
  transfers between devices with their start and end apart: 12, of which 8 were waited for; matrix products, arithmetic and copies ran while one was open for 4% of the time, Pallas kernels for 0%

commit v1 on v0

v1 whole, which is shorter than its diff:
```python
import functools

import jax
import jax.numpy as jnp
from jax import lax
from jax.experimental import pallas as pl
from jax.experimental.pallas import tpu as pltpu
from jax.sharding import Mesh
from jax.sharding import PartitionSpec as P

OV = 8
ITERS = 3
BLK = 128
DAMPING = 32.0
AXES = ("y", "z", "c", "xh", "xl")
NT = (((1,), (1,)), ((), ()))
VMEM_LIMIT = 50 * 2**20


def nt_dot(left, right):
    return lax.dot_general(left, right, NT, preferred_element_type=jnp.float32)


def pack_kernel(order, blocks, packed, sems):
    slots = packed.shape[0]

    def copy(slot):
        return pltpu.make_async_copy(blocks.at[order[slot]], packed.at[slot], sems.at[slot])

    def start(slot, carry):
        copy(slot).start()
        return carry

    def wait(slot, carry):
        copy(slot).wait()
        return carry

    lax.fori_loop(0, slots, start, 0)
    lax.fori_loop(0, slots, wait, 0)


def pack(blocks, order):
    slots = order.shape[0]
    return pl.pallas_call(
        pack_kernel,
        out_shape=jax.ShapeDtypeStruct((slots,) + blocks.shape[1:], blocks.dtype),
        grid_spec=pltpu.PrefetchScalarGridSpec(
            num_scalar_prefetch=1,
            grid=(1,),
            in_specs=[pl.BlockSpec(memory_space=pl.ANY)],
            out_specs=pl.BlockSpec(memory_space=pl.ANY),
            scratch_shapes=[pltpu.SemaphoreType.DMA((slots,))],
        ),
        compiler_params=pltpu.CompilerParams(vmem_limit_bytes=VMEM_LIMIT),
    )(order, blocks)


def sums_kernel(group, offs, live, blk, sums):
    step = pl.program_id(0)

    @pl.when(step == 0)
    def _():
        sums[...] = jnp.zeros_like(sums)

    rows = lax.broadcasted_iota(jnp.int32, (BLK, BLK), 0)

    def body(s, carry):
        slot = step * group + s
        keep = rows < live[slot]
        for k in range(2):
            wide = blk[s, k].astype(jnp.float32)
            part = jnp.sum(jnp.where(keep, wide * wide, 0.0), axis=0, keepdims=True)
            at = pl.ds(offs[2 * slot + k], 1)
            sums[at, :] = sums[at, :] + part
        return carry

    lax.fori_loop(0, group, body, 0)


def column_sums(blocks, offs, live, domain):
    slots = blocks.shape[0]
    group = min(16, slots)
    return pl.pallas_call(
        functools.partial(sums_kernel, group),
        out_shape=jax.ShapeDtypeStruct((domain, BLK), jnp.float32),
        grid_spec=pltpu.PrefetchScalarGridSpec(
            num_scalar_prefetch=2,
            grid=(slots // group,),
            in_specs=[pl.BlockSpec((group, 2, BLK, BLK), lambda i, *_: (i, 0, 0, 0))],
            out_specs=pl.BlockSpec((domain, BLK), lambda i, *_: (0, 0)),
        ),
        compiler_params=pltpu.CompilerParams(vmem_limit_bytes=VMEM_LIMIT),
    )(offs, live, blocks)


def apply_kernel(first, group, unroll, offs, live, core, blk, scale, own, peer, *rest):
    if first:
        keep, send, scaled, modes, total, sems = rest
    else:
        keep, send, modes, total, sems = rest
    step = pl.program_id(0)
    half = keep.shape[0]
    mine = core[0] * half
    other = (1 - core[0]) * half

    @pl.when(step == 0)
    def _():
        one = pltpu.make_async_copy(own, modes.at[pl.ds(mine, half)], sems.at[0])
        two = pltpu.make_async_copy(peer, modes.at[pl.ds(other, half)], sems.at[1])
        one.start()
        two.start()

        def clear(i, carry):
            total[pl.ds(2 * i, 2)] = jnp.zeros((2,) + total.shape[1:], jnp.float32)
            return carry

        lax.fori_loop(0, half, clear, 0)
        one.wait()
        two.wait()

    rows = lax.broadcasted_iota(jnp.int32, (BLK, BLK), 0)

    def body(g, carry):
        wide, places = [], []
        for u in range(unroll):
            s = g * unroll + u
            slot = step * group + s
            place = [offs[2 * slot], offs[2 * slot + 1]]
            pair = [blk[s, 0], blk[s, 1]]
            if first:
                alive = rows < live[slot]
                for k in range(2):
                    value = pair[k].astype(jnp.float32) * scale[pl.ds(place[k], 1), :]
                    pair[k] = jnp.where(alive, value, 0.0).astype(jnp.bfloat16)
                    scaled[s, k] = pair[k]
            wide.append(jnp.concatenate(pair, axis=1))
            places.append(place)
        picked = [jnp.concatenate([modes[p], modes[q]], axis=1) for p, q in places]
        projected = [nt_dot(v, a).astype(jnp.bfloat16) for v, a in zip(picked, wide)]
        spread = [
            jnp.dot(v, a, preferred_element_type=jnp.float32) for v, a in zip(projected, wide)
        ]
        for (p, q), value in zip(places, spread):
            total[p] += value[:, :BLK]
            total[q] += value[:, BLK:]
        return carry

    lax.fori_loop(0, group // unroll, body, 0)

    @pl.when(step == pl.num_programs(0) - 1)
    def _():
        def write(i, carry):
            keep[pl.ds(2 * i, 2)] = total[pl.ds(mine + 2 * i, 2)].astype(jnp.bfloat16)
            send[pl.ds(2 * i, 2)] = total[pl.ds(other + 2 * i, 2)].astype(jnp.bfloat16)
            return carry

        lax.fori_loop(0, half // 2, write, 0)


def apply_rows(first, blocks, offs, live, core, scale, own, peer):
    slots = blocks.shape[0]
    half, modes, _ = own.shape
    group = min(16, slots)
    unroll = min(8, group)
    block_spec = pl.BlockSpec((group, 2, BLK, BLK), lambda i, *_: (i, 0, 0, 0))
    half_spec = pl.BlockSpec((half, modes, BLK), lambda i, *_: (0, 0, 0))
    half_shape = jax.ShapeDtypeStruct(own.shape, jnp.bfloat16)
    out_shape, out_specs = [half_shape, half_shape], [half_spec, half_spec]
    if first:
        out_shape.append(jax.ShapeDtypeStruct(blocks.shape, jnp.bfloat16))
        out_specs.append(block_spec)
    return pl.pallas_call(
        functools.partial(apply_kernel, first, group, unroll),
        out_shape=out_shape,
        grid_spec=pltpu.PrefetchScalarGridSpec(
            num_scalar_prefetch=3,
            grid=(slots // group,),
            in_specs=[
                block_spec,
                pl.BlockSpec(scale.shape, lambda i, *_: (0, 0)),
                pl.BlockSpec(memory_space=pl.ANY),
                pl.BlockSpec(memory_space=pl.ANY),
            ],
            out_specs=out_specs,
            scratch_shapes=[
                pltpu.VMEM((2 * half, modes, BLK), jnp.bfloat16),
                pltpu.VMEM((2 * half, modes, BLK), jnp.float32),
                pltpu.SemaphoreType.DMA((2,)),
            ],
        ),
        compiler_params=pltpu.CompilerParams(vmem_limit_bytes=VMEM_LIMIT),
    )(offs, live, core, blocks, scale, own, peer)


def image_kernel(with_ritz, one, two, own, damped, applied, gram, *rest):
    step = pl.program_id(0)
    ritz = rest[0] if with_ritz else None

    @pl.when(step == 0)
    def _():
        gram[...] = jnp.zeros_like(gram)
        if with_ritz:
            ritz[...] = jnp.zeros_like(ritz)

    gram_part = jnp.zeros(gram.shape, jnp.float32)
    ritz_part = jnp.zeros(gram.shape, jnp.float32)
    for i in range(0, one.shape[0], 2):
        values, olds = [], []
        for l in (i, i + 1):
            old = own[l]
            total = one[l].astype(jnp.float32) + two[l].astype(jnp.float32)
            value = (total + damped[l] * old.astype(jnp.float32)).astype(jnp.bfloat16)
            applied[l] = value
            values.append(value)
            olds.append(old)
        value = jnp.concatenate(values, axis=1)
        gram_part += nt_dot(value, value)
        if with_ritz:
            ritz_part += nt_dot(jnp.concatenate(olds, axis=1), value)
    gram[...] += gram_part
    if with_ritz:
        ritz[...] += ritz_part


def form_image(with_ritz, one, two, own, damped, steps=3):
    half, modes, _ = own.shape
    part = half // steps
    part_spec = pl.BlockSpec((part, modes, BLK), lambda i: (i, 0, 0))
    square_spec = pl.BlockSpec((modes, modes), lambda i: (0, 0))
    square_shape = jax.ShapeDtypeStruct((modes, modes), jnp.float32)
    squares = 2 if with_ritz else 1
    return pl.pallas_call(
        functools.partial(image_kernel, with_ritz),
        out_shape=[jax.ShapeDtypeStruct(own.shape, jnp.bfloat16)] + [square_shape] * squares,
        grid=(steps,),
        in_specs=[part_spec] * 3 + [pl.BlockSpec((part, 1, BLK), lambda i: (i, 0, 0))],
        out_specs=[part_spec] + [square_spec] * squares,
        compiler_params=pltpu.CompilerParams(vmem_limit_bytes=VMEM_LIMIT),
    )(one, two, own, damped)


def inverse_factor(gram):
    size = gram.shape[0]
    both = (size, 2 * size)
    row_at = lax.broadcasted_iota(jnp.int32, both, 0)
    col_at = lax.broadcasted_iota(jnp.int32, both, 1)
    eye = (col_at == row_at + size).astype(jnp.float32)
    work = jnp.where(col_at < size, jnp.concatenate([gram, gram], axis=1), eye)
    for j in range(size):
        root = lax.rsqrt(work[j : j + 1, j : j + 1])
        row = work[j : j + 1, :] * root
        factor = jnp.where(row_at[:, :1] > j, work[:, j : j + 1] * root, 0.0)
        work = jnp.where(row_at == j, row, work - factor * row)
    return work[:, size:]


def solve_kernel(gram_one, gram_two, applied, new, inverse):
    @pl.when(pl.program_id(0) == 0)
    def _():
        inverse[...] = inverse_factor(gram_one[...] + gram_two[...]).astype(jnp.bfloat16)

    for i in range(0, applied.shape[0], 2):
        pair = jnp.concatenate([applied[i], applied[i + 1]], axis=1)
        value = jnp.dot(inverse[...], pair, preferred_element_type=jnp.float32)
        new[i] = value[:, :BLK].astype(jnp.bfloat16)
        new[i + 1] = value[:, BLK:].astype(jnp.bfloat16)


def new_modes(gram_one, gram_two, applied, steps=3):
    half, modes, _ = applied.shape
    part_spec = pl.BlockSpec((half // steps, modes, BLK), lambda i: (i, 0, 0))
    square_spec = pl.BlockSpec((modes, modes), lambda i: (0, 0))
    return pl.pallas_call(
        solve_kernel,
        out_shape=jax.ShapeDtypeStruct(applied.shape, jnp.bfloat16),
        grid=(steps,),
        in_specs=[square_spec, square_spec, part_spec],
        out_specs=part_spec,
        scratch_shapes=[pltpu.VMEM((modes, modes), jnp.bfloat16)],
        compiler_params=pltpu.CompilerParams(vmem_limit_bytes=VMEM_LIMIT),
    )(gram_one, gram_two, applied)


def side(xh, xl):
    return 1 - (xh ^ xl)


def flat(ny, nz, y, z, c, xh, xl):
    return (((y * nz + z) * 2 + c) * 2 + xh) * 2 + xl


def every(ny, nz):
    return [
        (y, z, c, xh, xl)
        for y in range(ny)
        for z in range(nz)
        for c in range(2)
        for xh in range(2)
        for xl in range(2)
    ]


def next_pairs(ny, nz):
    pairs = []
    for y, z, c, xh, xl in every(ny, nz):
        sub = ((y * nz + z) * 2 + side(xh, xl) + 1) % (ny * nz * 2)
        there = (sub // (2 * nz), sub // 2 % nz, c, xh, xh ^ (1 - sub % 2))
        pairs.append((flat(ny, nz, y, z, c, xh, xl), flat(ny, nz, *there)))
    return pairs


def out_pairs(ny, nz):
    pairs = []
    for y, z, c, xh, xl in every(ny, nz):
        if c != side(xh, xl):
            there = (y, z, 1 - c, xh, 1 - xl)
            pairs.append((flat(ny, nz, y, z, c, xh, xl), flat(ny, nz, *there)))
    return pairs


def spread_pairs():
    return [
        (side(xh, xl) * 4 + xh * 2 + xl, (1 - side(xh, xl)) * 4 + xh * 2 + xl)
        for xh in range(2)
        for xl in range(2)
    ]


def core_swap(value):
    return lax.ppermute(value, "c", [(0, 1), (1, 0)])


def chip_swap(value):
    return lax.ppermute(value, ("xh", "xl"), [(0, 3), (3, 0), (1, 2), (2, 1)])


def slot_rows(targets, wanted, rows):
    equal = targets[..., None, :] == wanted[:, None]
    at = jnp.arange(rows, dtype=jnp.int32)
    first = jnp.min(jnp.where(equal, at, rows), axis=-1)
    last = jnp.max(jnp.where(equal, at, -1), axis=-1)
    valid = jnp.stack([first < rows, last > first], axis=-1)
    return jnp.where(valid, jnp.stack([first, last], axis=-1), 0), valid


def shards(ny, nz, blocks, routes, offsets, live, start_modes):
    y, z, c, xh, xl = [lax.axis_index(axis) for axis in AXES]
    chip = 2 * xh + xl
    own_side = 1 - (xh ^ xl)
    subs = ny * nz * 2
    rows = blocks.shape[0]
    domain, share = start_modes.shape[1], start_modes.shape[2]
    half = domain // 2
    group = ("y", "z", "xl")

    targets = routes[:, 0]
    wanted = jnp.arange(subs, dtype=jnp.int32) ^ (1 - xh)
    order, _ = slot_rows(targets, wanted, rows)
    packed = pack(blocks, order.reshape(-1))
    received = lax.all_to_all(packed, group, split_axis=0, concat_axis=0, tiled=True)

    table = jnp.stack([targets, offsets[:, 0], offsets[:, 1], live], axis=0)
    tables = lax.all_gather(table, group, axis=0, tiled=False)
    here = ((y * nz + z) * 2 + own_side).astype(jnp.int32)
    index, valid = slot_rows(tables[:, 0, :], here[None], rows)
    index, valid = index[:, 0], valid[:, 0]
    onehot = index[..., None] == jnp.arange(rows, dtype=jnp.int32)
    picked = [
        jnp.sum(jnp.where(onehot & valid[..., None], tables[:, None, k, :], 0), axis=-1)
        for k in (1, 2, 3)
    ]
    offs = jnp.stack(picked[:2], axis=-1).reshape(-1)
    alive = picked[2].reshape(-1)

    gathered = lax.all_gather(start_modes[0], ("xh", "xl"), axis=1, tiled=True)
    sibling = lax.ppermute(gathered, ("c", "xh", "xl"), spread_pairs())
    start = jnp.where(c == own_side, gathered, sibling)
    own = lax.dynamic_slice_in_dim(start, c * half, half, 0)
    peer = lax.dynamic_slice_in_dim(start, (1 - c) * half, half, 0)

    sums = column_sums(received, offs, alive, domain)
    sums = sums + core_swap(sums)
    sums = sums + chip_swap(sums)
    forward = next_pairs(ny, nz)
    backward = [(there, here_) for here_, there in forward]
    low = lax.ppermute(sums[domain - OV :], AXES, forward)
    high = lax.ppermute(sums[:OV], AXES, backward)
    column_sq = sums + jnp.concatenate(
        [low, jnp.zeros((domain - 2 * OV, BLK), jnp.float32), high], axis=0
    )
    scale = lax.rsqrt(column_sq + DAMPING)
    damped = lax.dynamic_slice_in_dim(DAMPING * scale * scale, c * half, half, 0)[:, None, :]

    core = c.astype(jnp.int32)[None]
    work = received
    for step in range(ITERS):
        keep, send, *scaled = apply_rows(step == 0, work, offs, alive, core, scale, own, peer)
        if step == 0:
            work = scaled[0]
        other = core_swap(send)
        chip_sum = (keep.astype(jnp.float32) + other.astype(jnp.float32)).astype(jnp.bfloat16)
        last = step == ITERS - 1
        applied, gram, *ritz = form_image(last, chip_sum, chip_swap(chip_sum), own, damped)
        own = new_modes(gram, core_swap(gram), applied)
        if not last:
            peer = core_swap(own)

    ritz = ritz[0] + core_swap(ritz[0])
    at_home = c == own_side
    mine = lax.dynamic_slice_in_dim(own, chip * share, share, 1)
    beside = lax.dynamic_slice_in_dim(own, (chip ^ 1) * share, share, 1)
    held = jnp.where(at_home, mine, beside)
    swapped = core_swap(jnp.where(at_home, beside, mine))
    whole = jnp.where(
        c == 0, jnp.concatenate([held, swapped], 0), jnp.concatenate([swapped, held], 0)
    )
    pairs = out_pairs(ny, nz)
    modes = jnp.where(at_home, whole, lax.ppermute(whole, AXES, pairs))
    ritz = jnp.where(at_home, ritz, lax.ppermute(ritz, AXES, pairs))
    return modes[None], ritz[None]


def solution(mesh, ny=4):
    nz = mesh.shape["sub"] // (2 * ny)
    grid = Mesh(mesh.devices.reshape(ny, nz, 2, 2, 2), AXES)
    subs, inner = ("y", "z", "c"), ("xh", "xl")
    return jax.shard_map(
        functools.partial(shards, ny, nz),
        mesh=grid,
        in_specs=(
            P(subs + inner, None, None, None),
            P(subs + inner, None),
            P(subs + inner, None),
            P(subs + inner),
            P(subs, None, inner, None),
        ),
        out_specs=(P(subs, None, inner, None), P(subs, None, None)),
        check_vma=False,
    )
```

time: 820 us -> 863 us (1.052)
  Pallas kernels: 0 us -> 336 us
  other arithmetic: 181 us -> 11.7 us
  waiting for transfers between devices: 458 us -> 306 us
  blocking collectives: 14.7 us -> 155 us
  matrix products: 68.2 us -> 0 us
  local copies, waits for them, and re-layouts: 47.9 us -> 10 us
    pallas_call x0 -> x11, Pallas kernels: none -> 336 us  [the longest x1 257 us: pack(): pl.pallas_call(pack_kernel, out_shape=jax.ShapeDtypeStruct((slots,) + blo...]
    all_gather x0 -> x1, blocking collectives: none -> 155 us  [shards(): tables = lax.all_gather(table, group, axis=0, tiled=False)]
    ppermute x2 -> x20, waiting for transfers between devices: 0.01 us -> 152 us  [the longest x4 118 us: chip_swap(): return lax.ppermute(value, ('xh', 'xl'), [(0, 3), (3, 0), (1, 2), (2, 1)])]
    reduce_scatter x3 -> x0, waiting for transfers between devices: 122 us -> none  [shards(): lax.psum_scatter(jnp.zeros((domain, modes, width), jnp.float32).at[recv_o...]
    scatter-add x5 -> x0, other arithmetic: 118 us -> none  [the longest x3 116 us: shards(): image = lax.psum_scatter(jnp.zeros((domain, modes, width), jnp.float32).a...]
    all_to_all x3 -> x1, waiting for transfers between devices: 190 us -> 85.8 us  [shards(): lax.all_to_all(packed, group, split_axis=0, concat_axis=0, tiled=True)]
    all_gather x4 -> x1, waiting for transfers between devices: 145 us -> 67.9 us  [shards(): gathered = lax.all_gather(start_modes[0], ('xh', 'xl'), axis=1, tiled=True)]
    dot_general x11 -> x0, matrix products: 67.5 us -> none  [the longest x3 41.9 us: shards(): jnp.einsum('skrc,smr->skmc', scaled, projected, preferred_element_type=jn...]
  transfers between devices with their start and end apart: 12 -> 22, of which waited for: 8 -> 19; matrix products, arithmetic and copies ran while one was open for 4% -> 1% of each run, Pallas kernels for 0% -> 1%
where the time goes in v1:
time: 863 us; the launch traced here: 862 us
  Pallas kernels  336 us (39%)
  waiting for transfers between devices  306 us (35%)
  blocking collectives  155 us (18%)
  starting transfers between devices  28.3 us (3%)
  between operations  14.4 us (2%)
  other arithmetic  11.7 us (1%)
  local copies, waits for them, and re-layouts  10 us (1%)
    pallas_call x1, Pallas kernels, pack(): pl.pallas_call(pack_kernel, out_shape=jax.ShapeDtypeStruct((slots,) + blo...  257 us
    all_gather x1, blocking collectives, shards(): tables = lax.all_gather(table, group, axis=0, tiled=False)  155 us
    ppermute x4, waiting for transfers between devices, chip_swap(): return lax.ppermute(value, ('xh', 'xl'), [(0, 3), (3, 0), (1, 2), (2, 1)])  118 us
    all_to_all x1, waiting for transfers between devices, shards(): lax.all_to_all(packed, group, split_axis=0, concat_axis=0, tiled=True)  85.8 us
    all_gather x1, waiting for transfers between devices, shards(): gathered = lax.all_gather(start_modes[0], ('xh', 'xl'), axis=1, tiled=True)  67.9 us
    pallas_call x3, Pallas kernels, apply_rows(): pl.pallas_call(functools.partial(apply_kernel, first, group, unroll), out...  41 us
    ppermute x11, waiting for transfers between devices, core_swap(): return lax.ppermute(value, 'c', [(0, 1), (1, 0)])  24.8 us
    pallas_call x3, Pallas kernels, new_modes(): pl.pallas_call(solve_kernel, out_shape=jax.ShapeDtypeStruct(applied.shape...  19.2 us
  transfers between devices with their start and end apart: 22, of which 19 were waited for; matrix products, arithmetic and copies ran while one was open for 1% of the time, Pallas kernels for 1%

profile of v1, /device:TPU:6, one launch (start us, length us, event | category | flops | bytes accessed | tf_op | source)
XLA Modules:
  0.0 861.5 jit_solution(12080082332142609723)
XLA Ops:
  8.6 154.8 %all-gather.2 = s32[64,4,64]{2,1,0:T(4,128)S(1)} all-gather(s32[1,4,64]{2,1,0:T(4,128)S(1)} %add_bitcast_fusion), channel_id=2, replica_groups=mesh['y'=4,'z'=8,'c'=2,'xh'=2,'xl'=2] {'y','z','xl'}, dimensions={0}, use_global_device_ids=true | all-gather | bytes 66560 | tf_op jit(solution)/shard_map/all_gather | solution.py:363
  163.5 2.4 fusion.7
  167.0 256.9 %shard_map.68 = bf16[128,2,128,128]{3,2,1,0:T(8,128)(2,1)} custom-call(s32[128]{0:T(128)S(1)} %select_n.109.order, bf16[64,2,128,128]{3,2,1,0:T(8,128)(2,1)} %blocks.1), custom_call_target="tpu_custom_call" | custom-call | tf_op jit(solution)/shard_map/pallas_call | solution.py:44
  423.9 10.5 %all-to-all-start = ((bf16[128,2,128,128]{3,2,1,0:T(8,128)(2,1)}), bf16[128,2,128,128]{3,2,1,0:T(8,128)(2,1)}, u32[]{:S(2)}, u32[]{:S(2)}) async-start(bf16[128,2,128,128]{3,2,1,0:T(8,128)(2,1)} %shard_map.68), calls=%async_computation | async-start | bytes 16777216 | tf_op jit(solution)/shard_map/all_to_all | solution.py:360
  435.2 67.9 %all-gather.5.cloned.1.call-done = bf16[1,204,64,128]{3,2,1,0:T(8,128)(2,1)} async-done(((bf16[1,204,16,128]{3,2,1,0:T(8,128)(2,1)}), bf16[1,204,64,128]{3,2,1,0:T(8,128)(2,1)}) %all-gather.5.cloned.1.call-update) | async-done | bytes 3342352 | tf_op jit(solution)/shard_map/all_gather | solution.py:375
  505.2 85.8 %all-to-all-done.blk = bf16[128,2,128,128]{3,2,1,0:T(8,128)(2,1)} async-done(((bf16[128,2,128,128]{3,2,1,0:T(8,128)(2,1)}), bf16[128,2,128,128]{3,2,1,0:T(8,128)(2,1)}, u32[]{:S(2)}, u32[]{:S(2)}) %all-to-all-start) | async-done | bytes 8388640 | tf_op jit(solution)/shard_map/all_to_all | solution.py:360
  591.1 8.8 %shard_map.69 = f32[204,128]{1,0:T(8,128)S(1)} custom-call(s32[256]{0:T(256)S(1)} %reshape.134.offs, s32[128]{0:T(128)S(1)} %reshape.135.live, bf16[128,2,128,128]{3,2,1,0:T(8,128)(2,1)} %all-to-all-done.blk), custom_call_target="tpu_custom_call" | custom-call | tf_op jit(solution)/shard_map/pallas_call | solution.py:83
  602.3 3.5 collective-permute-start.1
  605.8 2.3 broadcast_select_fusion
  609.1 2.3 collective-permute-start.2
  611.4 2.4 constant_dynamic-slice_fusion
  613.8 2.1 collective-permute-done.3
  616.0 15.6 %shard_map.70 = (bf16[102,64,128]{2,1,0:T(8,128)(2,1)S(1)}, bf16[102,64,128]{2,1,0:T(8,128)(2,1)S(1)}, bf16[128,2,128,128]{3,2,1,0:T(8,128)(2,1)}) custom-call(s32[256]{0:T(256)S(1)} %reshape.134.offs, s32[128]{0:T(128)S(1)} %reshape.135.live, s32[1]{0:T(128)} %bitcast.15.core, bf16[128,2,128,128]{3,2,1,0:T(8,128)(2,1)} %all-to-all-done.blk, ...), custom_call_target="tpu_custom_call" | custom-call | tf_op jit(solution)/shard_map/pallas_call | solution.py:172
  631.7 3.5 collective-permute-done.5
  637.0 38.8 %collective-permute-done.6.two = bf16[102,64,128]{2,1,0:T(8,128)(2,1)S(1)} collective-permute-done((bf16[102,64,128]{2,1,0:T(8,128)(2,1)S(1)}, bf16[102,64,128]{2,1,0:T(8,128)(2,1)S(1)}, u32[]{:S(2)}, u32[]{:S(2)}) %collective-permute-start.6) | collective-permute-done | bytes 1671200 | tf_op jit(solution)/shard_map/ppermute | solution.py:334
  677.0 3.4 shard_map.71
  681.9 6.4 shard_map.72.own
  688.6 3.4 collective-permute-done.8.peer
  693.1 12.7 %shard_map.73 = (bf16[102,64,128]{2,1,0:T(8,128)(2,1)S(1)}, bf16[102,64,128]{2,1,0:T(8,128)(2,1)S(1)}) custom-call(s32[256]{0:T(256)S(1)} %reshape.134.offs, s32[128]{0:T(128)S(1)} %reshape.135.live, s32[1]{0:T(128)} %bitcast.15.core, bf16[128,2,128,128]{3,2,1,0:T(8,128)(2,1)} %get-tuple-element.16.blk, f32[204,128]{1,0:T(8,128)S(1)} %fusion.1.scale, ...), custom_call_target="tpu_custom_call" | custom-call | tf_op jit(solution)/shard_map/pallas_call | solution.py:172
  706.1 3.4 collective-permute-done.9
  711.2 38.9 %collective-permute-done.10.two = bf16[102,64,128]{2,1,0:T(8,128)(2,1)S(1)} collective-permute-done((bf16[102,64,128]{2,1,0:T(8,128)(2,1)S(1)}, bf16[102,64,128]{2,1,0:T(8,128)(2,1)S(1)}, u32[]{:S(2)}, u32[]{:S(2)}) %collective-permute-start.10) | collective-permute-done | bytes 1671200 | tf_op jit(solution)/shard_map/ppermute | solution.py:334
  751.3 3.4 shard_map.74
  755.9 6.4 shard_map.75.own
  762.6 3.4 collective-permute-done.12.peer
  767.2 12.7 %shard_map.76 = (bf16[102,64,128]{2,1,0:T(8,128)(2,1)S(1)}, bf16[102,64,128]{2,1,0:T(8,128)(2,1)S(1)}) custom-call(s32[256]{0:T(256)S(1)} %reshape.134.offs, s32[128]{0:T(128)S(1)} %reshape.135.live, s32[1]{0:T(128)} %bitcast.15.core, bf16[128,2,128,128]{3,2,1,0:T(8,128)(2,1)} %get-tuple-element.16.blk, f32[204,128]{1,0:T(8,128)S(1)} %fusion.1.scale, ...), custom_call_target="tpu_custom_call" | custom-call | tf_op jit(solution)/shard_map/pallas_call | solution.py:172
  780.1 3.4 collective-permute-done.13
  785.2 38.9 %collective-permute-done.14.two = bf16[102,64,128]{2,1,0:T(8,128)(2,1)S(1)} collective-permute-done((bf16[102,64,128]{2,1,0:T(8,128)(2,1)S(1)}, bf16[102,64,128]{2,1,0:T(8,128)(2,1)S(1)}, u32[]{:S(2)}, u32[]{:S(2)}) %collective-permute-start.14) | collective-permute-done | bytes 1671200 | tf_op jit(solution)/shard_map/ppermute | solution.py:334
  825.3 3.4 shard_map.77
  830.3 6.4 shard_map.78
  838.9 1.9 collective-permute-start.17
  842.1 3.6 collective-permute-start.19
  845.7 7.3 collective-permute-done.19
  (77 shorter events, 30.4 us)
Async XLA Ops:
  423.9 167.2 %all-to-all-start = ((bf16[128,2,128,128]{3,2,1,0:T(8,128)(2,1)}), bf16[128,2,128,128]{3,2,1,0:T(8,128)(2,1)}, u32[]{:S(2)}, u32[]{:S(2)}) async-start(bf16[128,2,128,128]{3,2,1,0:T(8,128)(2,1)} %shard_map.68), calls=%async_computation | async-start | bytes 16777216 | tf_op jit(solution)/shard_map/all_to_all | solution.py:360
  434.4 68.7 %all-gather.5.cloned.1.call-start = ((), (), s32[]{:S(2)}) async-start(), calls=%async_computation.1 | async-start | bytes 4177920 | tf_op jit(solution)/shard_map/all_gather | solution.py:375
  503.1 102.7 %collective-permute-start.4 = (bf16[204,64,128]{2,1,0:T(8,128)(2,1)}, bf16[204,64,128]{2,1,0:T(8,128)(2,1)}, u32[]{:S(2)}, u32[]{:S(2)}) collective-permute-start(bf16[204,64,128]{2,1,0:T(8,128)(2,1)} %bitcast.37), channel_id=1, source_target_pairs={{4,0},{1,5},{2,6},{7,3},{12,8},{9,13},{10,14},{15,11},{20,16},{17,... | collective-permute-start | bytes 10027016 | tf_op jit(solution)/shard_map/ppermute | solution.py:376
  591.1 14.7 %copy-start.2 = (bf16[1,204,64,128]{3,2,1,0:T(8,128)(2,1)S(1)}, bf16[1,204,64,128]{3,2,1,0:T(8,128)(2,1)}, u32[]{:S(2)}) copy-start(bf16[1,204,64,128]{3,2,1,0:T(8,128)(2,1)} %all-gather.5.cloned.1.call-done) | copy-start | bytes 10027012
  599.9 1.5 collective-permute-start
  602.3 6.8 collective-permute-start.1
  609.1 4.7 collective-permute-start.2
  611.4 4.5 collective-permute-start.3
  631.6 3.6 collective-permute-start.5
  636.0 39.8 %collective-permute-start.6 = (bf16[102,64,128]{2,1,0:T(8,128)(2,1)S(1)}, bf16[102,64,128]{2,1,0:T(8,128)(2,1)S(1)}, u32[]{:S(2)}, u32[]{:S(2)}) collective-permute-start(bf16[102,64,128]{2,1,0:T(8,128)(2,1)S(1)} %add_convert_fusion.2.one), channel_id=1, source_target_pairs={{0,3},{3,0},{1,2},{2,1},{4,7},{7,4},{5,6},{6,5},{8,11},{11,8},{9,1... | collective-permute-start | bytes 5013512 | tf_op jit(solution)/shard_map/ppermute | solution.py:334
  675.8 1.2 copy-start.3
  680.4 1.5 collective-permute-start.7
  688.3 3.7 copy-start.1
  688.3 3.6 collective-permute-start.8
  692.0 1.2 copy-start.7
  705.8 3.6 collective-permute-start.9
  710.2 39.9 %collective-permute-start.10 = (bf16[102,64,128]{2,1,0:T(8,128)(2,1)S(1)}, bf16[102,64,128]{2,1,0:T(8,128)(2,1)S(1)}, u32[]{:S(2)}, u32[]{:S(2)}) collective-permute-start(bf16[102,64,128]{2,1,0:T(8,128)(2,1)S(1)} %add_convert_fusion.1.one), channel_id=1, source_target_pairs={{0,3},{3,0},{1,2},{2,1},{4,7},{7,4},{5,6},{6,5},{8,11},{11,8},{9,1... | collective-permute-start | bytes 5013512 | tf_op jit(solution)/shard_map/ppermute | solution.py:334
  750.1 1.2 copy-start.5
  754.7 1.3 collective-permute-start.11
  762.3 3.7 copy-start
  762.4 3.6 collective-permute-start.12
  766.0 1.2 copy-start.6
  779.9 3.6 collective-permute-start.13
  784.2 39.9 %collective-permute-start.14 = (bf16[102,64,128]{2,1,0:T(8,128)(2,1)S(1)}, bf16[102,64,128]{2,1,0:T(8,128)(2,1)S(1)}, u32[]{:S(2)}, u32[]{:S(2)}) collective-permute-start(bf16[102,64,128]{2,1,0:T(8,128)(2,1)S(1)} %add_convert_fusion.one), channel_id=1, source_target_pairs={{0,3},{3,0},{1,2},{2,1},{4,7},{7,4},{5,6},{6,5},{8,11},{11,8},{9,1... | collective-permute-start | bytes 5013512 | tf_op jit(solution)/shard_map/ppermute | solution.py:334
  824.1 1.2 copy-start.4
  828.8 1.5 collective-permute-start.15
  836.9 1.8 collective-permute-start.16
  838.9 14.8 %collective-permute-start.17 = (bf16[204,16,128]{2,1,0:T(8,128)(2,1)S(1)}, bf16[204,16,128]{2,1,0:T(8,128)(2,1)S(1)}, u32[]{:S(2)}, u32[]{:S(2)}) collective-permute-start(bf16[204,16,128]{2,1,0:T(8,128)(2,1)S(1)} %maximum_select_fusion), channel_id=1, source_target_pairs={{0,5},{3,6},{5,0},{6,3},{8,13},{11,14},{13,8},{14,11},{16,21},{19,... | collective-permute-start | bytes 2506760 | tf_op jit(solution)/shard_map/ppermute | solution.py:418
  840.8 1.3 collective-permute-start.18
  842.1 11.0 %collective-permute-start.19 = (f32[64,64]{1,0:T(8,128)S(1)}, f32[64,64]{1,0:T(8,128)S(1)}, u32[]{:S(2)}, u32[]{:S(2)}) collective-permute-start(f32[64,64]{1,0:T(8,128)S(1)} %add.60), channel_id=1, source_target_pairs={{0,5},{3,6},{5,0},{6,3},{8,13},{11,14},{13,8},{14,11},{16,21},{19,... | collective-permute-start | bytes 49160 | tf_op jit(solution)/shard_map/ppermute | solution.py:419
Sparse Core Ops, SparseCore 0:
  437.1 65.9 all-gather.4

commit v2 on v1

--- a/solution.py
+++ b/solution.py
@@ -47,7 +47,7 @@
         grid_spec=pltpu.PrefetchScalarGridSpec(
             num_scalar_prefetch=1,
             grid=(1,),
-            in_specs=[pl.BlockSpec(memory_space=pl.ANY)],
+            in_specs=[pl.BlockSpec(blocks.shape, lambda i, *_: (0, 0, 0, 0))],
             out_specs=pl.BlockSpec(memory_space=pl.ANY),
             scratch_shapes=[pltpu.SemaphoreType.DMA((slots,))],
         ),
@@ -360,7 +360,10 @@
     received = lax.all_to_all(packed, group, split_axis=0, concat_axis=0, tiled=True)
 
     table = jnp.stack([targets, offsets[:, 0], offsets[:, 1], live], axis=0)
-    tables = lax.all_gather(table, group, axis=0, tiled=False)
+    tables = lax.all_gather(table.astype(jnp.float32), AXES, axis=0, tiled=False)
+    tables = tables.astype(jnp.int32).reshape(ny, nz, 2, 2, 2, 4, rows)
+    tables = lax.dynamic_index_in_dim(tables, c, 2, keepdims=False)
+    tables = lax.dynamic_index_in_dim(tables, xh, 2, keepdims=False).reshape(subs, 4, rows)
     here = ((y * nz + z) * 2 + own_side).astype(jnp.int32)
     index, valid = slot_rows(tables[:, 0, :], here[None], rows)
     index, valid = index[:, 0], valid[:, 0]

time: 863 us -> 601 us (0.70)
  Pallas kernels: 336 us -> 86.2 us
  blocking collectives: 155 us -> 121 us
  waiting for transfers between devices: 306 us -> 330 us
    pallas_call x1, Pallas kernels: 257 us -> 7.14 us  [pack(): pl.pallas_call(pack_kernel, out_shape=jax.ShapeDtypeStruct((slots,) + blo...]
    all_gather x1, blocking collectives: 155 us -> 121 us  [shards(): lax.all_gather(table.astype(jnp.float32), AXES, axis=0, tiled=False)]
    all_to_all x1, waiting for transfers between devices: 85.8 us -> 108 us  [shards(): lax.all_to_all(packed, group, split_axis=0, concat_axis=0, tiled=True)]
where the time goes in v2:
time: 601 us; the launch traced here: 600 us
  waiting for transfers between devices  330 us (55%)
  blocking collectives  121 us (20%)
  Pallas kernels  86.2 us (14%)
  starting transfers between devices  29.7 us (5%)
  between operations  14.5 us (2%)
  local copies, waits for them, and re-layouts  10.2 us (2%)
  other arithmetic  8.83 us (1%)
    all_gather x1, blocking collectives, shards(): lax.all_gather(table.astype(jnp.float32), AXES, axis=0, tiled=False)  121 us
    ppermute x4, waiting for transfers between devices, chip_swap(): return lax.ppermute(value, ('xh', 'xl'), [(0, 3), (3, 0), (1, 2), (2, 1)])  116 us
    all_to_all x1, waiting for transfers between devices, shards(): lax.all_to_all(packed, group, split_axis=0, concat_axis=0, tiled=True)  108 us
    all_gather x1, waiting for transfers between devices, shards(): gathered = lax.all_gather(start_modes[0], ('xh', 'xl'), axis=1, tiled=True)  70.5 us
    pallas_call x3, Pallas kernels, apply_rows(): pl.pallas_call(functools.partial(apply_kernel, first, group, unroll), out...  40.9 us
    ppermute x11, waiting for transfers between devices, core_swap(): return lax.ppermute(value, 'c', [(0, 1), (1, 0)])  24.7 us
    pallas_call x3, Pallas kernels, new_modes(): pl.pallas_call(solve_kernel, out_shape=jax.ShapeDtypeStruct(applied.shape...  19.2 us
  transfers between devices with their start and end apart: 22, of which 19 were waited for; matrix products, arithmetic and copies ran while one was open for 1% of the time, Pallas kernels for 1%

profile of v2, /device:TPU:6, one launch (start us, length us, event | category | flops | bytes accessed | tf_op | source)
XLA Modules:
  0.0 599.6 jit_solution(17337000115816661319)
XLA Ops:
  8.6 120.6 %all_gather.7 = f32[256,4,64]{2,1,0:T(4,128)S(1)} all-gather(f32[1,4,64]{2,1,0:T(4,128)S(1)} %add_convert_fusion.3), channel_id=1, replica_groups=mesh['y'=4,'z'=8,'c'=2,'xh'=2,'xl'=2] {'y','z','c','xh','xl'}, dimensions={0}, use_global_device_ids=true | all-gather | bytes 263168 | tf_op jit(solution)/shard_map/all_gather | solution.py:363
  130.1 7.1 %shard_map.68 = bf16[128,2,128,128]{3,2,1,0:T(8,128)(2,1)} custom-call(s32[128]{0:T(128)S(1)} %select_n.125.order, bf16[64,2,128,128]{3,2,1,0:T(8,128)(2,1)} %blocks.1), custom_call_target="tpu_custom_call" | custom-call | tf_op jit(solution)/shard_map/pallas_call | solution.py:44
  137.3 8.4 %all-to-all-start = ((bf16[128,2,128,128]{3,2,1,0:T(8,128)(2,1)}), bf16[128,2,128,128]{3,2,1,0:T(8,128)(2,1)}, u32[]{:S(2)}, u32[]{:S(2)}) async-start(bf16[128,2,128,128]{3,2,1,0:T(8,128)(2,1)} %shard_map.68), calls=%async_computation | async-start | bytes 16777216 | tf_op jit(solution)/shard_map/all_to_all | solution.py:360
  146.3 70.5 %all-gather.3.cloned.1.call-done = bf16[1,204,64,128]{3,2,1,0:T(8,128)(2,1)} async-done(((bf16[1,204,16,128]{3,2,1,0:T(8,128)(2,1)}), bf16[1,204,64,128]{3,2,1,0:T(8,128)(2,1)}) %all-gather.3.cloned.1.call-update) | async-done | bytes 3342352 | tf_op jit(solution)/shard_map/all_gather | solution.py:378
  218.9 108.5 %all-to-all-done.blk = bf16[128,2,128,128]{3,2,1,0:T(8,128)(2,1)} async-done(((bf16[128,2,128,128]{3,2,1,0:T(8,128)(2,1)}), bf16[128,2,128,128]{3,2,1,0:T(8,128)(2,1)}, u32[]{:S(2)}, u32[]{:S(2)}) %all-to-all-start) | async-done | bytes 8388640 | tf_op jit(solution)/shard_map/all_to_all | solution.py:360
  327.4 8.8 %shard_map.69 = f32[204,128]{1,0:T(8,128)S(1)} custom-call(s32[256]{0:T(256)S(1)} %reshape.204.offs, s32[128]{0:T(128)S(1)} %reshape.205.live, bf16[128,2,128,128]{3,2,1,0:T(8,128)(2,1)} %all-to-all-done.blk), custom_call_target="tpu_custom_call" | custom-call | tf_op jit(solution)/shard_map/pallas_call | solution.py:83
  338.7 5.8 collective-permute-start.1
  344.4 2.3 broadcast_select_fusion
  347.7 1.7 collective-permute-start.2
  349.8 2.4 constant_dynamic-slice_fusion
  352.3 1.7 collective-permute-done.3
  354.1 15.6 %shard_map.70 = (bf16[102,64,128]{2,1,0:T(8,128)(2,1)S(1)}, bf16[102,64,128]{2,1,0:T(8,128)(2,1)S(1)}, bf16[128,2,128,128]{3,2,1,0:T(8,128)(2,1)}) custom-call(s32[256]{0:T(256)S(1)} %reshape.204.offs, s32[128]{0:T(128)S(1)} %reshape.205.live, s32[1]{0:T(128)} %bitcast.16.core, bf16[128,2,128,128]{3,2,1,0:T(8,128)(2,1)} %all-to-all-done.blk, ...), custom_call_target="tpu_custom_call" | custom-call | tf_op jit(solution)/shard_map/pallas_call | solution.py:172
  369.8 3.5 collective-permute-done.5
  375.6 38.3 %collective-permute-done.6.two = bf16[102,64,128]{2,1,0:T(8,128)(2,1)S(1)} collective-permute-done((bf16[102,64,128]{2,1,0:T(8,128)(2,1)S(1)}, bf16[102,64,128]{2,1,0:T(8,128)(2,1)S(1)}, u32[]{:S(2)}, u32[]{:S(2)}) %collective-permute-start.6) | collective-permute-done | bytes 1671200 | tf_op jit(solution)/shard_map/ppermute | solution.py:334
  415.1 3.4 shard_map.71
  420.0 6.4 %shard_map.72.own = bf16[102,64,128]{2,1,0:T(8,128)(2,1)S(1)} custom-call(f32[64,64]{1,0:T(8,128)S(1)} %get-tuple-element.19.gram_one, f32[64,64]{1,0:T(8,128)S(1)} %collective-permute-done.7.gram_two, bf16[102,64,128]{2,1,0:T(8,128)(2,1)S(1)} %get-tuple-element.20.applied), custom_call_target="tpu_custom_call" | custom-call | tf_op jit(solution)/shard_map/pallas_call | solution.py:273
  426.7 3.4 collective-permute-done.8.peer
  431.2 12.7 %shard_map.73 = (bf16[102,64,128]{2,1,0:T(8,128)(2,1)S(1)}, bf16[102,64,128]{2,1,0:T(8,128)(2,1)S(1)}) custom-call(s32[256]{0:T(256)S(1)} %reshape.204.offs, s32[128]{0:T(128)S(1)} %reshape.205.live, s32[1]{0:T(128)} %bitcast.16.core, bf16[128,2,128,128]{3,2,1,0:T(8,128)(2,1)} %get-tuple-element.16.blk, f32[204,128]{1,0:T(8,128)S(1)} %fusion.1.scale, ...), custom_call_target="tpu_custom_call" | custom-call | tf_op jit(solution)/shard_map/pallas_call | solution.py:172
  444.2 3.4 collective-permute-done.9
  449.7 38.4 %collective-permute-done.10.two = bf16[102,64,128]{2,1,0:T(8,128)(2,1)S(1)} collective-permute-done((bf16[102,64,128]{2,1,0:T(8,128)(2,1)S(1)}, bf16[102,64,128]{2,1,0:T(8,128)(2,1)S(1)}, u32[]{:S(2)}, u32[]{:S(2)}) %collective-permute-start.10) | collective-permute-done | bytes 1671200 | tf_op jit(solution)/shard_map/ppermute | solution.py:334
  489.4 3.4 shard_map.74
  494.0 6.4 %shard_map.75.own = bf16[102,64,128]{2,1,0:T(8,128)(2,1)S(1)} custom-call(f32[64,64]{1,0:T(8,128)S(1)} %get-tuple-element.23.gram_one, f32[64,64]{1,0:T(8,128)S(1)} %collective-permute-done.11.gram_two, bf16[102,64,128]{2,1,0:T(8,128)(2,1)S(1)} %get-tuple-element.24.applied), custom_call_target="tpu_custom_call" | custom-call | tf_op jit(solution)/shard_map/pallas_call | solution.py:273
  500.7 3.4 collective-permute-done.12.peer
  505.3 12.7 %shard_map.76 = (bf16[102,64,128]{2,1,0:T(8,128)(2,1)S(1)}, bf16[102,64,128]{2,1,0:T(8,128)(2,1)S(1)}) custom-call(s32[256]{0:T(256)S(1)} %reshape.204.offs, s32[128]{0:T(128)S(1)} %reshape.205.live, s32[1]{0:T(128)} %bitcast.16.core, bf16[128,2,128,128]{3,2,1,0:T(8,128)(2,1)} %get-tuple-element.16.blk, f32[204,128]{1,0:T(8,128)S(1)} %fusion.1.scale, ...), custom_call_target="tpu_custom_call" | custom-call | tf_op jit(solution)/shard_map/pallas_call | solution.py:172
  518.2 3.4 collective-permute-done.13
  523.8 38.4 %collective-permute-done.14.two = bf16[102,64,128]{2,1,0:T(8,128)(2,1)S(1)} collective-permute-done((bf16[102,64,128]{2,1,0:T(8,128)(2,1)S(1)}, bf16[102,64,128]{2,1,0:T(8,128)(2,1)S(1)}, u32[]{:S(2)}, u32[]{:S(2)}) %collective-permute-start.14) | collective-permute-done | bytes 1671200 | tf_op jit(solution)/shard_map/ppermute | solution.py:334
  563.4 3.4 shard_map.77
  568.4 6.4 %shard_map.78 = bf16[102,64,128]{2,1,0:T(8,128)(2,1)S(1)} custom-call(f32[64,64]{1,0:T(8,128)S(1)} %get-tuple-element.27.gram_one, f32[64,64]{1,0:T(8,128)S(1)} %collective-permute-done.15.gram_two, bf16[102,64,128]{2,1,0:T(8,128)(2,1)S(1)} %get-tuple-element.28.applied), custom_call_target="tpu_custom_call" | custom-call | tf_op jit(solution)/shard_map/pallas_call | solution.py:273
  575.2 1.6 collective-permute-done.16
  577.0 1.9 collective-permute-start.17
  580.2 3.6 collective-permute-start.19
  583.8 7.3 %collective-permute-done.19 = f32[64,64]{1,0:T(8,128)S(1)} collective-permute-done((f32[64,64]{1,0:T(8,128)S(1)}, f32[64,64]{1,0:T(8,128)S(1)}, u32[]{:S(2)}, u32[]{:S(2)}) %collective-permute-start.19) | collective-permute-done | bytes 16416 | tf_op jit(solution)/shard_map/ppermute | solution.py:422
  (83 shorter events, 30.4 us)
Async XLA Ops:
  7.2 122.5 %copy-start.8 = (s32[64,1]{0,1:T(1,128)S(1)}, s32[64,1]{0,1:T(1,128)}, u32[]{:S(2)}) copy-start(s32[64,1]{0,1:T(1,128)} %param.6) | copy-start | bytes 772
  137.3 190.2 %all-to-all-start = ((bf16[128,2,128,128]{3,2,1,0:T(8,128)(2,1)}), bf16[128,2,128,128]{3,2,1,0:T(8,128)(2,1)}, u32[]{:S(2)}, u32[]{:S(2)}) async-start(bf16[128,2,128,128]{3,2,1,0:T(8,128)(2,1)} %shard_map.68), calls=%async_computation | async-start | bytes 16777216 | tf_op jit(solution)/shard_map/all_to_all | solution.py:360
  145.6 71.2 %all-gather.3.cloned.1.call-start = ((), (), s32[]{:S(2)}) async-start(), calls=%async_computation.1 | async-start | bytes 4177920 | tf_op jit(solution)/shard_map/all_gather | solution.py:378
  216.8 127.6 %collective-permute-start.4 = (bf16[204,64,128]{2,1,0:T(8,128)(2,1)}, bf16[204,64,128]{2,1,0:T(8,128)(2,1)}, u32[]{:S(2)}, u32[]{:S(2)}) collective-permute-start(bf16[204,64,128]{2,1,0:T(8,128)(2,1)} %bitcast.40), channel_id=1, source_target_pairs={{4,0},{1,5},{2,6},{7,3},{12,8},{9,13},{10,14},{15,11},{20,16},{17,... | collective-permute-start | bytes 10027016 | tf_op jit(solution)/shard_map/ppermute | solution.py:379
  327.4 17.0 %copy-start.2 = (bf16[1,204,64,128]{3,2,1,0:T(8,128)(2,1)S(1)}, bf16[1,204,64,128]{3,2,1,0:T(8,128)(2,1)}, u32[]{:S(2)}) copy-start(bf16[1,204,64,128]{3,2,1,0:T(8,128)(2,1)} %all-gather.3.cloned.1.call-done) | copy-start | bytes 10027012
  336.2 1.5 collective-permute-start
  338.7 9.0 %collective-permute-start.1 = (f32[204,128]{1,0:T(8,128)S(1)}, f32[204,128]{1,0:T(8,128)S(1)}, u32[]{:S(2)}, u32[]{:S(2)}) collective-permute-start(f32[204,128]{1,0:T(8,128)S(1)} %add.65), channel_id=1, source_target_pairs={{0,3},{3,0},{1,2},{2,1},{4,7},{7,4},{5,6},{6,5},{8,11},{11,8},{9,1... | collective-permute-start | bytes 313352 | tf_op jit(solution)/shard_map/ppermute | solution.py:334
  347.7 4.6 collective-permute-start.2
  349.5 4.5 collective-permute-start.3
  369.7 3.6 collective-permute-start.5
  374.1 39.8 %collective-permute-start.6 = (bf16[102,64,128]{2,1,0:T(8,128)(2,1)S(1)}, bf16[102,64,128]{2,1,0:T(8,128)(2,1)S(1)}, u32[]{:S(2)}, u32[]{:S(2)}) collective-permute-start(bf16[102,64,128]{2,1,0:T(8,128)(2,1)S(1)} %add_convert_fusion.2.one), channel_id=1, source_target_pairs={{0,3},{3,0},{1,2},{2,1},{4,7},{7,4},{5,6},{6,5},{8,11},{11,8},{9,1... | collective-permute-start | bytes 5013512 | tf_op jit(solution)/shard_map/ppermute | solution.py:334
  413.9 1.2 copy-start.3
  418.5 1.5 collective-permute-start.7
  426.4 3.7 copy-start.1
  426.4 3.6 collective-permute-start.8
  430.0 1.2 copy-start.7
  443.9 3.6 collective-permute-start.9
  448.3 39.9 %collective-permute-start.10 = (bf16[102,64,128]{2,1,0:T(8,128)(2,1)S(1)}, bf16[102,64,128]{2,1,0:T(8,128)(2,1)S(1)}, u32[]{:S(2)}, u32[]{:S(2)}) collective-permute-start(bf16[102,64,128]{2,1,0:T(8,128)(2,1)S(1)} %add_convert_fusion.1.one), channel_id=1, source_target_pairs={{0,3},{3,0},{1,2},{2,1},{4,7},{7,4},{5,6},{6,5},{8,11},{11,8},{9,1... | collective-permute-start | bytes 5013512 | tf_op jit(solution)/shard_map/ppermute | solution.py:334
  488.2 1.2 copy-start.5
  492.7 1.3 collective-permute-start.11
  500.4 3.7 copy-start
  500.4 3.6 collective-permute-start.12
  504.1 1.2 copy-start.6
  517.9 3.6 collective-permute-start.13
  522.3 39.9 %collective-permute-start.14 = (bf16[102,64,128]{2,1,0:T(8,128)(2,1)S(1)}, bf16[102,64,128]{2,1,0:T(8,128)(2,1)S(1)}, u32[]{:S(2)}, u32[]{:S(2)}) collective-permute-start(bf16[102,64,128]{2,1,0:T(8,128)(2,1)S(1)} %add_convert_fusion.one), channel_id=1, source_target_pairs={{0,3},{3,0},{1,2},{2,1},{4,7},{7,4},{5,6},{6,5},{8,11},{11,8},{9,1... | collective-permute-start | bytes 5013512 | tf_op jit(solution)/shard_map/ppermute | solution.py:334
  562.2 1.2 copy-start.4
  566.9 1.5 collective-permute-start.15
  575.0 1.8 collective-permute-start.16
  577.0 14.8 %collective-permute-start.17 = (bf16[204,16,128]{2,1,0:T(8,128)(2,1)S(1)}, bf16[204,16,128]{2,1,0:T(8,128)(2,1)S(1)}, u32[]{:S(2)}, u32[]{:S(2)}) collective-permute-start(bf16[204,16,128]{2,1,0:T(8,128)(2,1)S(1)} %maximum_select_fusion), channel_id=1, source_target_pairs={{0,5},{3,6},{5,0},{6,3},{8,13},{11,14},{13,8},{14,11},{16,21},{19,... | collective-permute-start | bytes 2506760 | tf_op jit(solution)/shard_map/ppermute | solution.py:421
  578.9 1.3 collective-permute-start.18
  580.2 11.0 %collective-permute-start.19 = (f32[64,64]{1,0:T(8,128)S(1)}, f32[64,64]{1,0:T(8,128)S(1)}, u32[]{:S(2)}, u32[]{:S(2)}) collective-permute-start(f32[64,64]{1,0:T(8,128)S(1)} %add.77), channel_id=1, source_target_pairs={{0,5},{3,6},{5,0},{6,3},{8,13},{11,14},{13,8},{14,11},{16,21},{19,... | collective-permute-start | bytes 49160 | tf_op jit(solution)/shard_map/ppermute | solution.py:422
Sparse Core Ops, SparseCore 0:
  148.3 68.5 all-gather.2

commit v3 on v2

--- a/solution.py
+++ b/solution.py
@@ -14,7 +14,9 @@
 DAMPING = 32.0
 AXES = ("y", "z", "c", "xh", "xl")
 NT = (((1,), (1,)), ((), ()))
-VMEM_LIMIT = 50 * 2**20
+VMEM_LIMIT = 20 * 2**20
+PACK_LIMIT = 50 * 2**20
+SMALL_LIMIT = 12 * 2**20
 
 
 def nt_dot(left, right):
@@ -51,7 +53,7 @@
             out_specs=pl.BlockSpec(memory_space=pl.ANY),
             scratch_shapes=[pltpu.SemaphoreType.DMA((slots,))],
         ),
-        compiler_params=pltpu.CompilerParams(vmem_limit_bytes=VMEM_LIMIT),
+        compiler_params=pltpu.CompilerParams(vmem_limit_bytes=PACK_LIMIT),
     )(order, blocks)
 
 
@@ -189,75 +191,114 @@
             ],
         ),
         compiler_params=pltpu.CompilerParams(vmem_limit_bytes=VMEM_LIMIT),
+        cost_estimate=pl.CostEstimate(
+            flops=10**10, bytes_accessed=12 * 10**6, transcendentals=0
+        ),
     )(offs, live, core, blocks, scale, own, peer)
 
 
-def image_kernel(with_ritz, one, two, own, damped, applied, gram, *rest):
-    step = pl.program_id(0)
-    ritz = rest[0] if with_ritz else None
-
-    @pl.when(step == 0)
+def image_kernel(second, with_ritz, *refs):
+    one, two, own, damped, *rest = refs
+    before = rest.pop(0) if second else None
+    own_before = rest.pop(0) if with_ritz else None
+    applied, gram = rest[:2]
+    ritz = rest[2] if with_ritz else None
+
+    @pl.when(pl.program_id(0) == 0)
     def _():
         gram[...] = jnp.zeros_like(gram)
         if with_ritz:
             ritz[...] = jnp.zeros_like(ritz)
 
     gram_part = jnp.zeros(gram.shape, jnp.float32)
-    ritz_part = jnp.zeros(gram.shape, jnp.float32)
+    ritz_part = jnp.zeros(ritz.shape, jnp.float32) if with_ritz else None
     for i in range(0, one.shape[0], 2):
-        values, olds = [], []
+        values = []
         for l in (i, i + 1):
-            old = own[l]
             total = one[l].astype(jnp.float32) + two[l].astype(jnp.float32)
-            value = (total + damped[l] * old.astype(jnp.float32)).astype(jnp.bfloat16)
+            old = own[l].astype(jnp.float32)
+            value = (total + damped[l] * old).astype(jnp.bfloat16)
             applied[l] = value
             values.append(value)
-            olds.append(old)
         value = jnp.concatenate(values, axis=1)
-        gram_part += nt_dot(value, value)
+        everything = value
+        if second:
+            earlier = jnp.concatenate([before[i], before[i + 1]], axis=1)
+            everything = jnp.concatenate([earlier, value], axis=0)
+        gram_part += nt_dot(value, everything)
         if with_ritz:
-            ritz_part += nt_dot(jnp.concatenate(olds, axis=1), value)
+            olds = [jnp.concatenate([own_before[l], own[l]], axis=0) for l in (i, i + 1)]
+            ritz_part += nt_dot(jnp.concatenate(olds, axis=1), everything)
     gram[...] += gram_part
     if with_ritz:
         ritz[...] += ritz_part
 
 
-def form_image(with_ritz, one, two, own, damped, steps=3):
+def form_image(one, two, own, damped, before=(), with_ritz=False, steps=3):
     half, modes, _ = own.shape
     part = half // steps
+    second = len(before) > 0
     part_spec = pl.BlockSpec((part, modes, BLK), lambda i: (i, 0, 0))
-    square_spec = pl.BlockSpec((modes, modes), lambda i: (0, 0))
-    square_shape = jax.ShapeDtypeStruct((modes, modes), jnp.float32)
-    squares = 2 if with_ritz else 1
+    shapes = [(modes, 2 * modes if second else modes)] + [(2 * modes, 2 * modes)] * with_ritz
     return pl.pallas_call(
-        functools.partial(image_kernel, with_ritz),
-        out_shape=[jax.ShapeDtypeStruct(own.shape, jnp.bfloat16)] + [square_shape] * squares,
+        functools.partial(image_kernel, second, with_ritz),
+        out_shape=[jax.ShapeDtypeStruct(own.shape, jnp.bfloat16)]
+        + [jax.ShapeDtypeStruct(shape, jnp.float32) for shape in shapes],
         grid=(steps,),
-        in_specs=[part_spec] * 3 + [pl.BlockSpec((part, 1, BLK), lambda i: (i, 0, 0))],
-        out_specs=[part_spec] + [square_spec] * squares,
-        compiler_params=pltpu.CompilerParams(vmem_limit_bytes=VMEM_LIMIT),
-    )(one, two, own, damped)
-
-
-def inverse_factor(gram):
+        in_specs=[part_spec] * 3
+        + [pl.BlockSpec((part, 1, BLK), lambda i: (i, 0, 0))]
+        + [part_spec] * len(before),
+        out_specs=[part_spec] + [pl.BlockSpec(shape, lambda i: (0, 0)) for shape in shapes],
+        compiler_params=pltpu.CompilerParams(vmem_limit_bytes=SMALL_LIMIT),
+        cost_estimate=pl.CostEstimate(flops=10**9, bytes_accessed=4 * 10**6, transcendentals=0),
+    )(one, two, own, damped, *before)
+
+
+def exact(left, right, dims):
+    return lax.dot_general(
+        left, right, (dims, ((), ())), precision=lax.Precision.HIGHEST,
+        preferred_element_type=jnp.float32,
+    )
+
+
+def eliminate(work, size, at):
+    row_at = lax.broadcasted_iota(jnp.int32, work.shape, 0)
+    for j in range(size):
+        root = lax.rsqrt(work[j : j + 1, at + j : at + j + 1])
+        row = work[j : j + 1, :] * root
+        factor = jnp.where(row_at[:, :1] > j, work[:, at + j : at + j + 1] * root, 0.0)
+        work = jnp.where(row_at == j, row, work - factor * row)
+    return work
+
+
+def unit(size):
+    at = lax.broadcasted_iota(jnp.int32, (size, size), 0)
+    return (at == lax.broadcasted_iota(jnp.int32, (size, size), 1)).astype(jnp.float32)
+
+
+def first_inverse(gram):
     size = gram.shape[0]
-    both = (size, 2 * size)
-    row_at = lax.broadcasted_iota(jnp.int32, both, 0)
-    col_at = lax.broadcasted_iota(jnp.int32, both, 1)
-    eye = (col_at == row_at + size).astype(jnp.float32)
-    work = jnp.where(col_at < size, jnp.concatenate([gram, gram], axis=1), eye)
-    for j in range(size):
-        root = lax.rsqrt(work[j : j + 1, j : j + 1])
-        row = work[j : j + 1, :] * root
-        factor = jnp.where(row_at[:, :1] > j, work[:, j : j + 1] * root, 0.0)
-        work = jnp.where(row_at == j, row, work - factor * row)
-    return work[:, size:]
-
-
-def solve_kernel(gram_one, gram_two, applied, new, inverse):
+    none = jnp.zeros((size, size), jnp.float32)
+    work = jnp.concatenate([unit(size), none, gram, none], axis=1)
+    return eliminate(work, size, 2 * size)[:, :size]
+
+
+def second_inverse(gram, first):
+    size = first.shape[0]
+    cross = exact(gram[:, :size], first, ((1,), (1,)))
+    rest = gram[:, size:] - exact(cross, cross, ((1,), (1,)))
+    left = -exact(cross, first, ((1,), (0,)))
+    none = jnp.zeros((size, size), jnp.float32)
+    work = jnp.concatenate([left, unit(size), rest, none], axis=1)
+    return eliminate(work, size, 2 * size)[:, : 2 * size]
+
+
+def first_kernel(gram_one, gram_two, applied, new, first, inverse):
     @pl.when(pl.program_id(0) == 0)
     def _():
-        inverse[...] = inverse_factor(gram_one[...] + gram_two[...]).astype(jnp.bfloat16)
+        value = first_inverse(gram_one[...] + gram_two[...])
+        first[...] = value
+        inverse[...] = value.astype(jnp.bfloat16)
 
     for i in range(0, applied.shape[0], 2):
         pair = jnp.concatenate([applied[i], applied[i + 1]], axis=1)
@@ -266,19 +307,58 @@
         new[i + 1] = value[:, BLK:].astype(jnp.bfloat16)
 
 
-def new_modes(gram_one, gram_two, applied, steps=3):
+def second_kernel(upper, gram_one, gram_two, first, before, applied, new, inverse):
+    @pl.when(pl.program_id(0) == 0)
+    def _():
+        value = second_inverse(gram_one[...] + gram_two[...], first[...])
+        above = jnp.concatenate([first[...], jnp.zeros_like(first)], axis=1)
+        inverse[...] = jnp.where(upper[0] == 1, above, value).astype(jnp.bfloat16)
+
+    for i in range(0, applied.shape[0], 2):
+        both = [jnp.concatenate([before[l], applied[l]], axis=0) for l in (i, i + 1)]
+        pair = jnp.concatenate(both, axis=1)
+        value = jnp.dot(inverse[...], pair, preferred_element_type=jnp.float32)
+        new[i] = value[:, :BLK].astype(jnp.bfloat16)
+        new[i + 1] = value[:, BLK:].astype(jnp.bfloat16)
+
+
+def first_modes(gram_one, gram_two, applied, steps=3):
     half, modes, _ = applied.shape
     part_spec = pl.BlockSpec((half // steps, modes, BLK), lambda i: (i, 0, 0))
     square_spec = pl.BlockSpec((modes, modes), lambda i: (0, 0))
     return pl.pallas_call(
-        solve_kernel,
-        out_shape=jax.ShapeDtypeStruct(applied.shape, jnp.bfloat16),
+        first_kernel,
+        out_shape=[
+            jax.ShapeDtypeStruct(applied.shape, jnp.bfloat16),
+            jax.ShapeDtypeStruct((modes, modes), jnp.float32),
+        ],
         grid=(steps,),
         in_specs=[square_spec, square_spec, part_spec],
-        out_specs=part_spec,
+        out_specs=[part_spec, square_spec],
         scratch_shapes=[pltpu.VMEM((modes, modes), jnp.bfloat16)],
-        compiler_params=pltpu.CompilerParams(vmem_limit_bytes=VMEM_LIMIT),
+        compiler_params=pltpu.CompilerParams(vmem_limit_bytes=SMALL_LIMIT),
+        cost_estimate=pl.CostEstimate(flops=3 * 10**9, bytes_accessed=10**6, transcendentals=0),
     )(gram_one, gram_two, applied)
+
+
+def second_modes(upper, gram_one, gram_two, first, before, applied, steps=3):
+    half, modes, _ = applied.shape
+    part_spec = pl.BlockSpec((half // steps, modes, BLK), lambda i, *_: (i, 0, 0))
+    rows_spec = pl.BlockSpec((modes, 2 * modes), lambda i, *_: (0, 0))
+    square_spec = pl.BlockSpec((modes, modes), lambda i, *_: (0, 0))
+    return pl.pallas_call(
+        second_kernel,
+        out_shape=jax.ShapeDtypeStruct(applied.shape, jnp.bfloat16),
+        grid_spec=pltpu.PrefetchScalarGridSpec(
+            num_scalar_prefetch=1,
+            grid=(steps,),
+            in_specs=[rows_spec, rows_spec, square_spec, part_spec, part_spec],
+            out_specs=part_spec,
+            scratch_shapes=[pltpu.VMEM((modes, 2 * modes), jnp.bfloat16)],
+        ),
+        compiler_params=pltpu.CompilerParams(vmem_limit_bytes=SMALL_LIMIT),
+        cost_estimate=pl.CostEstimate(flops=3 * 10**9, bytes_accessed=10**6, transcendentals=0),
+    )(upper, gram_one, gram_two, first, before, applied)
 
 
 def side(xh, xl):
@@ -300,11 +380,12 @@
     ]
 
 
-def next_pairs(ny, nz):
+def next_pairs(ny, nz, cross):
     pairs = []
     for y, z, c, xh, xl in every(ny, nz):
         sub = ((y * nz + z) * 2 + side(xh, xl) + 1) % (ny * nz * 2)
-        there = (sub // (2 * nz), sub // 2 % nz, c, xh, xh ^ (1 - sub % 2))
+        to = xh ^ cross
+        there = (sub // (2 * nz), sub // 2 % nz, c, to, to ^ (1 - sub % 2))
         pairs.append((flat(ny, nz, y, z, c, xh, xl), flat(ny, nz, *there)))
     return pairs
 
@@ -326,6 +407,12 @@
     ]
 
 
+def start_pairs(mask):
+    return [
+        (side(x // 2, x % 2) * 4 + (x ^ mask), side(x // 2, x % 2) * 4 + x) for x in range(4)
+    ]
+
+
 def core_swap(value):
     return lax.ppermute(value, "c", [(0, 1), (1, 0)])
 
@@ -345,7 +432,6 @@
 
 def shards(ny, nz, blocks, routes, offsets, live, start_modes):
     y, z, c, xh, xl = [lax.axis_index(axis) for axis in AXES]
-    chip = 2 * xh + xl
     own_side = 1 - (xh ^ xl)
     subs = ny * nz * 2
     rows = blocks.shape[0]
@@ -356,11 +442,14 @@
     targets = routes[:, 0]
     wanted = jnp.arange(subs, dtype=jnp.int32) ^ (1 - xh)
     order, _ = slot_rows(targets, wanted, rows)
-    packed = pack(blocks, order.reshape(-1))
+    table = jnp.stack([targets, offsets[:, 0], offsets[:, 1], live], axis=0)
+    table = jnp.pad(table.astype(jnp.float32), ((0, 4), (0, BLK - rows)))
+    packed, table, start_modes = lax.optimization_barrier(
+        (pack(blocks, order.reshape(-1)), table, start_modes)
+    )
     received = lax.all_to_all(packed, group, split_axis=0, concat_axis=0, tiled=True)
 
-    table = jnp.stack([targets, offsets[:, 0], offsets[:, 1], live], axis=0)
-    tables = lax.all_gather(table.astype(jnp.float32), AXES, axis=0, tiled=False)
+    tables = lax.all_gather(table, AXES, axis=0, tiled=False)[:, :4, :rows]
     tables = tables.astype(jnp.int32).reshape(ny, nz, 2, 2, 2, 4, rows)
     tables = lax.dynamic_index_in_dim(tables, c, 2, keepdims=False)
     tables = lax.dynamic_index_in_dim(tables, xh, 2, keepdims=False).reshape(subs, 4, rows)
@@ -375,43 +464,82 @@
     offs = jnp.stack(picked[:2], axis=-1).reshape(-1)
     alive = picked[2].reshape(-1)
 
-    gathered = lax.all_gather(start_modes[0], ("xh", "xl"), axis=1, tiled=True)
+    by = [start_modes[0]] + [
+        lax.ppermute(start_modes[0], ("c", "xh", "xl"), start_pairs(mask)) for mask in (1, 2, 3)
+    ]
+    quarters = []
+    for q in range(4):
+        near = [jnp.where(xl == q % 2, by[2 * m], by[2 * m + 1]) for m in range(2)]
+        quarters.append(jnp.where(xh == q // 2, near[0], near[1]))
+    gathered = jnp.concatenate(quarters, axis=1)
     sibling = lax.ppermute(gathered, ("c", "xh", "xl"), spread_pairs())
     start = jnp.where(c == own_side, gathered, sibling)
-    own = lax.dynamic_slice_in_dim(start, c * half, half, 0)
-    peer = lax.dynamic_slice_in_dim(start, (1 - c) * half, half, 0)
+    cut = start.shape[1] // 2
+    owns, peers = [
+        [
+            lax.dynamic_slice(start, (at * half, h * cut, 0), (half, cut, BLK))
+            for h in range(2)
+        ]
+        for at in (c, 1 - c)
+    ]
 
     sums = column_sums(received, offs, alive, domain)
     sums = sums + core_swap(sums)
-    sums = sums + chip_swap(sums)
-    forward = next_pairs(ny, nz)
-    backward = [(there, here_) for here_, there in forward]
-    low = lax.ppermute(sums[domain - OV :], AXES, forward)
-    high = lax.ppermute(sums[:OV], AXES, backward)
-    column_sq = sums + jnp.concatenate(
-        [low, jnp.zeros((domain - 2 * OV, BLK), jnp.float32), high], axis=0
+    low, high = [], []
+    for cross in range(2):
+        forward = next_pairs(ny, nz, cross)
+        backward = [(there, here_) for here_, there in forward]
+        low.append(lax.ppermute(sums[domain - OV :], AXES, forward))
+        high.append(lax.ppermute(sums[:OV], AXES, backward))
+    column_sq = (sums + chip_swap(sums)) + jnp.concatenate(
+        [low[0] + low[1], jnp.zeros((domain - 2 * OV, BLK), jnp.float32), high[0] + high[1]],
+        axis=0,
     )
     scale = lax.rsqrt(column_sq + DAMPING)
     damped = lax.dynamic_slice_in_dim(DAMPING * scale * scale, c * half, half, 0)[:, None, :]
 
     core = c.astype(jnp.int32)[None]
+    def apply_half(h, first=False):
+        return apply_rows(first, work, offs, alive, core, scale, owns[h], peers[h])
+
+    def add_cores(keep, send, after=None):
+        other = core_swap(send)
+        if after is not None:
+            keep, _ = lax.optimization_barrier((keep, after))
+        return (keep.astype(jnp.float32) + other.astype(jnp.float32)).astype(jnp.bfloat16)
+
     work = received
+    lower = jnp.zeros((1,), jnp.int32)
+    keep, send, work = apply_half(0, True)
+    one = add_cores(keep, send)
+    one, owns[1] = lax.optimization_barrier((one, owns[1]))
     for step in range(ITERS):
-        keep, send, *scaled = apply_rows(step == 0, work, offs, alive, core, scale, own, peer)
-        if step == 0:
-            work = scaled[0]
-        other = core_swap(send)
-        chip_sum = (keep.astype(jnp.float32) + other.astype(jnp.float32)).astype(jnp.bfloat16)
         last = step == ITERS - 1
-        applied, gram, *ritz = form_image(last, chip_sum, chip_swap(chip_sum), own, damped)
-        own = new_modes(gram, core_swap(gram), applied)
-        if not last:
-            peer = core_swap(own)
-
-    ritz = ritz[0] + core_swap(ritz[0])
+        one_there = chip_swap(one)
+        two = apply_half(1)
+        before, gram = form_image(one, one_there, owns[0], damped)
+        two = add_cores(*two, after=gram)
+        two_there = chip_swap(two)
+        new, first = first_modes(gram, core_swap(gram), before)
+        if last:
+            two_there, first = lax.optimization_barrier((two_there, first))
+            applied, gram, ritz = form_image(
+                two, two_there, owns[1], damped, (before, owns[0]), True
+            )
+            upper = (1 - xh).astype(jnp.int32)[None]
+            out = second_modes(upper, gram, core_swap(gram), first, before, applied)
+        else:
+            owns[0], peers[0] = new, core_swap(new)
+            one = apply_half(0)
+            applied, gram = form_image(two, two_there, owns[1], damped, (before,))
+            one = add_cores(*one, after=gram)
+            new = second_modes(lower, gram, core_swap(gram), first, before, applied)
+            owns[1], peers[1] = new, core_swap(new)
+
+    ritz = ritz + core_swap(ritz)
     at_home = c == own_side
-    mine = lax.dynamic_slice_in_dim(own, chip * share, share, 1)
-    beside = lax.dynamic_slice_in_dim(own, (chip ^ 1) * share, share, 1)
+    mine = lax.dynamic_slice_in_dim(out, xl * share, share, 1)
+    beside = lax.dynamic_slice_in_dim(out, (1 - xl) * share, share, 1)
     held = jnp.where(at_home, mine, beside)
     swapped = core_swap(jnp.where(at_home, beside, mine))
     whole = jnp.where(

time: 601 us -> 455 us (0.76)
  blocking collectives: 121 us -> 0 us
  waiting for transfers between devices: 330 us -> 277 us
  starting transfers between devices: 29.7 us -> 47.6 us
  Pallas kernels: 86.2 us -> 98.4 us
  local copies, waits for them, and re-layouts: 10.2 us -> 3.87 us
    all_gather x1 -> x0, blocking collectives: 121 us -> none  [shards(): lax.all_gather(table.astype(jnp.float32), AXES, axis=0, tiled=False)]
    all_to_all x1, waiting for transfers between devices: 108 us -> 33.5 us  [shards(): lax.all_to_all(packed, group, split_axis=0, concat_axis=0, tiled=True)]
    ppermute x2 -> x7, waiting for transfers between devices: 1.7 us -> 45.3 us  [the longest x3 44.6 us: shards(): lax.ppermute(start_modes[0], ('c', 'xh', 'xl'), start_pairs(mask))]
    ppermute x4 -> x7, waiting for transfers between devices: 116 us -> 86.4 us  [chip_swap(): return lax.ppermute(value, ('xh', 'xl'), [(0, 3), (3, 0), (1, 2), (2, 1)])]
    all_gather x1, waiting for transfers between devices: 70.5 us -> 92.5 us  [shards(): tables = lax.all_gather(table, AXES, axis=0, tiled=False)[:, :4, :rows]]
    ppermute x2 -> x7, starting transfers between devices: 2.1 us -> 16.6 us  [the longest x2 9.83 us: shards(): high.append(lax.ppermute(sums[:OV], AXES, backward))]
    pallas_call x3 -> x6, Pallas kernels: 40.9 us -> 54.5 us  [apply_rows(): pl.pallas_call(functools.partial(apply_kernel, first, group, unroll), out...]
    ppermute x11 -> x19, waiting for transfers between devices: 24.7 us -> 12.1 us  [core_swap(): return lax.ppermute(value, 'c', [(0, 1), (1, 0)])]
  transfers between devices with their start and end apart: 22 -> 38, of which waited for: 19 -> 21; matrix products, arithmetic and copies ran while one was open for 1% -> 2% of each run, Pallas kernels for 1% -> 16%
where the time goes in v3:
time: 455 us; the launch traced here: 454 us
  waiting for transfers between devices  277 us (61%)
  Pallas kernels  98.4 us (22%)
  starting transfers between devices  47.6 us (10%)
  between operations  14.7 us (3%)
  other arithmetic  12.7 us (3%)
    all_gather x1, waiting for transfers between devices, shards(): tables = lax.all_gather(table, AXES, axis=0, tiled=False)[:, :4, :rows]  92.5 us
    ppermute x7, waiting for transfers between devices, chip_swap(): return lax.ppermute(value, ('xh', 'xl'), [(0, 3), (3, 0), (1, 2), (2, 1)])  86.4 us
    pallas_call x6, Pallas kernels, apply_rows(): pl.pallas_call(functools.partial(apply_kernel, first, group, unroll), out...  54.5 us
    ppermute x3, waiting for transfers between devices, shards(): lax.ppermute(start_modes[0], ('c', 'xh', 'xl'), start_pairs(mask))  44.6 us
    all_to_all x1, waiting for transfers between devices, shards(): lax.all_to_all(packed, group, split_axis=0, concat_axis=0, tiled=True)  33.5 us
    all_to_all x1, starting transfers between devices, shards(): lax.all_to_all(packed, group, split_axis=0, concat_axis=0, tiled=True)  13.4 us
    ppermute x19, waiting for transfers between devices, core_swap(): return lax.ppermute(value, 'c', [(0, 1), (1, 0)])  12.1 us
    pallas_call x3, Pallas kernels, second_modes(): pl.pallas_call(second_kernel, out_shape=jax.ShapeDtypeStruct(applied.shap...  11.4 us
  transfers between devices with their start and end apart: 38, of which 21 were waited for; matrix products, arithmetic and copies ran while one was open for 2% of the time, Pallas kernels for 16%

profile of v3, /device:TPU:6, one launch (start us, length us, event | category | flops | bytes accessed | tf_op | source)
XLA Modules:
  0.0 454.5 jit_solution(14123960743824969326)
XLA Ops:
  9.1 7.1 %shard_map.68 = bf16[128,2,128,128]{3,2,1,0:T(8,128)(2,1)} custom-call(s32[128]{0:T(128)S(1)} %select_n.165.order, bf16[64,2,128,128]{3,2,1,0:T(8,128)(2,1)} %blocks.1), custom_call_target="tpu_custom_call" | custom-call | tf_op jit(solution)/shard_map/pallas_call | solution.py:46
  16.8 13.4 %all-to-all-start = ((bf16[128,2,128,128]{3,2,1,0:T(8,128)(2,1)}), bf16[128,2,128,128]{3,2,1,0:T(8,128)(2,1)}, u32[]{:S(2)}, u32[]{:S(2)}) async-start(bf16[128,2,128,128]{3,2,1,0:T(8,128)(2,1)} %shard_map.68), calls=%async_computation | async-start | bytes 16777216 | tf_op jit(solution)/shard_map/all_to_all | solution.py:450
  30.4 2.5 collective-permute-start.6
  36.6 30.8 %collective-permute-done.6 = bf16[204,16,128]{2,1,0:T(8,128)(2,1)S(1)} collective-permute-done((bf16[204,16,128]{2,1,0:T(8,128)(2,1)S(1)}, bf16[204,16,128]{2,1,0:T(8,128)(2,1)S(1)}, u32[]{:S(2)}, u32[]{:S(2)}) %collective-permute-start.6) | collective-permute-done | bytes 835616 | tf_op jit(solution)/shard_map/ppermute | solution.py:468
  67.4 13.8 %collective-permute-done.7 = bf16[204,16,128]{2,1,0:T(8,128)(2,1)S(1)} collective-permute-done((bf16[204,16,128]{2,1,0:T(8,128)(2,1)S(1)}, bf16[204,16,128]{2,1,0:T(8,128)(2,1)S(1)}, u32[]{:S(2)}, u32[]{:S(2)}) %collective-permute-start.7) | collective-permute-done | bytes 835616 | tf_op jit(solution)/shard_map/ppermute | solution.py:468
  87.7 92.5 %all-gather.3.cloned.1.call-done = f32[2048,128]{1,0:T(8,128)} async-done(((f32[8,128]{1,0:T(8,128)}), f32[2048,128]{1,0:T(8,128)}) %all-gather.3.cloned.1.call-update) | async-done | bytes 1048592 | tf_op jit(solution)/shard_map/all_gather | solution.py:452
  182.6 33.5 %all-to-all-done.blk = bf16[128,2,128,128]{3,2,1,0:T(8,128)(2,1)} async-done(((bf16[128,2,128,128]{3,2,1,0:T(8,128)(2,1)}), bf16[128,2,128,128]{3,2,1,0:T(8,128)(2,1)}, u32[]{:S(2)}, u32[]{:S(2)}) %all-to-all-start) | async-done | bytes 8388640 | tf_op jit(solution)/shard_map/all_to_all | solution.py:450
  216.1 8.5 %shard_map.69 = f32[204,128]{1,0:T(8,128)S(1)} custom-call(s32[256]{0:T(256)S(1)} %reshape.145.offs, s32[128]{0:T(128)S(1)} %reshape.146.live, bf16[128,2,128,128]{3,2,1,0:T(8,128)(2,1)} %all-to-all-done.blk), custom_call_target="tpu_custom_call" | custom-call | tf_op jit(solution)/shard_map/pallas_call | solution.py:85
  224.8 2.6 broadcast_select_fusion
  227.4 4.7 %collective-permute-start.1 = (f32[204,128]{1,0:T(8,128)S(1)}, f32[204,128]{1,0:T(8,128)S(1)}, u32[]{:S(2)}, u32[]{:S(2)}) collective-permute-start(f32[204,128]{1,0:T(8,128)S(1)} %add.81), channel_id=1, source_target_pairs={{0,3},{3,0},{1,2},{2,1},{4,7},{7,4},{5,6},{6,5},{8,11},{11,8},{9,1... | collective-permute-start | bytes 313352 | tf_op jit(solution)/shard_map/ppermute | solution.py:421
  234.1 8.4 %collective-permute-start.5 = (f32[8,128]{1,0:T(8,128)S(1)}, f32[8,128]{1,0:T(8,128)S(1)}, u32[]{:S(2)}, u32[]{:S(2)}) collective-permute-start(f32[8,128]{1,0:T(8,128)S(1)} %get-tuple-element.109), channel_id=1, source_target_pairs={{10,0},{3,1},{0,2},{9,3},{14,4},{7,5},{4,6},{13,7},{18,8},{11,9},{... | collective-permute-start | bytes 12296 | tf_op jit(solution)/shard_map/ppermute | solution.py:493
  243.9 11.6 %shard_map.70 = (bf16[102,32,128]{2,1,0:T(8,128)(2,1)S(1)}, bf16[102,32,128]{2,1,0:T(8,128)(2,1)S(1)}, bf16[128,2,128,128]{3,2,1,0:T(8,128)(2,1)S(1)}) custom-call(s32[256]{0:T(256)S(1)} %reshape.145.offs, s32[128]{0:T(128)S(1)} %reshape.146.live, s32[1]{0:T(128)} %bitcast.21.core, bf16[128,2,128,128]{3,2,1,0:T(8,128)(2,1)} %all-to-all-done.blk, ...), custom_call_target="tpu_custom_call" | custom-call | flops 10000000000 | bytes 12000000 | tf_op jit(solution)/shard_map/pallas_call | solution.py:174
  255.6 2.3 collective-permute-done.10
  258.3 8.6 %shard_map.71 = (bf16[102,32,128]{2,1,0:T(8,128)(2,1)S(1)}, bf16[102,32,128]{2,1,0:T(8,128)(2,1)S(1)}) custom-call(s32[256]{0:T(256)S(1)} %reshape.145.offs, s32[128]{0:T(128)S(1)} %reshape.146.live, s32[1]{0:T(128)} %bitcast.21.core, bf16[128,2,128,128]{3,2,1,0:T(8,128)(2,1)S(1)} %get-tuple-element.48.blk, f32[204,128]{1,0:T(8,128)S(1)} %fusion.1.scale, ...), custom_call_target="tpu_custom_call" | custom-call | flops 10000000000 | bytes 12000000 | tf_op jit(solution)/shard_map/pallas_call | solution.py:174
  267.2 12.9 %collective-permute-done.11.refs_1_ = bf16[102,32,128]{2,1,0:T(8,128)(2,1)S(1)} collective-permute-done((bf16[102,32,128]{2,1,0:T(8,128)(2,1)S(1)}, bf16[102,32,128]{2,1,0:T(8,128)(2,1)S(1)}, u32[]{:S(2)}, u32[]{:S(2)}) %collective-permute-start.11) | collective-permute-done | bytes 835616 | tf_op jit(solution)/shard_map/ppermute | solution.py:421
  282.4 3.4 shard_map.74
  286.0 17.7 %collective-permute-done.13.refs_1_ = bf16[102,32,128]{2,1,0:T(8,128)(2,1)S(1)} collective-permute-done((bf16[102,32,128]{2,1,0:T(8,128)(2,1)S(1)}, bf16[102,32,128]{2,1,0:T(8,128)(2,1)S(1)}, u32[]{:S(2)}, u32[]{:S(2)}) %collective-permute-start.13) | collective-permute-done | bytes 835616 | tf_op jit(solution)/shard_map/ppermute | solution.py:421
  304.7 8.6 %shard_map.77 = (bf16[102,32,128]{2,1,0:T(8,128)(2,1)S(1)}, bf16[102,32,128]{2,1,0:T(8,128)(2,1)S(1)}) custom-call(s32[256]{0:T(256)S(1)} %reshape.145.offs, s32[128]{0:T(128)S(1)} %reshape.146.live, s32[1]{0:T(128)} %bitcast.21.core, bf16[128,2,128,128]{3,2,1,0:T(8,128)(2,1)S(1)} %get-tuple-element.48.blk, f32[204,128]{1,0:T(8,128)S(1)} %fusion.1.scale, ...), custom_call_target="tpu_custom_call" | custom-call | flops 10000000000 | bytes 12000000 | tf_op jit(solution)/shard_map/pallas_call | solution.py:174
  313.9 3.8 shard_map.75.own.refs_2_
  320.2 8.6 %shard_map.76 = (bf16[102,32,128]{2,1,0:T(8,128)(2,1)S(1)}, bf16[102,32,128]{2,1,0:T(8,128)(2,1)S(1)}) custom-call(s32[256]{0:T(256)S(1)} %reshape.145.offs, s32[128]{0:T(128)S(1)} %reshape.146.live, s32[1]{0:T(128)} %bitcast.21.core, bf16[128,2,128,128]{3,2,1,0:T(8,128)(2,1)S(1)} %get-tuple-element.48.blk, f32[204,128]{1,0:T(8,128)S(1)} %fusion.1.scale, ...), custom_call_target="tpu_custom_call" | custom-call | flops 10000000000 | bytes 12000000 | tf_op jit(solution)/shard_map/pallas_call | solution.py:174
  329.0 11.3 %collective-permute-done.19.refs_1_ = bf16[102,32,128]{2,1,0:T(8,128)(2,1)S(1)} collective-permute-done((bf16[102,32,128]{2,1,0:T(8,128)(2,1)S(1)}, bf16[102,32,128]{2,1,0:T(8,128)(2,1)S(1)}, u32[]{:S(2)}, u32[]{:S(2)}) %collective-permute-start.19) | collective-permute-done | bytes 835616 | tf_op jit(solution)/shard_map/ppermute | solution.py:421
  342.4 3.4 shard_map.80
  346.1 17.7 %collective-permute-done.21.refs_1_ = bf16[102,32,128]{2,1,0:T(8,128)(2,1)S(1)} collective-permute-done((bf16[102,32,128]{2,1,0:T(8,128)(2,1)S(1)}, bf16[102,32,128]{2,1,0:T(8,128)(2,1)S(1)}, u32[]{:S(2)}, u32[]{:S(2)}) %collective-permute-start.21) | collective-permute-done | bytes 835616 | tf_op jit(solution)/shard_map/ppermute | solution.py:421
  364.8 8.6 %shard_map.83 = (bf16[102,32,128]{2,1,0:T(8,128)(2,1)S(1)}, bf16[102,32,128]{2,1,0:T(8,128)(2,1)S(1)}) custom-call(s32[256]{0:T(256)S(1)} %reshape.145.offs, s32[128]{0:T(128)S(1)} %reshape.146.live, s32[1]{0:T(128)} %bitcast.21.core, bf16[128,2,128,128]{3,2,1,0:T(8,128)(2,1)S(1)} %get-tuple-element.48.blk, f32[204,128]{1,0:T(8,128)S(1)} %fusion.1.scale, ...), custom_call_target="tpu_custom_call" | custom-call | flops 10000000000 | bytes 12000000 | tf_op jit(solution)/shard_map/pallas_call | solution.py:174
  374.0 3.8 shard_map.81.own.refs_2_
  380.5 8.6 %shard_map.82 = (bf16[102,32,128]{2,1,0:T(8,128)(2,1)S(1)}, bf16[102,32,128]{2,1,0:T(8,128)(2,1)S(1)}) custom-call(s32[256]{0:T(256)S(1)} %reshape.145.offs, s32[128]{0:T(128)S(1)} %reshape.146.live, s32[1]{0:T(128)} %bitcast.21.core, bf16[128,2,128,128]{3,2,1,0:T(8,128)(2,1)S(1)} %get-tuple-element.48.blk, f32[204,128]{1,0:T(8,128)S(1)} %fusion.1.scale, ...), custom_call_target="tpu_custom_call" | custom-call | flops 10000000000 | bytes 12000000 | tf_op jit(solution)/shard_map/pallas_call | solution.py:174
  389.3 11.3 %collective-permute-done.27.refs_1_ = bf16[102,32,128]{2,1,0:T(8,128)(2,1)S(1)} collective-permute-done((bf16[102,32,128]{2,1,0:T(8,128)(2,1)S(1)}, bf16[102,32,128]{2,1,0:T(8,128)(2,1)S(1)}, u32[]{:S(2)}, u32[]{:S(2)}) %collective-permute-start.27) | collective-permute-done | bytes 835616 | tf_op jit(solution)/shard_map/ppermute | solution.py:421
  403.3 4.5 shard_map.85
  407.8 15.4 %collective-permute-done.29.refs_1_ = bf16[102,32,128]{2,1,0:T(8,128)(2,1)S(1)} collective-permute-done((bf16[102,32,128]{2,1,0:T(8,128)(2,1)S(1)}, bf16[102,32,128]{2,1,0:T(8,128)(2,1)S(1)}, u32[]{:S(2)}, u32[]{:S(2)}) %collective-permute-start.29) | collective-permute-done | bytes 835616 | tf_op jit(solution)/shard_map/ppermute | solution.py:421
  425.8 3.8 shard_map.87
  435.0 3.6 collective-permute-start.35
  438.7 7.3 %collective-permute-done.35 = f32[64,64]{1,0:T(8,128)S(1)} collective-permute-done((f32[64,64]{1,0:T(8,128)S(1)}, f32[64,64]{1,0:T(8,128)S(1)}, u32[]{:S(2)}, u32[]{:S(2)}) %collective-permute-start.35) | collective-permute-done | bytes 16416 | tf_op jit(solution)/shard_map/ppermute | solution.py:550
  (123 shorter events, 44.9 us)
Async XLA Ops:
  16.8 199.3 %all-to-all-start = ((bf16[128,2,128,128]{3,2,1,0:T(8,128)(2,1)}), bf16[128,2,128,128]{3,2,1,0:T(8,128)(2,1)}, u32[]{:S(2)}, u32[]{:S(2)}) async-start(bf16[128,2,128,128]{3,2,1,0:T(8,128)(2,1)} %shard_map.68), calls=%async_computation | async-start | bytes 16777216 | tf_op jit(solution)/shard_map/all_to_all | solution.py:450
  30.3 149.9 %all-gather.3.cloned.1.call-start = ((), (), s32[]{:S(2)}) async-start(), calls=%async_computation.1 | async-start | bytes 1052672 | tf_op jit(solution)/shard_map/all_gather | solution.py:452
  30.4 37.1 %collective-permute-start.6 = (bf16[204,16,128]{2,1,0:T(8,128)(2,1)S(1)}, bf16[204,16,128]{2,1,0:T(8,128)(2,1)S(1)}, u32[]{:S(2)}, u32[]{:S(2)}) collective-permute-start(bf16[204,16,128]{2,1,0:T(8,128)(2,1)S(1)} %bitcast.45), channel_id=1, source_target_pairs={{5,4},{0,1},{3,2},{6,7},{13,12},{8,9},{11,10},{14,15},{21,20},{16,... | collective-permute-start | bytes 2506760 | tf_op jit(solution)/shard_map/ppermute | solution.py:468
  32.8 48.4 %collective-permute-start.7 = (bf16[204,16,128]{2,1,0:T(8,128)(2,1)S(1)}, bf16[204,16,128]{2,1,0:T(8,128)(2,1)S(1)}, u32[]{:S(2)}, u32[]{:S(2)}) collective-permute-start(bf16[204,16,128]{2,1,0:T(8,128)(2,1)S(1)} %bitcast.46), channel_id=1, source_target_pairs={{6,4},{3,1},{0,2},{5,7},{14,12},{11,9},{8,10},{13,15},{22,20},{19,... | collective-permute-start | bytes 2506760 | tf_op jit(solution)/shard_map/ppermute | solution.py:468
  35.0 47.1 %collective-permute-start.8 = (bf16[204,16,128]{2,1,0:T(8,128)(2,1)S(1)}, bf16[204,16,128]{2,1,0:T(8,128)(2,1)}, u32[]{:S(2)}, u32[]{:S(2)}) collective-permute-start(bf16[204,16,128]{2,1,0:T(8,128)(2,1)S(1)} %bitcast.47), channel_id=1, source_target_pairs={{7,4},{2,1},{1,2},{4,7},{15,12},{10,9},{9,10},{12,15},{23,20},{18,... | collective-permute-start | bytes 2506760 | tf_op jit(solution)/shard_map/ppermute | solution.py:468
  86.3 138.5 %collective-permute-start.9 = (bf16[204,64,128]{2,1,0:T(8,128)(2,1)}, bf16[204,64,128]{2,1,0:T(8,128)(2,1)}, u32[]{:S(2)}, u32[]{:S(2)}) collective-permute-start(bf16[204,64,128]{2,1,0:T(8,128)(2,1)} %pad_maximum_fusion), channel_id=1, source_target_pairs={{4,0},{1,5},{2,6},{7,3},{12,8},{9,13},{10,14},{15,11},{20,16},{17,... | collective-permute-start | bytes 10027016 | tf_op jit(solution)/shard_map/ppermute | solution.py:475
  224.6 2.7 collective-permute-start
  227.4 16.4 %collective-permute-start.1 = (f32[204,128]{1,0:T(8,128)S(1)}, f32[204,128]{1,0:T(8,128)S(1)}, u32[]{:S(2)}, u32[]{:S(2)}) collective-permute-start(f32[204,128]{1,0:T(8,128)S(1)} %add.81), channel_id=1, source_target_pairs={{0,3},{3,0},{1,2},{2,1},{4,7},{7,4},{5,6},{6,5},{8,11},{11,8},{9,1... | collective-permute-start | bytes 313352 | tf_op jit(solution)/shard_map/ppermute | solution.py:421
  232.1 11.0 %collective-permute-start.2 = (f32[8,128]{1,0:T(8,128)S(1)}, f32[8,128]{1,0:T(8,128)S(1)}, u32[]{:S(2)}, u32[]{:S(2)}) collective-permute-start(f32[8,128]{1,0:T(8,128)S(1)} %get-tuple-element.108), channel_id=1, source_target_pairs={{0,9},{1,0},{2,3},{3,10},{4,13},{5,4},{6,7},{7,14},{8,17},{9,8},{1... | collective-permute-start | bytes 12296 | tf_op jit(solution)/shard_map/ppermute | solution.py:492
  232.1 11.0 %collective-permute-start.3 = (f32[8,128]{1,0:T(8,128)S(1)}, f32[8,128]{1,0:T(8,128)S(1)}, u32[]{:S(2)}, u32[]{:S(2)}) collective-permute-start(f32[8,128]{1,0:T(8,128)S(1)} %get-tuple-element.108), channel_id=1, source_target_pairs={{0,10},{1,3},{2,0},{3,9},{4,14},{5,7},{6,4},{7,13},{8,18},{9,11},{... | collective-permute-start | bytes 12296 | tf_op jit(solution)/shard_map/ppermute | solution.py:492
  232.6 10.5 %collective-permute-start.4 = (f32[8,128]{1,0:T(8,128)S(1)}, f32[8,128]{1,0:T(8,128)S(1)}, u32[]{:S(2)}, u32[]{:S(2)}) collective-permute-start(f32[8,128]{1,0:T(8,128)S(1)} %get-tuple-element.109), channel_id=1, source_target_pairs={{9,0},{0,1},{3,2},{10,3},{13,4},{4,5},{7,6},{14,7},{17,8},{8,9},{1... | collective-permute-start | bytes 12296 | tf_op jit(solution)/shard_map/ppermute | solution.py:493
  234.1 9.7 %collective-permute-start.5 = (f32[8,128]{1,0:T(8,128)S(1)}, f32[8,128]{1,0:T(8,128)S(1)}, u32[]{:S(2)}, u32[]{:S(2)}) collective-permute-start(f32[8,128]{1,0:T(8,128)S(1)} %get-tuple-element.109), channel_id=1, source_target_pairs={{10,0},{3,1},{0,2},{9,3},{14,4},{7,5},{4,6},{13,7},{18,8},{11,9},{... | collective-permute-start | bytes 12296 | tf_op jit(solution)/shard_map/ppermute | solution.py:493
  255.5 2.4 collective-permute-start.10
  258.2 21.9 %collective-permute-start.11 = (bf16[102,32,128]{2,1,0:T(8,128)(2,1)S(1)}, bf16[102,32,128]{2,1,0:T(8,128)(2,1)S(1)}, u32[]{:S(2)}, u32[]{:S(2)}) collective-permute-start(bf16[102,32,128]{2,1,0:T(8,128)(2,1)S(1)} %add_convert_fusion.5.refs_0_), channel_id=1, source_target_pairs={{0,3},{3,0},{1,2},{2,1},{4,7},{7,4},{5,6},{6,5},{8,11},{11,8},{9,1... | collective-permute-start | bytes 2506760 | tf_op jit(solution)/shard_map/ppermute | solution.py:421
  266.9 14.2 %collective-permute-start.12 = (bf16[102,32,128]{2,1,0:T(8,128)(2,1)S(1)}, bf16[102,32,128]{2,1,0:T(8,128)(2,1)S(1)}, u32[]{:S(2)}, u32[]{:S(2)}) collective-permute-start(bf16[102,32,128]{2,1,0:T(8,128)(2,1)S(1)} %get-tuple-element.56), channel_id=1, source_target_pairs={{0,4},{4,0},{1,5},{5,1},{2,6},{6,2},{3,7},{7,3},{8,12},{12,8},{9,1... | collective-permute-start | bytes 2506760 | tf_op jit(solution)/shard_map/ppermute | solution.py:417
  281.4 22.3 %collective-permute-start.13 = (bf16[102,32,128]{2,1,0:T(8,128)(2,1)S(1)}, bf16[102,32,128]{2,1,0:T(8,128)(2,1)S(1)}, u32[]{:S(2)}, u32[]{:S(2)}) collective-permute-start(bf16[102,32,128]{2,1,0:T(8,128)(2,1)S(1)} %add_convert_fusion.4.refs_0_), channel_id=1, source_target_pairs={{0,3},{3,0},{1,2},{2,1},{4,7},{7,4},{5,6},{6,5},{8,11},{11,8},{9,1... | collective-permute-start | bytes 2506760 | tf_op jit(solution)/shard_map/ppermute | solution.py:421
  285.7 19.0 %collective-permute-start.17 = (bf16[102,32,128]{2,1,0:T(8,128)(2,1)S(1)}, bf16[102,32,128]{2,1,0:T(8,128)(2,1)S(1)}, u32[]{:S(2)}, u32[]{:S(2)}) collective-permute-start(bf16[102,32,128]{2,1,0:T(8,128)(2,1)S(1)} %get-tuple-element.62.own.refs_2_), channel_id=1, source_target_pairs={{0,4},{4,0},{1,5},{5,1},{2,6},{6,2},{3,7},{7,3},{8,12},{12,8},{9,1... | collective-permute-start | bytes 2506760 | tf_op jit(solution)/shard_map/ppermute | solution.py:417
  304.6 9.3 %collective-permute-start.14 = (f32[32,64]{1,0:T(8,128)S(1)}, f32[32,64]{1,0:T(8,128)S(1)}, u32[]{:S(2)}, u32[]{:S(2)}) collective-permute-start(f32[32,64]{1,0:T(8,128)S(1)} %get-tuple-element.58.gram_one), channel_id=1, source_target_pairs={{0,4},{4,0},{1,5},{5,1},{2,6},{6,2},{3,7},{7,3},{8,12},{12,8},{9,1... | collective-permute-start | bytes 24584 | tf_op jit(solution)/shard_map/ppermute | solution.py:417
  313.3 4.5 collective-permute-start.18
  317.7 2.4 collective-permute-start.16
  318.1 22.3 %collective-permute-start.19 = (bf16[102,32,128]{2,1,0:T(8,128)(2,1)S(1)}, bf16[102,32,128]{2,1,0:T(8,128)(2,1)S(1)}, u32[]{:S(2)}, u32[]{:S(2)}) collective-permute-start(bf16[102,32,128]{2,1,0:T(8,128)(2,1)S(1)} %add_convert_fusion.3.refs_0_), channel_id=1, source_target_pairs={{0,3},{3,0},{1,2},{2,1},{4,7},{7,4},{5,6},{6,5},{8,11},{11,8},{9,1... | collective-permute-start | bytes 2506760 | tf_op jit(solution)/shard_map/ppermute | solution.py:421
  328.8 12.5 %collective-permute-start.20 = (bf16[102,32,128]{2,1,0:T(8,128)(2,1)S(1)}, bf16[102,32,128]{2,1,0:T(8,128)(2,1)S(1)}, u32[]{:S(2)}, u32[]{:S(2)}) collective-permute-start(bf16[102,32,128]{2,1,0:T(8,128)(2,1)S(1)} %get-tuple-element.68), channel_id=1, source_target_pairs={{0,4},{4,0},{1,5},{5,1},{2,6},{6,2},{3,7},{7,3},{8,12},{12,8},{9,1... | collective-permute-start | bytes 2506760 | tf_op jit(solution)/shard_map/ppermute | solution.py:417
  341.5 22.3 %collective-permute-start.21 = (bf16[102,32,128]{2,1,0:T(8,128)(2,1)S(1)}, bf16[102,32,128]{2,1,0:T(8,128)(2,1)S(1)}, u32[]{:S(2)}, u32[]{:S(2)}) collective-permute-start(bf16[102,32,128]{2,1,0:T(8,128)(2,1)S(1)} %add_convert_fusion.2.refs_0_), channel_id=1, source_target_pairs={{0,3},{3,0},{1,2},{2,1},{4,7},{7,4},{5,6},{6,5},{8,11},{11,8},{9,1... | collective-permute-start | bytes 2506760 | tf_op jit(solution)/shard_map/ppermute | solution.py:421
  345.8 19.0 %collective-permute-start.25 = (bf16[102,32,128]{2,1,0:T(8,128)(2,1)S(1)}, bf16[102,32,128]{2,1,0:T(8,128)(2,1)S(1)}, u32[]{:S(2)}, u32[]{:S(2)}) collective-permute-start(bf16[102,32,128]{2,1,0:T(8,128)(2,1)S(1)} %get-tuple-element.74.own.refs_2_.refs_5_), channel_id=1, source_target_pairs={{0,4},{4,0},{1,5},{5,1},{2,6},{6,2},{3,7},{7,3},{8,12},{12,8},{9,1... | collective-permute-start | bytes 2506760 | tf_op jit(solution)/shard_map/ppermute | solution.py:417
  364.7 9.3 %collective-permute-start.22 = (f32[32,64]{1,0:T(8,128)S(1)}, f32[32,64]{1,0:T(8,128)S(1)}, u32[]{:S(2)}, u32[]{:S(2)}) collective-permute-start(f32[32,64]{1,0:T(8,128)S(1)} %get-tuple-element.70.gram_one), channel_id=1, source_target_pairs={{0,4},{4,0},{1,5},{5,1},{2,6},{6,2},{3,7},{7,3},{8,12},{12,8},{9,1... | collective-permute-start | bytes 24584 | tf_op jit(solution)/shard_map/ppermute | solution.py:417
  373.4 4.8 %collective-permute-start.26 = (bf16[102,32,128]{2,1,0:T(8,128)(2,1)S(1)}, bf16[102,32,128]{2,1,0:T(8,128)(2,1)S(1)}, u32[]{:S(2)}, u32[]{:S(2)}) collective-permute-start(bf16[102,32,128]{2,1,0:T(8,128)(2,1)S(1)} %get-tuple-element.77), channel_id=1, source_target_pairs={{0,4},{4,0},{1,5},{5,1},{2,6},{6,2},{3,7},{7,3},{8,12},{12,8},{9,1... | collective-permute-start | bytes 2506760 | tf_op jit(solution)/shard_map/ppermute | solution.py:417
  377.8 2.7 collective-permute-start.24
  378.4 22.3 %collective-permute-start.27 = (bf16[102,32,128]{2,1,0:T(8,128)(2,1)S(1)}, bf16[102,32,128]{2,1,0:T(8,128)(2,1)S(1)}, u32[]{:S(2)}, u32[]{:S(2)}) collective-permute-start(bf16[102,32,128]{2,1,0:T(8,128)(2,1)S(1)} %add_convert_fusion.1.refs_0_), channel_id=1, source_target_pairs={{0,3},{3,0},{1,2},{2,1},{4,7},{7,4},{5,6},{6,5},{8,11},{11,8},{9,1... | collective-permute-start | bytes 2506760 | tf_op jit(solution)/shard_map/ppermute | solution.py:421
  389.1 12.4 %collective-permute-start.28 = (bf16[102,32,128]{2,1,0:T(8,128)(2,1)S(1)}, bf16[102,32,128]{2,1,0:T(8,128)(2,1)S(1)}, u32[]{:S(2)}, u32[]{:S(2)}) collective-permute-start(bf16[102,32,128]{2,1,0:T(8,128)(2,1)S(1)} %get-tuple-element.80), channel_id=1, source_target_pairs={{0,4},{4,0},{1,5},{5,1},{2,6},{6,2},{3,7},{7,3},{8,12},{12,8},{9,1... | collective-permute-start | bytes 2506760 | tf_op jit(solution)/shard_map/ppermute | solution.py:417
  401.7 21.5 %collective-permute-start.29 = (bf16[102,32,128]{2,1,0:T(8,128)(2,1)S(1)}, bf16[102,32,128]{2,1,0:T(8,128)(2,1)S(1)}, u32[]{:S(2)}, u32[]{:S(2)}) collective-permute-start(bf16[102,32,128]{2,1,0:T(8,128)(2,1)S(1)} %add_convert_fusion.refs_0_), channel_id=1, source_target_pairs={{0,3},{3,0},{1,2},{2,1},{4,7},{7,4},{5,6},{6,5},{8,11},{11,8},{9,1... | collective-permute-start | bytes 2506760 | tf_op jit(solution)/shard_map/ppermute | solution.py:421
  431.8 14.8 %collective-permute-start.33 = (bf16[204,16,128]{2,1,0:T(8,128)(2,1)S(1)}, bf16[204,16,128]{2,1,0:T(8,128)(2,1)S(1)}, u32[]{:S(2)}, u32[]{:S(2)}) collective-permute-start(bf16[204,16,128]{2,1,0:T(8,128)(2,1)S(1)} %maximum_select_fusion), channel_id=1, source_target_pairs={{0,5},{3,6},{5,0},{6,3},{8,13},{11,14},{13,8},{14,11},{16,21},{19,... | collective-permute-start | bytes 2506760 | tf_op jit(solution)/shard_map/ppermute | solution.py:549
  435.0 11.0 %collective-permute-start.35 = (f32[64,64]{1,0:T(8,128)S(1)}, f32[64,64]{1,0:T(8,128)S(1)}, u32[]{:S(2)}, u32[]{:S(2)}) collective-permute-start(f32[64,64]{1,0:T(8,128)S(1)} %add.97), channel_id=1, source_target_pairs={{0,5},{3,6},{5,0},{6,3},{8,13},{11,14},{13,8},{14,11},{16,21},{19,... | collective-permute-start | bytes 49160 | tf_op jit(solution)/shard_map/ppermute | solution.py:550
  (11 other events, 50.9 us)
Sparse Core Ops, SparseCore 0:
  36.7 143.3 all-gather.2

commit v4 on v3

--- a/solution.py
+++ b/solution.py
@@ -57,7 +57,7 @@
     )(order, blocks)
 
 
-def sums_kernel(group, offs, live, blk, sums):
+def sums_kernel(group, offs, live, left, right, sums):
     step = pl.program_id(0)
 
     @pl.when(step == 0)
@@ -70,7 +70,7 @@
         slot = step * group + s
         keep = rows < live[slot]
         for k in range(2):
-            wide = blk[s, k].astype(jnp.float32)
+            wide = (left, right)[k][s, 0].astype(jnp.float32)
             part = jnp.sum(jnp.where(keep, wide * wide, 0.0), axis=0, keepdims=True)
             at = pl.ds(offs[2 * slot + k], 1)
             sums[at, :] = sums[at, :] + part
@@ -88,11 +88,14 @@
         grid_spec=pltpu.PrefetchScalarGridSpec(
             num_scalar_prefetch=2,
             grid=(slots // group,),
-            in_specs=[pl.BlockSpec((group, 2, BLK, BLK), lambda i, *_: (i, 0, 0, 0))],
+            in_specs=[
+                pl.BlockSpec((group, 1, BLK, BLK), lambda i, *_: (i, 0, 0, 0)),
+                pl.BlockSpec((group, 1, BLK, BLK), lambda i, *_: (i, 1, 0, 0)),
+            ],
             out_specs=pl.BlockSpec((domain, BLK), lambda i, *_: (0, 0)),
         ),
         compiler_params=pltpu.CompilerParams(vmem_limit_bytes=VMEM_LIMIT),
-    )(offs, live, blocks)
+    )(offs, live, blocks, blocks)
 
 
 def apply_kernel(first, group, unroll, offs, live, core, blk, scale, own, peer, *rest):
@@ -516,10 +519,12 @@
     for step in range(ITERS):
         last = step == ITERS - 1
         one_there = chip_swap(one)
-        two = apply_half(1)
+        keep, send = apply_half(1)
+        one_there, keep = lax.optimization_barrier((one_there, keep))
         before, gram = form_image(one, one_there, owns[0], damped)
-        two = add_cores(*two, after=gram)
+        two = add_cores(keep, send, after=gram)
         two_there = chip_swap(two)
+        two, gram = lax.optimization_barrier((two, gram))
         new, first = first_modes(gram, core_swap(gram), before)
         if last:
             two_there, first = lax.optimization_barrier((two_there, first))
@@ -530,9 +535,11 @@
             out = second_modes(upper, gram, core_swap(gram), first, before, applied)
         else:
             owns[0], peers[0] = new, core_swap(new)
-            one = apply_half(0)
+            keep, send = apply_half(0)
+            two_there, keep = lax.optimization_barrier((two_there, keep))
             applied, gram = form_image(two, two_there, owns[1], damped, (before,))
-            one = add_cores(*one, after=gram)
+            one = add_cores(keep, send, after=gram)
+            one, gram = lax.optimization_barrier((one, gram))
             new = second_modes(lower, gram, core_swap(gram), first, before, applied)
             owns[1], peers[1] = new, core_swap(new)
 

time: 455 us -> 448 us (0.985)
  waiting for transfers between devices: 277 us -> 270 us
    ppermute x7, waiting for transfers between devices: 86.4 us -> 72 us  [chip_swap(): return lax.ppermute(value, ('xh', 'xl'), [(0, 3), (3, 0), (1, 2), (2, 1)])]
    ppermute x19, waiting for transfers between devices: 12.1 us -> 19.8 us  [core_swap(): return lax.ppermute(value, 'c', [(0, 1), (1, 0)])]
  transfers between devices with their start and end apart: 38 -> 38, of which waited for: 21 -> 25; matrix products, arithmetic and copies ran while one was open for 2% -> 2% of each run, Pallas kernels for 16% -> 13%
where the time goes in v4:
time: 448 us; the launch traced here: 447 us
  waiting for transfers between devices  270 us (60%)
  Pallas kernels  98.4 us (22%)
  starting transfers between devices  46.9 us (10%)
  between operations  14.7 us (3%)
  other arithmetic  12.7 us (3%)
    all_gather x1, waiting for transfers between devices, shards(): tables = lax.all_gather(table, AXES, axis=0, tiled=False)[:, :4, :rows]  92.5 us
    ppermute x7, waiting for transfers between devices, chip_swap(): return lax.ppermute(value, ('xh', 'xl'), [(0, 3), (3, 0), (1, 2), (2, 1)])  72 us
    pallas_call x6, Pallas kernels, apply_rows(): pl.pallas_call(functools.partial(apply_kernel, first, group, unroll), out...  54.6 us
    ppermute x3, waiting for transfers between devices, shards(): lax.ppermute(start_modes[0], ('c', 'xh', 'xl'), start_pairs(mask))  44.6 us
    all_to_all x1, waiting for transfers between devices, shards(): lax.all_to_all(packed, group, split_axis=0, concat_axis=0, tiled=True)  33.5 us
    ppermute x19, waiting for transfers between devices, core_swap(): return lax.ppermute(value, 'c', [(0, 1), (1, 0)])  19.8 us
    all_to_all x1, starting transfers between devices, shards(): lax.all_to_all(packed, group, split_axis=0, concat_axis=0, tiled=True)  13.4 us
    pallas_call x3, Pallas kernels, second_modes(): pl.pallas_call(second_kernel, out_shape=jax.ShapeDtypeStruct(applied.shap...  11.4 us
  transfers between devices with their start and end apart: 38, of which 25 were waited for; matrix products, arithmetic and copies ran while one was open for 2% of the time, Pallas kernels for 13%

profile of v4, /device:TPU:6, one launch (start us, length us, event | category | flops | bytes accessed | tf_op | source)
XLA Modules:
  0.0 447.0 jit_solution(1644316822421325740)
XLA Ops:
  9.1 7.1 %shard_map.68 = bf16[128,2,128,128]{3,2,1,0:T(8,128)(2,1)} custom-call(s32[128]{0:T(128)S(1)} %select_n.165.order, bf16[64,2,128,128]{3,2,1,0:T(8,128)(2,1)} %blocks.1), custom_call_target="tpu_custom_call" | custom-call | tf_op jit(solution)/shard_map/pallas_call | solution.py:46
  16.8 13.4 %all-to-all-start = ((bf16[128,2,128,128]{3,2,1,0:T(8,128)(2,1)}), bf16[128,2,128,128]{3,2,1,0:T(8,128)(2,1)}, u32[]{:S(2)}, u32[]{:S(2)}) async-start(bf16[128,2,128,128]{3,2,1,0:T(8,128)(2,1)} %shard_map.68), calls=%async_computation | async-start | bytes 16777216 | tf_op jit(solution)/shard_map/all_to_all | solution.py:453
  30.4 2.5 collective-permute-start.6
  36.6 30.8 %collective-permute-done.6 = bf16[204,16,128]{2,1,0:T(8,128)(2,1)S(1)} collective-permute-done((bf16[204,16,128]{2,1,0:T(8,128)(2,1)S(1)}, bf16[204,16,128]{2,1,0:T(8,128)(2,1)S(1)}, u32[]{:S(2)}, u32[]{:S(2)}) %collective-permute-start.6) | collective-permute-done | bytes 835616 | tf_op jit(solution)/shard_map/ppermute | solution.py:471
  67.4 13.8 %collective-permute-done.7 = bf16[204,16,128]{2,1,0:T(8,128)(2,1)S(1)} collective-permute-done((bf16[204,16,128]{2,1,0:T(8,128)(2,1)S(1)}, bf16[204,16,128]{2,1,0:T(8,128)(2,1)S(1)}, u32[]{:S(2)}, u32[]{:S(2)}) %collective-permute-start.7) | collective-permute-done | bytes 835616 | tf_op jit(solution)/shard_map/ppermute | solution.py:471
  87.7 92.5 %all-gather.3.cloned.1.call-done = f32[2048,128]{1,0:T(8,128)} async-done(((f32[8,128]{1,0:T(8,128)}), f32[2048,128]{1,0:T(8,128)}) %all-gather.3.cloned.1.call-update) | async-done | bytes 1048592 | tf_op jit(solution)/shard_map/all_gather | solution.py:455
  182.6 33.5 %all-to-all-done.left.right.blk = bf16[128,2,128,128]{3,2,1,0:T(8,128)(2,1)} async-done(((bf16[128,2,128,128]{3,2,1,0:T(8,128)(2,1)}), bf16[128,2,128,128]{3,2,1,0:T(8,128)(2,1)}, u32[]{:S(2)}, u32[]{:S(2)}) %all-to-all-start) | async-done | bytes 8388640 | tf_op jit(solution)/shard_map/all_to_all | solution.py:453
  216.1 8.4 %shard_map.69 = f32[204,128]{1,0:T(8,128)S(1)} custom-call(s32[256]{0:T(256)S(1)} %reshape.145.offs, s32[128]{0:T(128)S(1)} %reshape.146.live, bf16[128,2,128,128]{3,2,1,0:T(8,128)(2,1)} %all-to-all-done.left.right.blk, bf16[128,2,128,128]{3,2,1,0:T(8,128)(2,1)} %all-to-all-done.left.right.blk), custom_call_target="tpu_custom_call" | custom-call | tf_op jit(solution)/shard_map/pallas_call | solution.py:85
  224.7 2.6 broadcast_select_fusion
  227.3 4.7 %collective-permute-start.1 = (f32[204,128]{1,0:T(8,128)S(1)}, f32[204,128]{1,0:T(8,128)S(1)}, u32[]{:S(2)}, u32[]{:S(2)}) collective-permute-start(f32[204,128]{1,0:T(8,128)S(1)} %add.81), channel_id=1, source_target_pairs={{0,3},{3,0},{1,2},{2,1},{4,7},{7,4},{5,6},{6,5},{8,11},{11,8},{9,1... | collective-permute-start | bytes 313352 | tf_op jit(solution)/shard_map/ppermute | solution.py:424
  234.1 8.4 %collective-permute-start.5 = (f32[8,128]{1,0:T(8,128)S(1)}, f32[8,128]{1,0:T(8,128)S(1)}, u32[]{:S(2)}, u32[]{:S(2)}) collective-permute-start(f32[8,128]{1,0:T(8,128)S(1)} %get-tuple-element.149), channel_id=1, source_target_pairs={{10,0},{3,1},{0,2},{9,3},{14,4},{7,5},{4,6},{13,7},{18,8},{11,9},{... | collective-permute-start | bytes 12296 | tf_op jit(solution)/shard_map/ppermute | solution.py:496
  243.9 11.6 %shard_map.70 = (bf16[102,32,128]{2,1,0:T(8,128)(2,1)S(1)}, bf16[102,32,128]{2,1,0:T(8,128)(2,1)S(1)}, bf16[128,2,128,128]{3,2,1,0:T(8,128)(2,1)S(1)}) custom-call(s32[256]{0:T(256)S(1)} %reshape.145.offs, s32[128]{0:T(128)S(1)} %reshape.146.live, s32[1]{0:T(128)} %bitcast.21.core, bf16[128,2,128,128]{3,2,1,0:T(8,128)(2,1)} %all-to-all-done.left.right.blk, ...), custom_call_target="tpu_custom_call" | custom-call | flops 10000000000 | bytes 12000000 | tf_op jit(solution)/shard_map/pallas_call | solution.py:177
  255.6 2.3 collective-permute-done.10
  258.3 8.6 %shard_map.71 = (bf16[102,32,128]{2,1,0:T(8,128)(2,1)S(1)}, bf16[102,32,128]{2,1,0:T(8,128)(2,1)S(1)}) custom-call(s32[256]{0:T(256)S(1)} %reshape.145.offs, s32[128]{0:T(128)S(1)} %reshape.146.live, s32[1]{0:T(128)} %bitcast.21.core, bf16[128,2,128,128]{3,2,1,0:T(8,128)(2,1)S(1)} %get-tuple-element.71.blk, f32[204,128]{1,0:T(8,128)S(1)} %fusion.1.scale, ...), custom_call_target="tpu_custom_call" | custom-call | flops 10000000000 | bytes 12000000 | tf_op jit(solution)/shard_map/pallas_call | solution.py:177
  267.3 12.7 %collective-permute-done.11.refs_1_ = bf16[102,32,128]{2,1,0:T(8,128)(2,1)S(1)} collective-permute-done((bf16[102,32,128]{2,1,0:T(8,128)(2,1)S(1)}, bf16[102,32,128]{2,1,0:T(8,128)(2,1)S(1)}, u32[]{:S(2)}, u32[]{:S(2)}) %collective-permute-start.11) | collective-permute-done | bytes 835616 | tf_op jit(solution)/shard_map/ppermute | solution.py:424
  282.4 3.4 shard_map.73
  288.2 8.6 %shard_map.74 = (bf16[102,32,128]{2,1,0:T(8,128)(2,1)S(1)}, bf16[102,32,128]{2,1,0:T(8,128)(2,1)S(1)}) custom-call(s32[256]{0:T(256)S(1)} %reshape.145.offs, s32[128]{0:T(128)S(1)} %reshape.146.live, s32[1]{0:T(128)} %bitcast.21.core, bf16[128,2,128,128]{3,2,1,0:T(8,128)(2,1)S(1)} %get-tuple-element.71.blk, f32[204,128]{1,0:T(8,128)S(1)} %fusion.1.scale, ...), custom_call_target="tpu_custom_call" | custom-call | flops 10000000000 | bytes 12000000 | tf_op jit(solution)/shard_map/pallas_call | solution.py:177
  297.1 11.0 %collective-permute-done.13.refs_1_ = bf16[102,32,128]{2,1,0:T(8,128)(2,1)S(1)} collective-permute-done((bf16[102,32,128]{2,1,0:T(8,128)(2,1)S(1)}, bf16[102,32,128]{2,1,0:T(8,128)(2,1)S(1)}, u32[]{:S(2)}, u32[]{:S(2)}) %collective-permute-start.13) | collective-permute-done | bytes 835616 | tf_op jit(solution)/shard_map/ppermute | solution.py:424
  310.5 3.8 shard_map.76.own.refs_2_
  316.7 8.6 %shard_map.77 = (bf16[102,32,128]{2,1,0:T(8,128)(2,1)S(1)}, bf16[102,32,128]{2,1,0:T(8,128)(2,1)S(1)}) custom-call(s32[256]{0:T(256)S(1)} %reshape.145.offs, s32[128]{0:T(128)S(1)} %reshape.146.live, s32[1]{0:T(128)} %bitcast.21.core, bf16[128,2,128,128]{3,2,1,0:T(8,128)(2,1)S(1)} %get-tuple-element.71.blk, f32[204,128]{1,0:T(8,128)S(1)} %fusion.1.scale, ...), custom_call_target="tpu_custom_call" | custom-call | flops 10000000000 | bytes 12000000 | tf_op jit(solution)/shard_map/pallas_call | solution.py:177
  325.6 11.0 %collective-permute-done.17.refs_1_ = bf16[102,32,128]{2,1,0:T(8,128)(2,1)S(1)} collective-permute-done((bf16[102,32,128]{2,1,0:T(8,128)(2,1)S(1)}, bf16[102,32,128]{2,1,0:T(8,128)(2,1)S(1)}, u32[]{:S(2)}, u32[]{:S(2)}) %collective-permute-start.17) | collective-permute-done | bytes 835616 | tf_op jit(solution)/shard_map/ppermute | solution.py:424
  338.9 3.4 shard_map.79
  344.7 8.6 %shard_map.80 = (bf16[102,32,128]{2,1,0:T(8,128)(2,1)S(1)}, bf16[102,32,128]{2,1,0:T(8,128)(2,1)S(1)}) custom-call(s32[256]{0:T(256)S(1)} %reshape.145.offs, s32[128]{0:T(128)S(1)} %reshape.146.live, s32[1]{0:T(128)} %bitcast.21.core, bf16[128,2,128,128]{3,2,1,0:T(8,128)(2,1)S(1)} %get-tuple-element.71.blk, f32[204,128]{1,0:T(8,128)S(1)} %fusion.1.scale, ...), custom_call_target="tpu_custom_call" | custom-call | flops 10000000000 | bytes 12000000 | tf_op jit(solution)/shard_map/pallas_call | solution.py:177
  353.6 11.0 %collective-permute-done.21.refs_1_ = bf16[102,32,128]{2,1,0:T(8,128)(2,1)S(1)} collective-permute-done((bf16[102,32,128]{2,1,0:T(8,128)(2,1)S(1)}, bf16[102,32,128]{2,1,0:T(8,128)(2,1)S(1)}, u32[]{:S(2)}, u32[]{:S(2)}) %collective-permute-start.21) | collective-permute-done | bytes 835616 | tf_op jit(solution)/shard_map/ppermute | solution.py:424
  367.2 3.8 shard_map.82.own.refs_2_
  373.5 8.6 %shard_map.83 = (bf16[102,32,128]{2,1,0:T(8,128)(2,1)S(1)}, bf16[102,32,128]{2,1,0:T(8,128)(2,1)S(1)}) custom-call(s32[256]{0:T(256)S(1)} %reshape.145.offs, s32[128]{0:T(128)S(1)} %reshape.146.live, s32[1]{0:T(128)} %bitcast.21.core, bf16[128,2,128,128]{3,2,1,0:T(8,128)(2,1)S(1)} %get-tuple-element.71.blk, f32[204,128]{1,0:T(8,128)S(1)} %fusion.1.scale, ...), custom_call_target="tpu_custom_call" | custom-call | flops 10000000000 | bytes 12000000 | tf_op jit(solution)/shard_map/pallas_call | solution.py:177
  382.3 11.0 %collective-permute-done.25.refs_1_ = bf16[102,32,128]{2,1,0:T(8,128)(2,1)S(1)} collective-permute-done((bf16[102,32,128]{2,1,0:T(8,128)(2,1)S(1)}, bf16[102,32,128]{2,1,0:T(8,128)(2,1)S(1)}, u32[]{:S(2)}, u32[]{:S(2)}) %collective-permute-start.25) | collective-permute-done | bytes 835616 | tf_op jit(solution)/shard_map/ppermute | solution.py:424
  395.9 4.6 %shard_map.85 = (bf16[102,32,128]{2,1,0:T(8,128)(2,1)}, f32[32,32]{1,0:T(8,128)S(1)}) custom-call(f32[32,32]{1,0:T(8,128)S(1)} %get-tuple-element.120.gram_one, f32[32,32]{1,0:T(8,128)S(1)} %collective-permute-done.30.gram_two, bf16[102,32,128]{2,1,0:T(8,128)(2,1)S(1)} %get-tuple-element.121.applied.refs_4_.before), custom_call_target="tpu_custom_call" | custom-call | flops 3000000000 | bytes 1000000 | tf_op jit(solution)/shard_map/pallas_call | solution.py:332
  400.5 15.2 %collective-permute-done.29.refs_1_ = bf16[102,32,128]{2,1,0:T(8,128)(2,1)S(1)} collective-permute-done((bf16[102,32,128]{2,1,0:T(8,128)(2,1)S(1)}, bf16[102,32,128]{2,1,0:T(8,128)(2,1)S(1)}, u32[]{:S(2)}, u32[]{:S(2)}) %collective-permute-start.29) | collective-permute-done | bytes 835616 | tf_op jit(solution)/shard_map/ppermute | solution.py:424
  418.4 3.8 shard_map.87
  427.6 3.6 collective-permute-start.35
  431.2 7.3 %collective-permute-done.35 = f32[64,64]{1,0:T(8,128)S(1)} collective-permute-done((f32[64,64]{1,0:T(8,128)S(1)}, f32[64,64]{1,0:T(8,128)S(1)}, u32[]{:S(2)}, u32[]{:S(2)}) %collective-permute-start.35) | collective-permute-done | bytes 16416 | tf_op jit(solution)/shard_map/ppermute | solution.py:557
  (123 shorter events, 52.0 us)
Async XLA Ops:
  16.8 199.3 %all-to-all-start = ((bf16[128,2,128,128]{3,2,1,0:T(8,128)(2,1)}), bf16[128,2,128,128]{3,2,1,0:T(8,128)(2,1)}, u32[]{:S(2)}, u32[]{:S(2)}) async-start(bf16[128,2,128,128]{3,2,1,0:T(8,128)(2,1)} %shard_map.68), calls=%async_computation | async-start | bytes 16777216 | tf_op jit(solution)/shard_map/all_to_all | solution.py:453
  30.3 149.9 %all-gather.3.cloned.1.call-start = ((), (), s32[]{:S(2)}) async-start(), calls=%async_computation.1 | async-start | bytes 1052672 | tf_op jit(solution)/shard_map/all_gather | solution.py:455
  30.4 37.1 %collective-permute-start.6 = (bf16[204,16,128]{2,1,0:T(8,128)(2,1)S(1)}, bf16[204,16,128]{2,1,0:T(8,128)(2,1)S(1)}, u32[]{:S(2)}, u32[]{:S(2)}) collective-permute-start(bf16[204,16,128]{2,1,0:T(8,128)(2,1)S(1)} %bitcast.45), channel_id=1, source_target_pairs={{5,4},{0,1},{3,2},{6,7},{13,12},{8,9},{11,10},{14,15},{21,20},{16,... | collective-permute-start | bytes 2506760 | tf_op jit(solution)/shard_map/ppermute | solution.py:471
  32.8 48.4 %collective-permute-start.7 = (bf16[204,16,128]{2,1,0:T(8,128)(2,1)S(1)}, bf16[204,16,128]{2,1,0:T(8,128)(2,1)S(1)}, u32[]{:S(2)}, u32[]{:S(2)}) collective-permute-start(bf16[204,16,128]{2,1,0:T(8,128)(2,1)S(1)} %bitcast.46), channel_id=1, source_target_pairs={{6,4},{3,1},{0,2},{5,7},{14,12},{11,9},{8,10},{13,15},{22,20},{19,... | collective-permute-start | bytes 2506760 | tf_op jit(solution)/shard_map/ppermute | solution.py:471
  35.0 47.1 %collective-permute-start.8 = (bf16[204,16,128]{2,1,0:T(8,128)(2,1)S(1)}, bf16[204,16,128]{2,1,0:T(8,128)(2,1)}, u32[]{:S(2)}, u32[]{:S(2)}) collective-permute-start(bf16[204,16,128]{2,1,0:T(8,128)(2,1)S(1)} %bitcast.47), channel_id=1, source_target_pairs={{7,4},{2,1},{1,2},{4,7},{15,12},{10,9},{9,10},{12,15},{23,20},{18,... | collective-permute-start | bytes 2506760 | tf_op jit(solution)/shard_map/ppermute | solution.py:471
  86.3 138.4 %collective-permute-start.9 = (bf16[204,64,128]{2,1,0:T(8,128)(2,1)}, bf16[204,64,128]{2,1,0:T(8,128)(2,1)}, u32[]{:S(2)}, u32[]{:S(2)}) collective-permute-start(bf16[204,64,128]{2,1,0:T(8,128)(2,1)} %pad_maximum_fusion), channel_id=1, source_target_pairs={{4,0},{1,5},{2,6},{7,3},{12,8},{9,13},{10,14},{15,11},{20,16},{17,... | collective-permute-start | bytes 10027016 | tf_op jit(solution)/shard_map/ppermute | solution.py:478
  224.6 2.7 collective-permute-start
  227.3 16.4 %collective-permute-start.1 = (f32[204,128]{1,0:T(8,128)S(1)}, f32[204,128]{1,0:T(8,128)S(1)}, u32[]{:S(2)}, u32[]{:S(2)}) collective-permute-start(f32[204,128]{1,0:T(8,128)S(1)} %add.81), channel_id=1, source_target_pairs={{0,3},{3,0},{1,2},{2,1},{4,7},{7,4},{5,6},{6,5},{8,11},{11,8},{9,1... | collective-permute-start | bytes 313352 | tf_op jit(solution)/shard_map/ppermute | solution.py:424
  232.0 11.0 %collective-permute-start.2 = (f32[8,128]{1,0:T(8,128)S(1)}, f32[8,128]{1,0:T(8,128)S(1)}, u32[]{:S(2)}, u32[]{:S(2)}) collective-permute-start(f32[8,128]{1,0:T(8,128)S(1)} %get-tuple-element.148), channel_id=1, source_target_pairs={{0,9},{1,0},{2,3},{3,10},{4,13},{5,4},{6,7},{7,14},{8,17},{9,8},{1... | collective-permute-start | bytes 12296 | tf_op jit(solution)/shard_map/ppermute | solution.py:495
  232.0 11.0 %collective-permute-start.3 = (f32[8,128]{1,0:T(8,128)S(1)}, f32[8,128]{1,0:T(8,128)S(1)}, u32[]{:S(2)}, u32[]{:S(2)}) collective-permute-start(f32[8,128]{1,0:T(8,128)S(1)} %get-tuple-element.148), channel_id=1, source_target_pairs={{0,10},{1,3},{2,0},{3,9},{4,14},{5,7},{6,4},{7,13},{8,18},{9,11},{... | collective-permute-start | bytes 12296 | tf_op jit(solution)/shard_map/ppermute | solution.py:495
  232.6 10.5 %collective-permute-start.4 = (f32[8,128]{1,0:T(8,128)S(1)}, f32[8,128]{1,0:T(8,128)S(1)}, u32[]{:S(2)}, u32[]{:S(2)}) collective-permute-start(f32[8,128]{1,0:T(8,128)S(1)} %get-tuple-element.149), channel_id=1, source_target_pairs={{9,0},{0,1},{3,2},{10,3},{13,4},{4,5},{7,6},{14,7},{17,8},{8,9},{1... | collective-permute-start | bytes 12296 | tf_op jit(solution)/shard_map/ppermute | solution.py:496
  234.1 9.7 %collective-permute-start.5 = (f32[8,128]{1,0:T(8,128)S(1)}, f32[8,128]{1,0:T(8,128)S(1)}, u32[]{:S(2)}, u32[]{:S(2)}) collective-permute-start(f32[8,128]{1,0:T(8,128)S(1)} %get-tuple-element.149), channel_id=1, source_target_pairs={{10,0},{3,1},{0,2},{9,3},{14,4},{7,5},{4,6},{13,7},{18,8},{11,9},{... | collective-permute-start | bytes 12296 | tf_op jit(solution)/shard_map/ppermute | solution.py:496
  255.5 2.4 collective-permute-start.10
  258.1 21.9 %collective-permute-start.11 = (bf16[102,32,128]{2,1,0:T(8,128)(2,1)S(1)}, bf16[102,32,128]{2,1,0:T(8,128)(2,1)S(1)}, u32[]{:S(2)}, u32[]{:S(2)}) collective-permute-start(bf16[102,32,128]{2,1,0:T(8,128)(2,1)S(1)} %add_convert_fusion.5.refs_0_), channel_id=1, source_target_pairs={{0,3},{3,0},{1,2},{2,1},{4,7},{7,4},{5,6},{6,5},{8,11},{11,8},{9,1... | collective-permute-start | bytes 2506760 | tf_op jit(solution)/shard_map/ppermute | solution.py:424
  266.9 14.0 %collective-permute-start.12 = (bf16[102,32,128]{2,1,0:T(8,128)(2,1)S(1)}, bf16[102,32,128]{2,1,0:T(8,128)(2,1)S(1)}, u32[]{:S(2)}, u32[]{:S(2)}) collective-permute-start(bf16[102,32,128]{2,1,0:T(8,128)(2,1)S(1)} %get-tuple-element.78), channel_id=1, source_target_pairs={{0,4},{4,0},{1,5},{5,1},{2,6},{6,2},{3,7},{7,3},{8,12},{12,8},{9,1... | collective-permute-start | bytes 2506760 | tf_op jit(solution)/shard_map/ppermute | solution.py:420
  285.7 2.4 collective-permute-start.15
  286.0 22.1 %collective-permute-start.13 = (bf16[102,32,128]{2,1,0:T(8,128)(2,1)S(1)}, bf16[102,32,128]{2,1,0:T(8,128)(2,1)S(1)}, u32[]{:S(2)}, u32[]{:S(2)}) collective-permute-start(bf16[102,32,128]{2,1,0:T(8,128)(2,1)S(1)} %add_convert_fusion.4.refs_0_), channel_id=1, source_target_pairs={{0,3},{3,0},{1,2},{2,1},{4,7},{7,4},{5,6},{6,5},{8,11},{11,8},{9,1... | collective-permute-start | bytes 2506760 | tf_op jit(solution)/shard_map/ppermute | solution.py:424
  296.8 12.2 %collective-permute-start.16 = (bf16[102,32,128]{2,1,0:T(8,128)(2,1)S(1)}, bf16[102,32,128]{2,1,0:T(8,128)(2,1)S(1)}, u32[]{:S(2)}, u32[]{:S(2)}) collective-permute-start(bf16[102,32,128]{2,1,0:T(8,128)(2,1)S(1)} %get-tuple-element.88), channel_id=1, source_target_pairs={{0,4},{4,0},{1,5},{5,1},{2,6},{6,2},{3,7},{7,3},{8,12},{12,8},{9,1... | collective-permute-start | bytes 2506760 | tf_op jit(solution)/shard_map/ppermute | solution.py:420
  314.3 2.4 collective-permute-start.19
  314.5 22.1 %collective-permute-start.17 = (bf16[102,32,128]{2,1,0:T(8,128)(2,1)S(1)}, bf16[102,32,128]{2,1,0:T(8,128)(2,1)S(1)}, u32[]{:S(2)}, u32[]{:S(2)}) collective-permute-start(bf16[102,32,128]{2,1,0:T(8,128)(2,1)S(1)} %add_convert_fusion.3.refs_0_), channel_id=1, source_target_pairs={{0,3},{3,0},{1,2},{2,1},{4,7},{7,4},{5,6},{6,5},{8,11},{11,8},{9,1... | collective-permute-start | bytes 2506760 | tf_op jit(solution)/shard_map/ppermute | solution.py:424
  325.3 12.1 %collective-permute-start.20 = (bf16[102,32,128]{2,1,0:T(8,128)(2,1)S(1)}, bf16[102,32,128]{2,1,0:T(8,128)(2,1)S(1)}, u32[]{:S(2)}, u32[]{:S(2)}) collective-permute-start(bf16[102,32,128]{2,1,0:T(8,128)(2,1)S(1)} %get-tuple-element.98), channel_id=1, source_target_pairs={{0,4},{4,0},{1,5},{5,1},{2,6},{6,2},{3,7},{7,3},{8,12},{12,8},{9,1... | collective-permute-start | bytes 2506760 | tf_op jit(solution)/shard_map/ppermute | solution.py:420
  342.3 2.4 collective-permute-start.23
  342.5 22.1 %collective-permute-start.21 = (bf16[102,32,128]{2,1,0:T(8,128)(2,1)S(1)}, bf16[102,32,128]{2,1,0:T(8,128)(2,1)S(1)}, u32[]{:S(2)}, u32[]{:S(2)}) collective-permute-start(bf16[102,32,128]{2,1,0:T(8,128)(2,1)S(1)} %add_convert_fusion.2.refs_0_), channel_id=1, source_target_pairs={{0,3},{3,0},{1,2},{2,1},{4,7},{7,4},{5,6},{6,5},{8,11},{11,8},{9,1... | collective-permute-start | bytes 2506760 | tf_op jit(solution)/shard_map/ppermute | solution.py:424
  353.3 12.2 %collective-permute-start.24 = (bf16[102,32,128]{2,1,0:T(8,128)(2,1)S(1)}, bf16[102,32,128]{2,1,0:T(8,128)(2,1)S(1)}, u32[]{:S(2)}, u32[]{:S(2)}) collective-permute-start(bf16[102,32,128]{2,1,0:T(8,128)(2,1)S(1)} %get-tuple-element.108), channel_id=1, source_target_pairs={{0,4},{4,0},{1,5},{5,1},{2,6},{6,2},{3,7},{7,3},{8,12},{12,8},{9,1... | collective-permute-start | bytes 2506760 | tf_op jit(solution)/shard_map/ppermute | solution.py:420
  365.7 1.5 collective-permute-start.26
  371.0 2.4 collective-permute-start.27
  371.3 22.1 %collective-permute-start.25 = (bf16[102,32,128]{2,1,0:T(8,128)(2,1)S(1)}, bf16[102,32,128]{2,1,0:T(8,128)(2,1)S(1)}, u32[]{:S(2)}, u32[]{:S(2)}) collective-permute-start(bf16[102,32,128]{2,1,0:T(8,128)(2,1)S(1)} %add_convert_fusion.1.refs_0_), channel_id=1, source_target_pairs={{0,3},{3,0},{1,2},{2,1},{4,7},{7,4},{5,6},{6,5},{8,11},{11,8},{9,1... | collective-permute-start | bytes 2506760 | tf_op jit(solution)/shard_map/ppermute | solution.py:424
  382.1 12.1 %collective-permute-start.28 = (bf16[102,32,128]{2,1,0:T(8,128)(2,1)S(1)}, bf16[102,32,128]{2,1,0:T(8,128)(2,1)S(1)}, u32[]{:S(2)}, u32[]{:S(2)}) collective-permute-start(bf16[102,32,128]{2,1,0:T(8,128)(2,1)S(1)} %get-tuple-element.118), channel_id=1, source_target_pairs={{0,4},{4,0},{1,5},{5,1},{2,6},{6,2},{3,7},{7,3},{8,12},{12,8},{9,1... | collective-permute-start | bytes 2506760 | tf_op jit(solution)/shard_map/ppermute | solution.py:420
  394.4 21.3 %collective-permute-start.29 = (bf16[102,32,128]{2,1,0:T(8,128)(2,1)S(1)}, bf16[102,32,128]{2,1,0:T(8,128)(2,1)S(1)}, u32[]{:S(2)}, u32[]{:S(2)}) collective-permute-start(bf16[102,32,128]{2,1,0:T(8,128)(2,1)S(1)} %add_convert_fusion.refs_0_), channel_id=1, source_target_pairs={{0,3},{3,0},{1,2},{2,1},{4,7},{7,4},{5,6},{6,5},{8,11},{11,8},{9,1... | collective-permute-start | bytes 2506760 | tf_op jit(solution)/shard_map/ppermute | solution.py:424
  422.4 1.8 collective-permute-start.32
  424.4 14.8 %collective-permute-start.33 = (bf16[204,16,128]{2,1,0:T(8,128)(2,1)S(1)}, bf16[204,16,128]{2,1,0:T(8,128)(2,1)S(1)}, u32[]{:S(2)}, u32[]{:S(2)}) collective-permute-start(bf16[204,16,128]{2,1,0:T(8,128)(2,1)S(1)} %maximum_select_fusion), channel_id=1, source_target_pairs={{0,5},{3,6},{5,0},{6,3},{8,13},{11,14},{13,8},{14,11},{16,21},{19,... | collective-permute-start | bytes 2506760 | tf_op jit(solution)/shard_map/ppermute | solution.py:556
  427.6 11.0 %collective-permute-start.35 = (f32[64,64]{1,0:T(8,128)S(1)}, f32[64,64]{1,0:T(8,128)S(1)}, u32[]{:S(2)}, u32[]{:S(2)}) collective-permute-start(f32[64,64]{1,0:T(8,128)S(1)} %add.97), channel_id=1, source_target_pairs={{0,5},{3,6},{5,0},{6,3},{8,13},{11,14},{13,8},{14,11},{16,21},{19,... | collective-permute-start | bytes 49160 | tf_op jit(solution)/shard_map/ppermute | solution.py:557
  (11 other events, 50.1 us)
Sparse Core Ops, SparseCore 0:
  36.7 143.3 all-gather.2

commit v5 on v4

--- a/solution.py
+++ b/solution.py
@@ -393,12 +393,12 @@
     return pairs
 
 
-def out_pairs(ny, nz):
+def out_pairs(ny, nz, crossed):
     pairs = []
     for y, z, c, xh, xl in every(ny, nz):
         if c != side(xh, xl):
-            there = (y, z, 1 - c, xh, 1 - xl)
-            pairs.append((flat(ny, nz, y, z, c, xh, xl), flat(ny, nz, *there)))
+            there = (y, z, 1 - c if crossed else c, xh, 1 - xl)
+            pairs.append((flat(ny, nz, *there), flat(ny, nz, y, z, c, xh, xl)))
     return pairs
 
 
@@ -543,19 +543,19 @@
             new = second_modes(lower, gram, core_swap(gram), first, before, applied)
             owns[1], peers[1] = new, core_swap(new)
 
+    at_home = c == own_side
     ritz = ritz + core_swap(ritz)
-    at_home = c == own_side
+    ritz = jnp.where(at_home, ritz, lax.ppermute(ritz, AXES, out_pairs(ny, nz, True)))
     mine = lax.dynamic_slice_in_dim(out, xl * share, share, 1)
     beside = lax.dynamic_slice_in_dim(out, (1 - xl) * share, share, 1)
-    held = jnp.where(at_home, mine, beside)
-    swapped = core_swap(jnp.where(at_home, beside, mine))
-    whole = jnp.where(
-        c == 0, jnp.concatenate([held, swapped], 0), jnp.concatenate([swapped, held], 0)
-    )
-    pairs = out_pairs(ny, nz)
-    modes = jnp.where(at_home, whole, lax.ppermute(whole, AXES, pairs))
-    ritz = jnp.where(at_home, ritz, lax.ppermute(ritz, AXES, pairs))
-    return modes[None], ritz[None]
+    same = lax.ppermute(beside, AXES, out_pairs(ny, nz, False))
+    crossed = lax.ppermute(beside, AXES, out_pairs(ny, nz, True))
+    sibling = core_swap(mine)
+    this_half = jnp.where(at_home, mine, same)
+    other_half = jnp.where(at_home, sibling, crossed)
+    low = jnp.where(c == 0, this_half, other_half)
+    high = jnp.where(c == 0, other_half, this_half)
+    return jnp.concatenate([low, high], axis=0)[None], ritz[None]
 
 
 def solution(mesh, ny=4):

time: 448 us -> 446 us (level)
  transfers between devices with their start and end apart: 38 -> 39, of which waited for: 25 -> 24; matrix products, arithmetic and copies ran while one was open for 2% -> 2% of each run, Pallas kernels for 13% -> 13%
where the time goes in v5:
time: 446 us
  waiting for transfers between devices  267 us (60%)
  Pallas kernels  98.3 us (22%)
  starting transfers between devices  49.2 us (11%)
  between operations  14.7 us (3%)
  other arithmetic  12.4 us (3%)
    all_gather x1, waiting for transfers between devices, shards(): tables = lax.all_gather(table, AXES, axis=0, tiled=False)[:, :4, :rows]  92.5 us
    ppermute x7, waiting for transfers between devices, chip_swap(): return lax.ppermute(value, ('xh', 'xl'), [(0, 3), (3, 0), (1, 2), (2, 1)])  72 us
    pallas_call x6, Pallas kernels, apply_rows(): pl.pallas_call(functools.partial(apply_kernel, first, group, unroll), out...  54.5 us
    ppermute x3, waiting for transfers between devices, shards(): lax.ppermute(start_modes[0], ('c', 'xh', 'xl'), start_pairs(mask))  44.6 us
    all_to_all x1, waiting for transfers between devices, shards(): lax.all_to_all(packed, group, split_axis=0, concat_axis=0, tiled=True)  33.5 us
    ppermute x19, waiting for transfers between devices, core_swap(): return lax.ppermute(value, 'c', [(0, 1), (1, 0)])  18.2 us
    all_to_all x1, starting transfers between devices, shards(): lax.all_to_all(packed, group, split_axis=0, concat_axis=0, tiled=True)  13.4 us
    pallas_call x3, Pallas kernels, second_modes(): pl.pallas_call(second_kernel, out_shape=jax.ShapeDtypeStruct(applied.shap...  11.4 us
  transfers between devices with their start and end apart: 39, of which 24 were waited for; matrix products, arithmetic and copies ran while one was open for 2% of the time, Pallas kernels for 13%

profile of v5, /device:TPU:6, one launch (start us, length us, event | category | flops | bytes accessed | tf_op | source)
XLA Modules:
  0.0 445.7 jit_solution(4661116182397072003)
XLA Ops:
  9.1 7.2 %shard_map.68 = bf16[128,2,128,128]{3,2,1,0:T(8,128)(2,1)} custom-call(s32[128]{0:T(128)S(1)} %select_n.162.order, bf16[64,2,128,128]{3,2,1,0:T(8,128)(2,1)} %blocks.1), custom_call_target="tpu_custom_call" | custom-call | tf_op jit(solution)/shard_map/pallas_call | solution.py:46
  16.9 13.4 %all-to-all-start = ((bf16[128,2,128,128]{3,2,1,0:T(8,128)(2,1)}), bf16[128,2,128,128]{3,2,1,0:T(8,128)(2,1)}, u32[]{:S(2)}, u32[]{:S(2)}) async-start(bf16[128,2,128,128]{3,2,1,0:T(8,128)(2,1)} %shard_map.68), calls=%async_computation | async-start | bytes 16777216 | tf_op jit(solution)/shard_map/all_to_all | solution.py:453
  30.4 2.5 collective-permute-start.6
  36.7 30.8 %collective-permute-done.6 = bf16[204,16,128]{2,1,0:T(8,128)(2,1)S(1)} collective-permute-done((bf16[204,16,128]{2,1,0:T(8,128)(2,1)S(1)}, bf16[204,16,128]{2,1,0:T(8,128)(2,1)S(1)}, u32[]{:S(2)}, u32[]{:S(2)}) %collective-permute-start.6) | collective-permute-done | bytes 835616 | tf_op jit(solution)/shard_map/ppermute | solution.py:471
  67.4 13.8 %collective-permute-done.7 = bf16[204,16,128]{2,1,0:T(8,128)(2,1)S(1)} collective-permute-done((bf16[204,16,128]{2,1,0:T(8,128)(2,1)S(1)}, bf16[204,16,128]{2,1,0:T(8,128)(2,1)S(1)}, u32[]{:S(2)}, u32[]{:S(2)}) %collective-permute-start.7) | collective-permute-done | bytes 835616 | tf_op jit(solution)/shard_map/ppermute | solution.py:471
  87.7 92.5 %all-gather.3.cloned.1.call-done = f32[2048,128]{1,0:T(8,128)} async-done(((f32[8,128]{1,0:T(8,128)}), f32[2048,128]{1,0:T(8,128)}) %all-gather.3.cloned.1.call-update) | async-done | bytes 1048592 | tf_op jit(solution)/shard_map/all_gather | solution.py:455
  182.6 33.5 %all-to-all-done.left.right.blk = bf16[128,2,128,128]{3,2,1,0:T(8,128)(2,1)} async-done(((bf16[128,2,128,128]{3,2,1,0:T(8,128)(2,1)}), bf16[128,2,128,128]{3,2,1,0:T(8,128)(2,1)}, u32[]{:S(2)}, u32[]{:S(2)}) %all-to-all-start) | async-done | bytes 8388640 | tf_op jit(solution)/shard_map/all_to_all | solution.py:453
  216.1 8.4 %shard_map.69 = f32[204,128]{1,0:T(8,128)S(1)} custom-call(s32[256]{0:T(256)S(1)} %reshape.145.offs, s32[128]{0:T(128)S(1)} %reshape.146.live, bf16[128,2,128,128]{3,2,1,0:T(8,128)(2,1)} %all-to-all-done.left.right.blk, bf16[128,2,128,128]{3,2,1,0:T(8,128)(2,1)} %all-to-all-done.left.right.blk), custom_call_target="tpu_custom_call" | custom-call | tf_op jit(solution)/shard_map/pallas_call | solution.py:85
  224.7 2.6 broadcast_select_fusion
  227.3 4.7 %collective-permute-start.1 = (f32[204,128]{1,0:T(8,128)S(1)}, f32[204,128]{1,0:T(8,128)S(1)}, u32[]{:S(2)}, u32[]{:S(2)}) collective-permute-start(f32[204,128]{1,0:T(8,128)S(1)} %add.81), channel_id=1, source_target_pairs={{0,3},{3,0},{1,2},{2,1},{4,7},{7,4},{5,6},{6,5},{8,11},{11,8},{9,1... | collective-permute-start | bytes 313352 | tf_op jit(solution)/shard_map/ppermute | solution.py:424
  234.1 8.4 %collective-permute-start.5 = (f32[8,128]{1,0:T(8,128)S(1)}, f32[8,128]{1,0:T(8,128)S(1)}, u32[]{:S(2)}, u32[]{:S(2)}) collective-permute-start(f32[8,128]{1,0:T(8,128)S(1)} %get-tuple-element.151), channel_id=1, source_target_pairs={{10,0},{3,1},{0,2},{9,3},{14,4},{7,5},{4,6},{13,7},{18,8},{11,9},{... | collective-permute-start | bytes 12296 | tf_op jit(solution)/shard_map/ppermute | solution.py:496
  243.9 11.6 %shard_map.70 = (bf16[102,32,128]{2,1,0:T(8,128)(2,1)S(1)}, bf16[102,32,128]{2,1,0:T(8,128)(2,1)S(1)}, bf16[128,2,128,128]{3,2,1,0:T(8,128)(2,1)S(1)}) custom-call(s32[256]{0:T(256)S(1)} %reshape.145.offs, s32[128]{0:T(128)S(1)} %reshape.146.live, s32[1]{0:T(128)} %bitcast.21.core, bf16[128,2,128,128]{3,2,1,0:T(8,128)(2,1)} %all-to-all-done.left.right.blk, ...), custom_call_target="tpu_custom_call" | custom-call | flops 10000000000 | bytes 12000000 | tf_op jit(solution)/shard_map/pallas_call | solution.py:177
  255.5 2.3 collective-permute-done.10
  258.3 8.6 %shard_map.71 = (bf16[102,32,128]{2,1,0:T(8,128)(2,1)S(1)}, bf16[102,32,128]{2,1,0:T(8,128)(2,1)S(1)}) custom-call(s32[256]{0:T(256)S(1)} %reshape.145.offs, s32[128]{0:T(128)S(1)} %reshape.146.live, s32[1]{0:T(128)} %bitcast.21.core, bf16[128,2,128,128]{3,2,1,0:T(8,128)(2,1)S(1)} %get-tuple-element.71.blk, f32[204,128]{1,0:T(8,128)S(1)} %fusion.1.scale, ...), custom_call_target="tpu_custom_call" | custom-call | flops 10000000000 | bytes 12000000 | tf_op jit(solution)/shard_map/pallas_call | solution.py:177
  267.3 12.8 %collective-permute-done.11.refs_1_ = bf16[102,32,128]{2,1,0:T(8,128)(2,1)S(1)} collective-permute-done((bf16[102,32,128]{2,1,0:T(8,128)(2,1)S(1)}, bf16[102,32,128]{2,1,0:T(8,128)(2,1)S(1)}, u32[]{:S(2)}, u32[]{:S(2)}) %collective-permute-start.11) | collective-permute-done | bytes 835616 | tf_op jit(solution)/shard_map/ppermute | solution.py:424
  282.4 3.4 shard_map.73
  288.2 8.6 %shard_map.74 = (bf16[102,32,128]{2,1,0:T(8,128)(2,1)S(1)}, bf16[102,32,128]{2,1,0:T(8,128)(2,1)S(1)}) custom-call(s32[256]{0:T(256)S(1)} %reshape.145.offs, s32[128]{0:T(128)S(1)} %reshape.146.live, s32[1]{0:T(128)} %bitcast.21.core, bf16[128,2,128,128]{3,2,1,0:T(8,128)(2,1)S(1)} %get-tuple-element.71.blk, f32[204,128]{1,0:T(8,128)S(1)} %fusion.1.scale, ...), custom_call_target="tpu_custom_call" | custom-call | flops 10000000000 | bytes 12000000 | tf_op jit(solution)/shard_map/pallas_call | solution.py:177
  297.0 11.0 %collective-permute-done.13.refs_1_ = bf16[102,32,128]{2,1,0:T(8,128)(2,1)S(1)} collective-permute-done((bf16[102,32,128]{2,1,0:T(8,128)(2,1)S(1)}, bf16[102,32,128]{2,1,0:T(8,128)(2,1)S(1)}, u32[]{:S(2)}, u32[]{:S(2)}) %collective-permute-start.13) | collective-permute-done | bytes 835616 | tf_op jit(solution)/shard_map/ppermute | solution.py:424
  310.4 3.8 shard_map.76.own.refs_2_
  316.7 8.6 %shard_map.77 = (bf16[102,32,128]{2,1,0:T(8,128)(2,1)S(1)}, bf16[102,32,128]{2,1,0:T(8,128)(2,1)S(1)}) custom-call(s32[256]{0:T(256)S(1)} %reshape.145.offs, s32[128]{0:T(128)S(1)} %reshape.146.live, s32[1]{0:T(128)} %bitcast.21.core, bf16[128,2,128,128]{3,2,1,0:T(8,128)(2,1)S(1)} %get-tuple-element.71.blk, f32[204,128]{1,0:T(8,128)S(1)} %fusion.1.scale, ...), custom_call_target="tpu_custom_call" | custom-call | flops 10000000000 | bytes 12000000 | tf_op jit(solution)/shard_map/pallas_call | solution.py:177
  325.6 11.0 %collective-permute-done.17.refs_1_ = bf16[102,32,128]{2,1,0:T(8,128)(2,1)S(1)} collective-permute-done((bf16[102,32,128]{2,1,0:T(8,128)(2,1)S(1)}, bf16[102,32,128]{2,1,0:T(8,128)(2,1)S(1)}, u32[]{:S(2)}, u32[]{:S(2)}) %collective-permute-start.17) | collective-permute-done | bytes 835616 | tf_op jit(solution)/shard_map/ppermute | solution.py:424
  338.9 3.4 shard_map.79
  344.7 8.6 %shard_map.80 = (bf16[102,32,128]{2,1,0:T(8,128)(2,1)S(1)}, bf16[102,32,128]{2,1,0:T(8,128)(2,1)S(1)}) custom-call(s32[256]{0:T(256)S(1)} %reshape.145.offs, s32[128]{0:T(128)S(1)} %reshape.146.live, s32[1]{0:T(128)} %bitcast.21.core, bf16[128,2,128,128]{3,2,1,0:T(8,128)(2,1)S(1)} %get-tuple-element.71.blk, f32[204,128]{1,0:T(8,128)S(1)} %fusion.1.scale, ...), custom_call_target="tpu_custom_call" | custom-call | flops 10000000000 | bytes 12000000 | tf_op jit(solution)/shard_map/pallas_call | solution.py:177
  353.6 11.0 %collective-permute-done.21.refs_1_ = bf16[102,32,128]{2,1,0:T(8,128)(2,1)S(1)} collective-permute-done((bf16[102,32,128]{2,1,0:T(8,128)(2,1)S(1)}, bf16[102,32,128]{2,1,0:T(8,128)(2,1)S(1)}, u32[]{:S(2)}, u32[]{:S(2)}) %collective-permute-start.21) | collective-permute-done | bytes 835616 | tf_op jit(solution)/shard_map/ppermute | solution.py:424
  367.2 3.8 shard_map.82.own.refs_2_
  373.5 8.6 %shard_map.83 = (bf16[102,32,128]{2,1,0:T(8,128)(2,1)S(1)}, bf16[102,32,128]{2,1,0:T(8,128)(2,1)S(1)}) custom-call(s32[256]{0:T(256)S(1)} %reshape.145.offs, s32[128]{0:T(128)S(1)} %reshape.146.live, s32[1]{0:T(128)} %bitcast.21.core, bf16[128,2,128,128]{3,2,1,0:T(8,128)(2,1)S(1)} %get-tuple-element.71.blk, f32[204,128]{1,0:T(8,128)S(1)} %fusion.1.scale, ...), custom_call_target="tpu_custom_call" | custom-call | flops 10000000000 | bytes 12000000 | tf_op jit(solution)/shard_map/pallas_call | solution.py:177
  382.3 11.0 %collective-permute-done.25.refs_1_ = bf16[102,32,128]{2,1,0:T(8,128)(2,1)S(1)} collective-permute-done((bf16[102,32,128]{2,1,0:T(8,128)(2,1)S(1)}, bf16[102,32,128]{2,1,0:T(8,128)(2,1)S(1)}, u32[]{:S(2)}, u32[]{:S(2)}) %collective-permute-start.25) | collective-permute-done | bytes 835616 | tf_op jit(solution)/shard_map/ppermute | solution.py:424
  395.9 4.6 %shard_map.85 = (bf16[102,32,128]{2,1,0:T(8,128)(2,1)}, f32[32,32]{1,0:T(8,128)S(1)}) custom-call(f32[32,32]{1,0:T(8,128)S(1)} %get-tuple-element.120.gram_one, f32[32,32]{1,0:T(8,128)S(1)} %collective-permute-done.30.gram_two, bf16[102,32,128]{2,1,0:T(8,128)(2,1)S(1)} %get-tuple-element.121.applied.refs_4_.before), custom_call_target="tpu_custom_call" | custom-call | flops 3000000000 | bytes 1000000 | tf_op jit(solution)/shard_map/pallas_call | solution.py:332
  400.5 15.2 %collective-permute-done.29.refs_1_ = bf16[102,32,128]{2,1,0:T(8,128)(2,1)S(1)} collective-permute-done((bf16[102,32,128]{2,1,0:T(8,128)(2,1)S(1)}, bf16[102,32,128]{2,1,0:T(8,128)(2,1)S(1)}, u32[]{:S(2)}, u32[]{:S(2)}) %collective-permute-start.29) | collective-permute-done | bytes 835616 | tf_op jit(solution)/shard_map/ppermute | solution.py:424
  418.4 3.8 shard_map.87
  423.9 4.5 %collective-permute-start.34 = (bf16[102,16,128]{2,1,0:T(8,128)(2,1)S(1)}, bf16[102,16,128]{2,1,0:T(8,128)(2,1)S(1)}, u32[]{:S(2)}, u32[]{:S(2)}) collective-permute-start(bf16[102,16,128]{2,1,0:T(8,128)(2,1)S(1)} %get-tuple-element.145), channel_id=1, source_target_pairs={{5,0},{6,3},{0,5},{3,6},{13,8},{14,11},{8,13},{11,14},{21,16},{22,... | collective-permute-start | bytes 1253384 | tf_op jit(solution)/shard_map/ppermute | solution.py:552
  431.6 5.5 %collective-permute-done.36 = f32[64,64]{1,0:T(8,128)S(1)} collective-permute-done((f32[64,64]{1,0:T(8,128)S(1)}, f32[64,64]{1,0:T(8,128)S(1)}, u32[]{:S(2)}, u32[]{:S(2)}) %collective-permute-start.36) | collective-permute-done | bytes 16416 | tf_op jit(solution)/shard_map/ppermute | solution.py:548
  (125 shorter events, 51.7 us)
Async XLA Ops:
  16.9 199.3 %all-to-all-start = ((bf16[128,2,128,128]{3,2,1,0:T(8,128)(2,1)}), bf16[128,2,128,128]{3,2,1,0:T(8,128)(2,1)}, u32[]{:S(2)}, u32[]{:S(2)}) async-start(bf16[128,2,128,128]{3,2,1,0:T(8,128)(2,1)} %shard_map.68), calls=%async_computation | async-start | bytes 16777216 | tf_op jit(solution)/shard_map/all_to_all | solution.py:453
  30.3 149.9 %all-gather.3.cloned.1.call-start = ((), (), s32[]{:S(2)}) async-start(), calls=%async_computation.1 | async-start | bytes 1052672 | tf_op jit(solution)/shard_map/all_gather | solution.py:455
  30.4 37.1 %collective-permute-start.6 = (bf16[204,16,128]{2,1,0:T(8,128)(2,1)S(1)}, bf16[204,16,128]{2,1,0:T(8,128)(2,1)S(1)}, u32[]{:S(2)}, u32[]{:S(2)}) collective-permute-start(bf16[204,16,128]{2,1,0:T(8,128)(2,1)S(1)} %bitcast.45), channel_id=1, source_target_pairs={{5,4},{0,1},{3,2},{6,7},{13,12},{8,9},{11,10},{14,15},{21,20},{16,... | collective-permute-start | bytes 2506760 | tf_op jit(solution)/shard_map/ppermute | solution.py:471
  32.9 48.4 %collective-permute-start.7 = (bf16[204,16,128]{2,1,0:T(8,128)(2,1)S(1)}, bf16[204,16,128]{2,1,0:T(8,128)(2,1)S(1)}, u32[]{:S(2)}, u32[]{:S(2)}) collective-permute-start(bf16[204,16,128]{2,1,0:T(8,128)(2,1)S(1)} %bitcast.46), channel_id=1, source_target_pairs={{6,4},{3,1},{0,2},{5,7},{14,12},{11,9},{8,10},{13,15},{22,20},{19,... | collective-permute-start | bytes 2506760 | tf_op jit(solution)/shard_map/ppermute | solution.py:471
  35.0 47.1 %collective-permute-start.8 = (bf16[204,16,128]{2,1,0:T(8,128)(2,1)S(1)}, bf16[204,16,128]{2,1,0:T(8,128)(2,1)}, u32[]{:S(2)}, u32[]{:S(2)}) collective-permute-start(bf16[204,16,128]{2,1,0:T(8,128)(2,1)S(1)} %bitcast.47), channel_id=1, source_target_pairs={{7,4},{2,1},{1,2},{4,7},{15,12},{10,9},{9,10},{12,15},{23,20},{18,... | collective-permute-start | bytes 2506760 | tf_op jit(solution)/shard_map/ppermute | solution.py:471
  86.3 138.4 %collective-permute-start.9 = (bf16[204,64,128]{2,1,0:T(8,128)(2,1)}, bf16[204,64,128]{2,1,0:T(8,128)(2,1)}, u32[]{:S(2)}, u32[]{:S(2)}) collective-permute-start(bf16[204,64,128]{2,1,0:T(8,128)(2,1)} %pad_maximum_fusion), channel_id=1, source_target_pairs={{4,0},{1,5},{2,6},{7,3},{12,8},{9,13},{10,14},{15,11},{20,16},{17,... | collective-permute-start | bytes 10027016 | tf_op jit(solution)/shard_map/ppermute | solution.py:478
  224.6 2.7 collective-permute-start
  227.3 16.4 %collective-permute-start.1 = (f32[204,128]{1,0:T(8,128)S(1)}, f32[204,128]{1,0:T(8,128)S(1)}, u32[]{:S(2)}, u32[]{:S(2)}) collective-permute-start(f32[204,128]{1,0:T(8,128)S(1)} %add.81), channel_id=1, source_target_pairs={{0,3},{3,0},{1,2},{2,1},{4,7},{7,4},{5,6},{6,5},{8,11},{11,8},{9,1... | collective-permute-start | bytes 313352 | tf_op jit(solution)/shard_map/ppermute | solution.py:424
  232.0 11.0 %collective-permute-start.2 = (f32[8,128]{1,0:T(8,128)S(1)}, f32[8,128]{1,0:T(8,128)S(1)}, u32[]{:S(2)}, u32[]{:S(2)}) collective-permute-start(f32[8,128]{1,0:T(8,128)S(1)} %get-tuple-element.150), channel_id=1, source_target_pairs={{0,9},{1,0},{2,3},{3,10},{4,13},{5,4},{6,7},{7,14},{8,17},{9,8},{1... | collective-permute-start | bytes 12296 | tf_op jit(solution)/shard_map/ppermute | solution.py:495
  232.0 11.0 %collective-permute-start.3 = (f32[8,128]{1,0:T(8,128)S(1)}, f32[8,128]{1,0:T(8,128)S(1)}, u32[]{:S(2)}, u32[]{:S(2)}) collective-permute-start(f32[8,128]{1,0:T(8,128)S(1)} %get-tuple-element.150), channel_id=1, source_target_pairs={{0,10},{1,3},{2,0},{3,9},{4,14},{5,7},{6,4},{7,13},{8,18},{9,11},{... | collective-permute-start | bytes 12296 | tf_op jit(solution)/shard_map/ppermute | solution.py:495
  232.6 10.5 %collective-permute-start.4 = (f32[8,128]{1,0:T(8,128)S(1)}, f32[8,128]{1,0:T(8,128)S(1)}, u32[]{:S(2)}, u32[]{:S(2)}) collective-permute-start(f32[8,128]{1,0:T(8,128)S(1)} %get-tuple-element.151), channel_id=1, source_target_pairs={{9,0},{0,1},{3,2},{10,3},{13,4},{4,5},{7,6},{14,7},{17,8},{8,9},{1... | collective-permute-start | bytes 12296 | tf_op jit(solution)/shard_map/ppermute | solution.py:496
  234.1 9.7 %collective-permute-start.5 = (f32[8,128]{1,0:T(8,128)S(1)}, f32[8,128]{1,0:T(8,128)S(1)}, u32[]{:S(2)}, u32[]{:S(2)}) collective-permute-start(f32[8,128]{1,0:T(8,128)S(1)} %get-tuple-element.151), channel_id=1, source_target_pairs={{10,0},{3,1},{0,2},{9,3},{14,4},{7,5},{4,6},{13,7},{18,8},{11,9},{... | collective-permute-start | bytes 12296 | tf_op jit(solution)/shard_map/ppermute | solution.py:496
  255.4 2.4 collective-permute-start.10
  258.1 21.9 %collective-permute-start.11 = (bf16[102,32,128]{2,1,0:T(8,128)(2,1)S(1)}, bf16[102,32,128]{2,1,0:T(8,128)(2,1)S(1)}, u32[]{:S(2)}, u32[]{:S(2)}) collective-permute-start(bf16[102,32,128]{2,1,0:T(8,128)(2,1)S(1)} %add_convert_fusion.5.refs_0_), channel_id=1, source_target_pairs={{0,3},{3,0},{1,2},{2,1},{4,7},{7,4},{5,6},{6,5},{8,11},{11,8},{9,1... | collective-permute-start | bytes 2506760 | tf_op jit(solution)/shard_map/ppermute | solution.py:424
  266.9 14.0 %collective-permute-start.12 = (bf16[102,32,128]{2,1,0:T(8,128)(2,1)S(1)}, bf16[102,32,128]{2,1,0:T(8,128)(2,1)S(1)}, u32[]{:S(2)}, u32[]{:S(2)}) collective-permute-start(bf16[102,32,128]{2,1,0:T(8,128)(2,1)S(1)} %get-tuple-element.78), channel_id=1, source_target_pairs={{0,4},{4,0},{1,5},{5,1},{2,6},{6,2},{3,7},{7,3},{8,12},{12,8},{9,1... | collective-permute-start | bytes 2506760 | tf_op jit(solution)/shard_map/ppermute | solution.py:420
  285.7 2.4 collective-permute-start.15
  286.0 22.1 %collective-permute-start.13 = (bf16[102,32,128]{2,1,0:T(8,128)(2,1)S(1)}, bf16[102,32,128]{2,1,0:T(8,128)(2,1)S(1)}, u32[]{:S(2)}, u32[]{:S(2)}) collective-permute-start(bf16[102,32,128]{2,1,0:T(8,128)(2,1)S(1)} %add_convert_fusion.4.refs_0_), channel_id=1, source_target_pairs={{0,3},{3,0},{1,2},{2,1},{4,7},{7,4},{5,6},{6,5},{8,11},{11,8},{9,1... | collective-permute-start | bytes 2506760 | tf_op jit(solution)/shard_map/ppermute | solution.py:424
  296.8 12.2 %collective-permute-start.16 = (bf16[102,32,128]{2,1,0:T(8,128)(2,1)S(1)}, bf16[102,32,128]{2,1,0:T(8,128)(2,1)S(1)}, u32[]{:S(2)}, u32[]{:S(2)}) collective-permute-start(bf16[102,32,128]{2,1,0:T(8,128)(2,1)S(1)} %get-tuple-element.88), channel_id=1, source_target_pairs={{0,4},{4,0},{1,5},{5,1},{2,6},{6,2},{3,7},{7,3},{8,12},{12,8},{9,1... | collective-permute-start | bytes 2506760 | tf_op jit(solution)/shard_map/ppermute | solution.py:420
  314.3 2.4 collective-permute-start.19
  314.5 22.1 %collective-permute-start.17 = (bf16[102,32,128]{2,1,0:T(8,128)(2,1)S(1)}, bf16[102,32,128]{2,1,0:T(8,128)(2,1)S(1)}, u32[]{:S(2)}, u32[]{:S(2)}) collective-permute-start(bf16[102,32,128]{2,1,0:T(8,128)(2,1)S(1)} %add_convert_fusion.3.refs_0_), channel_id=1, source_target_pairs={{0,3},{3,0},{1,2},{2,1},{4,7},{7,4},{5,6},{6,5},{8,11},{11,8},{9,1... | collective-permute-start | bytes 2506760 | tf_op jit(solution)/shard_map/ppermute | solution.py:424
  325.3 12.1 %collective-permute-start.20 = (bf16[102,32,128]{2,1,0:T(8,128)(2,1)S(1)}, bf16[102,32,128]{2,1,0:T(8,128)(2,1)S(1)}, u32[]{:S(2)}, u32[]{:S(2)}) collective-permute-start(bf16[102,32,128]{2,1,0:T(8,128)(2,1)S(1)} %get-tuple-element.98), channel_id=1, source_target_pairs={{0,4},{4,0},{1,5},{5,1},{2,6},{6,2},{3,7},{7,3},{8,12},{12,8},{9,1... | collective-permute-start | bytes 2506760 | tf_op jit(solution)/shard_map/ppermute | solution.py:420
  342.3 2.4 collective-permute-start.23
  342.5 22.1 %collective-permute-start.21 = (bf16[102,32,128]{2,1,0:T(8,128)(2,1)S(1)}, bf16[102,32,128]{2,1,0:T(8,128)(2,1)S(1)}, u32[]{:S(2)}, u32[]{:S(2)}) collective-permute-start(bf16[102,32,128]{2,1,0:T(8,128)(2,1)S(1)} %add_convert_fusion.2.refs_0_), channel_id=1, source_target_pairs={{0,3},{3,0},{1,2},{2,1},{4,7},{7,4},{5,6},{6,5},{8,11},{11,8},{9,1... | collective-permute-start | bytes 2506760 | tf_op jit(solution)/shard_map/ppermute | solution.py:424
  353.3 12.2 %collective-permute-start.24 = (bf16[102,32,128]{2,1,0:T(8,128)(2,1)S(1)}, bf16[102,32,128]{2,1,0:T(8,128)(2,1)S(1)}, u32[]{:S(2)}, u32[]{:S(2)}) collective-permute-start(bf16[102,32,128]{2,1,0:T(8,128)(2,1)S(1)} %get-tuple-element.108), channel_id=1, source_target_pairs={{0,4},{4,0},{1,5},{5,1},{2,6},{6,2},{3,7},{7,3},{8,12},{12,8},{9,1... | collective-permute-start | bytes 2506760 | tf_op jit(solution)/shard_map/ppermute | solution.py:420
  371.0 2.4 collective-permute-start.27
  371.3 22.1 %collective-permute-start.25 = (bf16[102,32,128]{2,1,0:T(8,128)(2,1)S(1)}, bf16[102,32,128]{2,1,0:T(8,128)(2,1)S(1)}, u32[]{:S(2)}, u32[]{:S(2)}) collective-permute-start(bf16[102,32,128]{2,1,0:T(8,128)(2,1)S(1)} %add_convert_fusion.1.refs_0_), channel_id=1, source_target_pairs={{0,3},{3,0},{1,2},{2,1},{4,7},{7,4},{5,6},{6,5},{8,11},{11,8},{9,1... | collective-permute-start | bytes 2506760 | tf_op jit(solution)/shard_map/ppermute | solution.py:424
  382.0 12.1 %collective-permute-start.28 = (bf16[102,32,128]{2,1,0:T(8,128)(2,1)S(1)}, bf16[102,32,128]{2,1,0:T(8,128)(2,1)S(1)}, u32[]{:S(2)}, u32[]{:S(2)}) collective-permute-start(bf16[102,32,128]{2,1,0:T(8,128)(2,1)S(1)} %get-tuple-element.118), channel_id=1, source_target_pairs={{0,4},{4,0},{1,5},{5,1},{2,6},{6,2},{3,7},{7,3},{8,12},{12,8},{9,1... | collective-permute-start | bytes 2506760 | tf_op jit(solution)/shard_map/ppermute | solution.py:420
  394.4 21.3 %collective-permute-start.29 = (bf16[102,32,128]{2,1,0:T(8,128)(2,1)S(1)}, bf16[102,32,128]{2,1,0:T(8,128)(2,1)S(1)}, u32[]{:S(2)}, u32[]{:S(2)}) collective-permute-start(bf16[102,32,128]{2,1,0:T(8,128)(2,1)S(1)} %add_convert_fusion.refs_0_), channel_id=1, source_target_pairs={{0,3},{3,0},{1,2},{2,1},{4,7},{7,4},{5,6},{6,5},{8,11},{11,8},{9,1... | collective-permute-start | bytes 2506760 | tf_op jit(solution)/shard_map/ppermute | solution.py:424
  422.4 15.4 %collective-permute-start.32 = (bf16[102,16,128]{2,1,0:T(8,128)(2,1)S(1)}, bf16[102,16,128]{2,1,0:T(8,128)(2,1)S(1)}, u32[]{:S(2)}, u32[]{:S(2)}) collective-permute-start(bf16[102,16,128]{2,1,0:T(8,128)(2,1)S(1)} %get-tuple-element.145), channel_id=1, source_target_pairs={{1,0},{2,3},{4,5},{7,6},{9,8},{10,11},{12,13},{15,14},{17,16},{18,... | collective-permute-start | bytes 1253384 | tf_op jit(solution)/shard_map/ppermute | solution.py:551
  423.7 14.1 %collective-permute-start.33 = (bf16[102,16,128]{2,1,0:T(8,128)(2,1)S(1)}, bf16[102,16,128]{2,1,0:T(8,128)(2,1)S(1)}, u32[]{:S(2)}, u32[]{:S(2)}) collective-permute-start(bf16[102,16,128]{2,1,0:T(8,128)(2,1)S(1)} %get-tuple-element.146), channel_id=1, source_target_pairs={{0,4},{4,0},{1,5},{5,1},{2,6},{6,2},{3,7},{7,3},{8,12},{12,8},{9,1... | collective-permute-start | bytes 1253384 | tf_op jit(solution)/shard_map/ppermute | solution.py:420
  423.9 13.8 %collective-permute-start.34 = (bf16[102,16,128]{2,1,0:T(8,128)(2,1)S(1)}, bf16[102,16,128]{2,1,0:T(8,128)(2,1)S(1)}, u32[]{:S(2)}, u32[]{:S(2)}) collective-permute-start(bf16[102,16,128]{2,1,0:T(8,128)(2,1)S(1)} %get-tuple-element.145), channel_id=1, source_target_pairs={{5,0},{6,3},{0,5},{3,6},{13,8},{14,11},{8,13},{11,14},{21,16},{22,... | collective-permute-start | bytes 1253384 | tf_op jit(solution)/shard_map/ppermute | solution.py:552
  429.7 7.4 %collective-permute-start.36 = (f32[64,64]{1,0:T(8,128)S(1)}, f32[64,64]{1,0:T(8,128)S(1)}, u32[]{:S(2)}, u32[]{:S(2)}) collective-permute-start(f32[64,64]{1,0:T(8,128)S(1)} %add.97), channel_id=1, source_target_pairs={{5,0},{6,3},{0,5},{3,6},{13,8},{14,11},{8,13},{11,14},{21,16},{22,... | collective-permute-start | bytes 49160 | tf_op jit(solution)/shard_map/ppermute | solution.py:548
  (12 other events, 51.6 us)
Sparse Core Ops, SparseCore 0:
  36.8 143.3 all-gather.2
